TPU v7x, 32 devices: a whole 2x2x4 slice. The times are simulated.
32 devices in a mesh: rep: 2 (over y), dp: 8 (over z, x), tensor: 2 (over core).
Axes of the slice: x: 2, y: 2, z: 4, core: 2. Of those that a mesh axis runs over, the one named last changes fastest.
Arguments:
- queries: bfloat16 [32, 256, 2048], P(('rep', 'dp'), None, 'tensor'), parts along dimension 0, may hold values from -18 to 18
- key_rows: bfloat16 [32, 256, 2048], P(('rep', 'dp'), None, 'tensor'), parts along dimension 0, may hold values from -4 to 4
- values: bfloat16 [32, 256, 2048], P(('rep', 'dp'), None, 'tensor'), parts along dimension 0, may hold values from -5 to 5
- position_bias: float32 [32, 32], P(None, 'tensor'), may hold values from -3 to 3
- out_weight: bfloat16 [2048, 2048], P('tensor', 'dp'), may hold values from -1 to 1
- counts: int32 [16], P(('rep', 'dp')), parts along dimension 0, may hold values from 0 to 2, as said below
- donors: int32 [8], P('rep'), parts along dimension 0, may hold values from 0 to 7, as said below
Outputs:
- encoded: bfloat16 [32, 256, 2048], P(('rep', 'dp'), None, 'tensor'), parts along dimension 0
There are 2 independent parts, one for each index of `rep`. A program takes and returns all parts, laid end to end along the dimension named above; an argument that names none is the same for every part. Nothing has to cross between parts.
Inputs may be any that keep to these rules, and one draw needn't show every extreme that they name: `counts`: exactly 4 data groups hold 2 passages, the others 0 or 1. `donors`: the data groups whose count is 2, ascending.
All inputs are finite; a program needn't handle non-finite values.
Results may differ from a plain program's by a relative error of at most 0.013.
Values may be sent and summed in bfloat16 or wider, within the bound.
No kernel may reach another device: no remote copies, remote signals or barrier semaphores. Data moves between devices by JAX's collectives and lax.ppermute only.
A program may use at most 64 MiB of HBM per device.

v0:
```python
import jax
import jax.numpy as jnp
from jax import lax
from jax.sharding import PartitionSpec as P

HEAD_DIM = 64


def position_buckets(length):
    position = jnp.arange(length, dtype=jnp.int32)
    relative = position[None, :] - position[:, None]
    distance = jnp.abs(relative)
    far_bucket = 8 + sum(
        ((distance >= threshold).astype(jnp.int32) for threshold in (12, 16, 23, 32, 46, 64, 91))
    )
    near_bucket = jnp.where(distance < 8, distance, far_bucket)
    return near_bucket + 16 * (relative > 0).astype(jnp.int32)


def attend(queries, key_rows, values, position_bias):
    slot_count, seq_tokens, features = queries.shape
    head_count = features // HEAD_DIM
    buckets = position_buckets(seq_tokens)
    bucket_count = position_bias.shape[0]
    one_hot = (
        buckets[:, :, None] == jnp.arange(bucket_count, dtype=jnp.int32)[None, None, :]
    ).astype(jnp.float32)
    position_terms = jnp.einsum(
        "ijb,bh->hij", one_hot, position_bias, precision=lax.Precision.HIGHEST
    )
    query = queries.reshape(slot_count, seq_tokens, head_count, HEAD_DIM)
    keyed = key_rows.reshape(slot_count, seq_tokens, head_count, HEAD_DIM)
    valued = values.reshape(slot_count, seq_tokens, head_count, HEAD_DIM)
    scores = (
        jnp.einsum("sihd,sjhd->shij", query, keyed, preferred_element_type=jnp.float32)
        + position_terms[None]
    )
    highest = jnp.max(scores, axis=-1, keepdims=True)
    expd = jnp.exp(scores - highest)
    attention = (expd / jnp.sum(expd, axis=-1, keepdims=True)).astype(jnp.bfloat16)
    context = jnp.einsum("shij,sjhd->sihd", attention, valued, preferred_element_type=jnp.float32)
    return context.astype(jnp.bfloat16).reshape(slot_count, seq_tokens, features)


def on_device(queries, key_rows, values, position_bias, out_weight, counts, donors):
    slot_count, seq_tokens, features = queries.shape
    context = attend(queries, key_rows, values, position_bias)
    row_block = context.reshape(slot_count * seq_tokens, features)
    merged = lax.psum_scatter(
        jnp.dot(
            row_block,
            lax.all_gather(out_weight, "dp", axis=1, tiled=True),
            preferred_element_type=jnp.float32,
        ).astype(jnp.bfloat16),
        "tensor",
        scatter_dimension=1,
        tiled=True,
    )
    result = merged.reshape(slot_count, seq_tokens, merged.shape[1])
    my_group = lax.axis_index("dp")
    first_live = counts[0] >= 1
    second_live = jnp.any(donors == my_group)
    live_mask = jnp.stack([first_live, second_live]).astype(jnp.bfloat16)
    return result * live_mask[:, None, None]


def solution(mesh):
    in_specs = (
        P(("rep", "dp"), None, "tensor"),
        P(("rep", "dp"), None, "tensor"),
        P(("rep", "dp"), None, "tensor"),
        P(None, "tensor"),
        P("tensor", "dp"),
        P(("rep", "dp")),
        P("rep"),
    )
    out_specs = P(("rep", "dp"), None, "tensor")
    return jax.shard_map(
        on_device, mesh=mesh, in_specs=in_specs, out_specs=out_specs, check_vma=False
    )
```

profile of v0, /device:TPU:0, one launch (start us, length us, event | category | flops | bytes accessed | tf_op | source)
XLA Modules:
  0.0 110.2 jit_solution(3000838185553283963)
XLA Ops:
  6.5 0.0 copy-start
  6.5 0.0 all-gather.2.cloned.1.call-start
  6.5 0.7 all-gather.2.cloned.1.call-update
  7.3 0.0 reduce-scatter.2.cloned.1.call-start
  7.3 0.2 fusion.11
  7.5 0.0 copy-done
  7.5 4.2 %fusion.8 = f32[16,256,256]{2,0,1:T(8,128)} fusion(s32[256,256]{1,0:T(8,128)S(1)} %fusion.11, f32[32,16]{0,1:T(8,128)S(1)} %copy-done), kind=kOutput, calls=%fused_computation.11 | convolution fusion | flops 404750336 | bytes 4458496 | tf_op jit(solution)/shard_map/ijb,bh->hij/dot_general | solution.py:28
  11.7 5.4 %copy.15 = f32[16,256,256]{1,2,0:T(8,128)} copy(f32[16,256,256]{2,0,1:T(8,128)} %fusion.8) | data formatting | bytes 8388608 | tf_op jit(solution)/shard_map/ijb,bh->hij/dot_general | solution.py:28
  17.1 0.0 copy-done.1
  17.1 0.5 copy.13
  17.6 0.0 copy-done.2
  17.6 0.5 copy.14
  18.1 1.5 %copy.16 = bf16[2,256,1024]{1,2,0:T(8,128)(2,1)S(1)} copy(bf16[2,256,1024]{2,1,0:T(8,128)(2,1)} %param.9) | data formatting | bytes 2097152 | tf_op args[2]
  19.6 6.6 %fusion.24 = (f32[2,16,256]{2,1,0:T(8,128)S(1)}, f32[2,16,256,256]{2,3,1,0:T(8,128)}) fusion(f32[16,256,256]{1,2,0:T(8,128)} %copy.15, bf16[2,256,16,64]{1,3,2,0:T(8,128)(2,1)S(1)} %bitcast.24, bf16[2,256,16,64]{1,3,2,0:T(8,128)(2,1)S(1)} %bitcast.25), kind=kOutput, calls=%fused_computation.31 | convolution fusion | flops 274727168 | bytes 14712832 | tf_op jit(solution)/shard_map/sub | solution.py:39
  26.2 4.3 %fusion.10 = bf16[2,256,16,64]{1,3,2,0:T(8,128)(2,1)S(1)} fusion(bf16[2,256,16,64]{1,3,2,0:T(8,128)(2,1)S(1)} %bitcast.28, f32[2,16,256,256]{2,3,1,0:T(8,128)} %get-tuple-element.6, f32[2,16,256]{2,1,0:T(8,128)S(1)} %get-tuple-element.5), kind=kOutput, calls=%fused_computation.13 | convolution fusion | flops 273154048 | bytes 10518528 | tf_op jit(solution)/shard_map/shij,sjhd->sihd/dot_general | solution.py:41
  30.5 1.1 copy.18
  31.6 0.2 copy.20
  31.9 55.3 %all-gather.2.cloned.1.call-done = bf16[1024,2048]{1,0:T(8,128)(2,1)} async-done(((bf16[1024,256]{1,0:T(8,128)(2,1)}), bf16[1024,2048]{1,0:T(8,128)(2,1)}) %all-gather.2.cloned.1.call-update) | async-done | bytes 4194320 | tf_op jit(solution)/shard_map/all_gather | solution.py:52
  87.2 5.9 %convolution_convert_fusion = bf16[512,2048]{1,0:T(8,128)(2,1)} fusion(bf16[512,1024]{0,1:T(8,128)(2,1)S(1)} %bitcast.29, bf16[1024,2048]{1,0:T(8,128)(2,1)} %all-gather.2.cloned.1.call-done), kind=kOutput, calls=%fused_computation.10 | convolution fusion | flops 2148532224 | bytes 7340032 | tf_op jit(solution)/shard_map/dot_general | solution.py:50
  93.1 0.0 reduce-scatter.2.cloned.1.call-update
  93.8 0.6 compare_reduce_fusion
  94.4 0.7 add_convert_fusion
  95.1 5.9 %reduce-scatter.2.cloned.1.call-done = bf16[512,1024]{1,0:T(8,128)(2,1)} async-done(((bf16[512,2048]{1,0:T(8,128)(2,1)}), bf16[512,1024]{1,0:T(8,128)(2,1)}) %reduce-scatter.2.cloned.1.call-update) | async-done | bytes 1048592 | tf_op jit(solution)/shard_map/reduce_scatter | solution.py:49
  101.1 2.3 %broadcast_multiply_fusion = bf16[2,256,1024]{2,1,0:T(8,128)(2,1)} fusion(bf16[2,256,1024]{2,1,0:T(8,128)(2,1)} %bitcast.27, bf16[2]{0:T(256)(128)(2,1)S(1)} %add_convert_fusion), kind=kLoop, calls=%fused_computation.15 | loop fusion | flops 524288 | bytes 2097156 | tf_op jit(solution)/shard_map/mul | solution.py:64
  (4 shorter events, 0.0 us)
Async XLA Ops:
  6.5 1.0 copy-start
  6.5 80.6 %all-gather.2.cloned.1.call-start = ((), (), s32[]{:S(2)}) async-start(), calls=%async_computation.1 | async-start | bytes 4718592 | tf_op jit(solution)/shard_map/all_gather | solution.py:52
  7.3 93.8 %reduce-scatter.2.cloned.1.call-start = ((), (), s32[]{:S(2)}) async-start(), calls=%async_computation.2 | async-start | bytes 3145728 | tf_op jit(solution)/shard_map/reduce_scatter | solution.py:49
  11.7 5.4 %copy-start.1 = (bf16[2,256,1024]{2,1,0:T(8,128)(2,1)S(1)}, bf16[2,256,1024]{2,1,0:T(8,128)(2,1)}, u32[]{:S(2)}) copy-start(bf16[2,256,1024]{2,1,0:T(8,128)(2,1)} %param.7) | copy-start | bytes 3145732
  11.7 5.9 %copy-start.2 = (bf16[2,256,1024]{2,1,0:T(8,128)(2,1)S(1)}, bf16[2,256,1024]{2,1,0:T(8,128)(2,1)}, u32[]{:S(2)}) copy-start(bf16[2,256,1024]{2,1,0:T(8,128)(2,1)} %param.8) | copy-start | bytes 3145732
  87.2 6.6 %copy-start.3 = (s32[4]{0:T(128)S(1)}, s32[4]{0:T(128)}, u32[]{:S(2)}) copy-start(s32[4]{0:T(128)} %param.13) | copy-start | bytes 52
Sparse Core Ops, SparseCore 0:
  9.4 77.7 all-gather.1
  93.2 7.7 reduce-scatter.1
where the time goes:
time: 111 us; the launch traced here: 110 us
  waiting for transfers between devices  61.9 us (56%)
  matrix products  21 us (19%)
  between operations  14.1 us (13%)
  local copies, waits for them, and re-layouts  9.27 us (8%)
  other arithmetic  3.87 us (3%)
    all_gather x1, waiting for transfers between devices, on_device(): lax.all_gather(out_weight, 'dp', axis=1, tiled=True)  55.3 us
    sub x1, matrix products, attend(): expd = jnp.exp(scores - highest)  6.59 us
    reduce_scatter x1, waiting for transfers between devices, on_device(): lax.psum_scatter(jnp.dot(row_block, lax.all_gather(out_weight, 'dp', axis...  5.93 us
    dot_general x1, matrix products, on_device(): jnp.dot(row_block, lax.all_gather(out_weight, 'dp', axis=1, tiled=True),...  5.92 us
    dot_general x1, local copies, waits for them, and re-layouts, attend(): jnp.einsum('ijb,bh->hij', one_hot, position_bias, precision=lax.Precision...  5.39 us
    dot_general x1, matrix products, attend(): jnp.einsum('shij,sjhd->sihd', attention, valued, preferred_element_type=j...  4.3 us
    dot_general x1, matrix products, attend(): jnp.einsum('ijb,bh->hij', one_hot, position_bias, precision=lax.Precision...  4.16 us
    unnamed x12, local copies, waits for them, and re-layouts  2.79 us
  transfers between devices with their start and end apart: 2, of which 2 were waited for; matrix products, arithmetic and copies ran while one was open for 23% of the time, Pallas kernels for 0%

commit v1 on v0

v1 whole, which is shorter than its diff:
```python
import functools

import jax
import jax.numpy as jnp
from jax import lax
from jax.experimental import pallas as pl
from jax.experimental.pallas import tpu as pltpu
from jax.sharding import PartitionSpec as P

HEAD_DIM = 64
PAIR = 2 * HEAD_DIM
CHUNK = 256
THRESHOLDS = (12, 16, 23, 32, 46, 64, 91)
AXES = ("rep", "dp", "tensor")


def bias_rows(position_bias, tokens):
    bucket_count = position_bias.shape[0]
    shape = (bucket_count, 2 * tokens)
    relative = lax.broadcasted_iota(jnp.int32, shape, 1) - (tokens - 1)
    distance = jnp.abs(relative)
    far = jnp.full(shape, 8, jnp.int32)
    for threshold in THRESHOLDS:
        far = far + jnp.where(distance >= threshold, 1, 0)
    bucket = jnp.where(distance < 8, distance, far) + jnp.where(relative > 0, 16, 0)
    one_hot = jnp.where(bucket == lax.broadcasted_iota(jnp.int32, shape, 0), 1.0, 0.0)
    return lax.dot_general(
        position_bias,
        one_hot,
        (((0,), (0,)), ((), ())),
        precision=lax.Precision.HIGHEST,
        preferred_element_type=jnp.float32,
    )


def attention_kernel(first_head, bias_ref, query_ref, key_ref, value_ref, out_ref):
    slots, tokens, width = query_ref.shape
    rows = bias_rows(bias_ref[...], tokens)
    lower = lax.broadcasted_iota(jnp.int32, (tokens, PAIR), 1) < HEAD_DIM
    for pair in range(width // PAIR):
        columns = slice(pair * PAIR, (pair + 1) * PAIR)
        terms = []
        for head in range(2):
            at = first_head + 2 * pair + head
            spread = jnp.broadcast_to(rows[at : at + 1], (tokens, 2 * tokens))
            rolled = pltpu.roll(spread, tokens + 1, 1, stride=1, stride_axis=0)
            terms.append(rolled[:, :tokens])
        for slot in range(slots):
            query = query_ref[slot, :, columns]
            key = key_ref[slot, :, columns]
            value = value_ref[slot, :, columns]
            sums = []
            for head in range(2):
                own = lower if head == 0 else jnp.logical_not(lower)
                scores = lax.dot_general(
                    query,
                    jnp.where(own, key, 0),
                    (((1,), (1,)), ((), ())),
                    preferred_element_type=jnp.float32,
                )
                scores = scores + terms[head]
                highest = jnp.max(scores, axis=-1, keepdims=True)
                expd = jnp.exp(scores - highest).astype(jnp.bfloat16)
                sums.append(
                    jnp.dot(expd, jnp.where(own, value, 1), preferred_element_type=jnp.float32)
                )
            weighted = jnp.where(lower, sums[0], sums[1])
            total = pltpu.roll(jnp.where(lower, sums[1], sums[0]), HEAD_DIM, 1)
            out_ref[slot * tokens : (slot + 1) * tokens, columns] = (weighted / total).astype(
                jnp.bfloat16
            )


def attend(queries, key_rows, values, position_bias, chunk):
    slots, tokens, _ = queries.shape
    block = pl.BlockSpec((slots, tokens, CHUNK), lambda i: (0, 0, chunk))
    heads = CHUNK // HEAD_DIM
    scores = slots * heads * tokens * tokens
    return pl.pallas_call(
        functools.partial(attention_kernel, chunk * heads),
        out_shape=jax.ShapeDtypeStruct((slots * tokens, CHUNK), jnp.bfloat16),
        grid=(1,),
        in_specs=[pl.BlockSpec(position_bias.shape, lambda i: (0, 0)), block, block, block],
        out_specs=pl.BlockSpec((slots * tokens, CHUNK), lambda i: (0, 0)),
        compiler_params=pltpu.CompilerParams(vmem_limit_bytes=24 << 20),
        cost_estimate=pl.CostEstimate(
            flops=4 * scores * HEAD_DIM,
            bytes_accessed=8 * slots * tokens * CHUNK,
            transcendentals=scores,
        ),
    )(position_bias, queries, key_rows, values)


def device_index(rep, dp, tensor, dp_size):
    return (rep * dp_size + dp) * 2 + tensor


def ring_order(dp_size):
    half = dp_size // 2
    return [2 * i for i in range(half)] + [2 * i + 1 for i in reversed(range(half))]


def ring_pairs(reps, dp_size, way):
    order = ring_order(dp_size)
    pairs = []
    for rep in range(reps):
        step = way if rep == 0 else -way
        for place in range(dp_size):
            to = order[(place + step) % dp_size]
            for tensor in range(2):
                pairs.append(
                    (
                        device_index(rep, order[place], tensor, dp_size),
                        device_index(rep, to, tensor, dp_size),
                    )
                )
    return pairs


def block_of(distance):
    dp = lax.axis_index("dp")
    place = jnp.where(dp % 2 == 0, dp // 2, 7 - dp // 2)
    way = jnp.where(lax.axis_index("rep") == 0, 1, -1)
    place = (place - way * distance + 16) % 8
    return jnp.where(place < 4, 2 * place, 2 * (7 - place) + 1)


def project_kernel(plan, n_weights, *refs):
    context = refs[:4]
    weights = refs[4 : 4 + n_weights]
    kept_ref, sent_ref, product, sem = refs[-4:]
    tensor = lax.axis_index("tensor")

    def copies(slot, block):
        column = pl.multiple_of((block % 4) * CHUNK, CHUNK)
        source = product.at[slot]
        return (
            pltpu.make_async_copy(source, kept_ref.at[:, pl.ds(column, CHUNK)], sem.at[slot]),
            pltpu.make_async_copy(source, sent_ref.at[:, pl.ds(column, CHUNK)], sem.at[slot]),
        )

    for slot, (distance, pieces) in enumerate(plan):
        total = None
        for weight, row, column, rows in pieces:
            part = jnp.dot(
                context[column // CHUNK][:, column % CHUNK : column % CHUNK + rows],
                weights[weight][row : row + rows],
                preferred_element_type=jnp.float32,
            )
            total = part if total is None else total + part
        product[slot] = total.astype(jnp.bfloat16)
        block = block_of(distance)
        kept, sent = copies(slot, block)

        @pl.when(block // 4 == tensor)
        def _():
            kept.start()

        @pl.when(block // 4 != tensor)
        def _():
            sent.start()

    for slot, (distance, _) in enumerate(plan):
        copies(slot, jnp.int32(0))[0].wait()


def project(context, weights, plan, held):
    rows = context[0].shape[0]
    wide = jax.ShapeDtypeStruct((rows, 4 * CHUNK), jnp.bfloat16)
    vmem = pl.BlockSpec(memory_space=pltpu.VMEM)
    away = pl.BlockSpec(memory_space=pl.ANY)
    n_in = 4 + len(weights)
    return pl.pallas_call(
        functools.partial(project_kernel, plan, len(weights)),
        out_shape=[wide, wide],
        in_specs=[vmem] * n_in + [away] * len(held),
        out_specs=[away, away],
        scratch_shapes=[
            pltpu.VMEM((len(plan), rows, CHUNK), jnp.bfloat16),
            pltpu.SemaphoreType.DMA((len(plan),)),
        ],
        input_output_aliases={n_in: 0, n_in + 1: 1} if held else {},
        compiler_params=pltpu.CompilerParams(vmem_limit_bytes=24 << 20),
        cost_estimate=pl.CostEstimate(
            flops=len(plan) * 2 * rows * 4 * CHUNK * CHUNK,
            bytes_accessed=len(plan) * 2 * (rows * CHUNK + 4 * CHUNK * CHUNK),
            transcendentals=0,
        ),
    )(*context, *weights, *held)


def finish_kernel(counts_ref, donors_ref, kept_ref, other_ref, out_ref):
    slots = out_ref.shape[0]
    tokens = out_ref.shape[1]
    my_group = lax.axis_index("dp")
    second = donors_ref[0] == my_group
    for at in range(1, donors_ref.shape[0]):
        second = jnp.logical_or(second, donors_ref[at] == my_group)
    live = [counts_ref[0] >= 1, second]
    for slot in range(slots):
        rows = slice(slot * tokens, (slot + 1) * tokens)
        both = kept_ref[rows].astype(jnp.float32) + other_ref[rows].astype(jnp.float32)
        both = both * jnp.where(live[slot], 1.0, 0.0)
        out_ref[slot] = both.astype(jnp.bfloat16)


def finish(kept, other, counts, donors, slots):
    rows, columns = kept.shape
    width = CHUNK
    tokens = rows // slots
    smem = pl.BlockSpec(memory_space=pltpu.SMEM)
    block = pl.BlockSpec((rows, width), lambda i: (0, i))
    return pl.pallas_call(
        finish_kernel,
        out_shape=jax.ShapeDtypeStruct((slots, tokens, columns), jnp.bfloat16),
        grid=(columns // width,),
        in_specs=[smem, smem, block, block],
        out_specs=pl.BlockSpec((slots, tokens, width), lambda i: (0, 0, i)),
    )(counts, donors, kept, other)


def with_ring(queries, key_rows, values, position_bias, out_weight, counts, donors, reps, dp_size):
    slots = queries.shape[0]
    ahead = ring_pairs(reps, dp_size, 1)
    back = ring_pairs(reps, dp_size, -1)
    across = [
        (device_index(r, d, t, dp_size), device_index(1 - r, d, t, dp_size))
        for r in range(2)
        for d in range(dp_size)
        for t in range(2)
    ]
    cores = [
        (device_index(r, d, t, dp_size), device_index(r, d, 1 - t, dp_size))
        for r in range(2)
        for d in range(dp_size)
        for t in range(2)
    ]
    send = lambda value, pairs: lax.ppermute(value, AXES, pairs)
    depth = out_weight.shape[0]
    cut = depth // 4

    def attention(chunk, held):
        return attend(queries, key_rows, values, held, chunk)

    upper, lower = out_weight[: depth - cut], out_weight[cut:]
    p1, q1 = send(upper, ahead), send(lower, back)
    c0 = attention(0, position_bias)
    c1 = attention(1, position_bias)
    p1, q1, c0, c1, bias = lax.optimization_barrier((p1, q1, c0, c1, position_bias))

    edge = lambda p, q: jnp.concatenate([p[:cut], q[-cut:]], axis=0)
    p2, q2, y1 = send(p1, ahead), send(q1, back), send(edge(p1, q1), across)
    c2 = attention(2, bias)
    c3 = attention(3, bias)
    p2, q2, y1, c2, c3 = lax.optimization_barrier((p2, q2, y1, c2, c3))
    context = (c0, c1, c2, c3)

    def block_pieces(p, y):
        head = [(p, CHUNK * i, CHUNK * i, CHUNK) for i in range(3)]
        return head + [(y, CHUNK, 3 * CHUNK, CHUNK)]

    def block_pieces_back(q, y):
        tail = [(q, CHUNK * i, CHUNK * (i + 1), CHUNK) for i in range(3)]
        return [(y, 0, 0, CHUNK)] + tail

    p3, q3, y2 = send(p2, ahead), send(q2, back), send(edge(p2, q2), across)
    own = [(0, CHUNK * i, CHUNK * i, CHUNK) for i in range(4)]
    held = project(
        context,
        (out_weight, p1, q1, y1),
        [(0, own), (1, block_pieces(1, 3)), (-1, block_pieces_back(2, 3))],
        (),
    )
    p3, q3, y2, held = lax.optimization_barrier((p3, q3, y2, held))

    half = depth // 2
    p4, q4 = send(p3[:half], ahead), send(q3[-half:], back)
    y3 = send(edge(p3, q3), across)
    held = project(
        context,
        (p2, q2, y2),
        [(2, block_pieces(0, 2)), (-2, block_pieces_back(1, 2))],
        held,
    )
    p4, q4, y3, held = lax.optimization_barrier((p4, q4, y3, held))
    opposite = [(3, 0, 0, CHUNK), (3, CHUNK, CHUNK, CHUNK)]
    opposite += [(4, 0, 2 * CHUNK, CHUNK), (4, CHUNK, 3 * CHUNK, CHUNK)]
    kept, sent = project(
        context,
        (p3, q3, y3, p4, q4),
        [(3, block_pieces(0, 2)), (-3, block_pieces_back(1, 2)), (4, opposite)],
        held,
    )
    return finish(kept, send(sent, cores), counts, donors, slots)


def with_gather(queries, key_rows, values, position_bias, out_weight, counts, donors):
    slots, tokens, features = queries.shape
    whole = lax.all_gather(out_weight, "dp", axis=1, tiled=True)
    context = jnp.concatenate(
        [attend(queries, key_rows, values, position_bias, i) for i in range(features // CHUNK)],
        axis=1,
    )
    product = jnp.dot(context, whole, preferred_element_type=jnp.float32).astype(jnp.bfloat16)
    merged = lax.psum_scatter(product, "tensor", scatter_dimension=1, tiled=True)
    first_live = counts[0] >= 1
    second_live = jnp.any(donors == lax.axis_index("dp"))
    live = jnp.stack([first_live, second_live]).astype(jnp.bfloat16)
    return merged.reshape(slots, tokens, merged.shape[1]) * live[:, None, None]


def solution(mesh):
    in_specs = (
        P(("rep", "dp"), None, "tensor"),
        P(("rep", "dp"), None, "tensor"),
        P(("rep", "dp"), None, "tensor"),
        P(None, "tensor"),
        P("tensor", "dp"),
        P(("rep", "dp")),
        P("rep"),
    )
    out_specs = P(("rep", "dp"), None, "tensor")
    reps, dp_size = mesh.shape["rep"], mesh.shape["dp"]
    if reps == 2 and dp_size == 8 and mesh.shape["tensor"] == 2:
        on_device = functools.partial(with_ring, reps=reps, dp_size=dp_size)
    else:
        on_device = with_gather
    return jax.shard_map(
        on_device, mesh=mesh, in_specs=in_specs, out_specs=out_specs, check_vma=False
    )
```

time: 111 us -> 57.9 us (0.52)
  waiting for transfers between devices: 61.9 us -> 10 us
  matrix products: 21 us -> 0 us
  Pallas kernels: 0 us -> 21 us
  starting transfers between devices: 0.04 us -> 13.7 us
  between operations: 14.1 us -> 0.82 us
  other arithmetic: 3.87 us -> 0.76 us
  local copies, waits for them, and re-layouts: 9.27 us -> 11.2 us
    all_gather x1 -> x0, waiting for transfers between devices: 55.3 us -> none  [on_device(): lax.all_gather(out_weight, 'dp', axis=1, tiled=True)]
    pallas_call x0 -> x8, Pallas kernels: none -> 21 us  [the longest x4 9.64 us: attend(): pl.pallas_call(functools.partial(attention_kernel, chunk * heads), out_sh...]
    dot_general x3 -> x0, matrix products: 14.4 us -> none  [the longest x1 5.92 us: on_device(): jnp.dot(row_block, lax.all_gather(out_weight, 'dp', axis=1, tiled=True),...]
    ppermute x0 -> x12, starting transfers between devices: none -> 13.7 us  [with_ring(): send = lambda value, pairs: lax.ppermute(value, AXES, pairs)]
    ppermute x0 -> x12, waiting for transfers between devices: none -> 10 us  [with_ring(): send = lambda value, pairs: lax.ppermute(value, AXES, pairs)]
    sub x1 -> x0, matrix products: 6.59 us -> none  [attend(): expd = jnp.exp(scores - highest)]
    reduce_scatter x1 -> x0, waiting for transfers between devices: 5.93 us -> none  [on_device(): lax.psum_scatter(jnp.dot(row_block, lax.all_gather(out_weight, 'dp', axis...]
    slice x0 -> x9, local copies, waits for them, and re-layouts: none -> 5.87 us  [the longest x6 3.67 us: with_ring(): edge = lambda p, q: jnp.concatenate([p[:cut], q[-cut:]], axis=0)]
  transfers between devices with their start and end apart: 2 -> 12, of which waited for: 2 -> 8; matrix products, arithmetic and copies ran while one was open for 23% -> 8% of each run, Pallas kernels for 0% -> 27%
where the time goes in v1:
time: 57.9 us; the launch traced here: 57.5 us
  Pallas kernels  21 us (36%)
  starting transfers between devices  13.7 us (24%)
  local copies, waits for them, and re-layouts  11.2 us (19%)
  waiting for transfers between devices  10 us (17%)
  between operations  0.82 us (1%)
  other arithmetic  0.76 us (1%)
    ppermute x12, starting transfers between devices, with_ring(): send = lambda value, pairs: lax.ppermute(value, AXES, pairs)  13.7 us
    ppermute x12, waiting for transfers between devices, with_ring(): send = lambda value, pairs: lax.ppermute(value, AXES, pairs)  10 us
    pallas_call x4, Pallas kernels, attend(): pl.pallas_call(functools.partial(attention_kernel, chunk * heads), out_sh...  9.64 us
    pallas_call x3, Pallas kernels, project(): pl.pallas_call(functools.partial(project_kernel, plan, len(weights)), out...  7.7 us
    unnamed x23, local copies, waits for them, and re-layouts  5.24 us
    pallas_call x1, Pallas kernels, finish(): pl.pallas_call(finish_kernel, out_shape=jax.ShapeDtypeStruct((slots, toke...  3.68 us
    slice x6, local copies, waits for them, and re-layouts, with_ring(): edge = lambda p, q: jnp.concatenate([p[:cut], q[-cut:]], axis=0)  3.67 us
    slice x1, local copies, waits for them, and re-layouts, with_ring(): upper, lower = (out_weight[:depth - cut], out_weight[cut:])  2.16 us
  transfers between devices with their start and end apart: 12, of which 8 were waited for; matrix products, arithmetic and copies ran while one was open for 8% of the time, Pallas kernels for 27%

profile of v1, /device:TPU:0, one launch (start us, length us, event | category | flops | bytes accessed | tf_op | source)
XLA Modules:
  0.0 57.5 jit_solution(1024643938069647687)
XLA Ops:
  0.0 2.2 %fusion = (bf16[768,256]{1,0:T(8,128)(2,1)}, bf16[768,256]{1,0:T(8,128)(2,1)}) fusion(bf16[1024,256]{1,0:T(8,128)(2,1)} %refs_4_.1), kind=kLoop, calls=%fused_computation.3 | loop fusion | bytes 1572864 | tf_op jit(solution)/shard_map/slice | solution.py:245
  2.2 3.0 %collective-permute-start = (bf16[768,256]{1,0:T(8,128)(2,1)}, bf16[768,256]{1,0:T(8,128)(2,1)}, u32[]{:S(2)}, u32[]{:S(2)}) collective-permute-start(bf16[768,256]{1,0:T(8,128)(2,1)} %get-tuple-element.58), channel_id=1, source_target_pairs={{0,4},{1,5},{4,8},{5,9},{8,12},{9,13},{12,14},{13,15},{14,10},{15,... | collective-permute-start | bytes 1179656 | tf_op jit(solution)/shard_map/ppermute | solution.py:238
  5.3 1.2 %copy-done.1 = bf16[2,256,1024]{2,1,0:T(8,128)(2,1)S(1)} copy-done((bf16[2,256,1024]{2,1,0:T(8,128)(2,1)S(1)}, bf16[2,256,1024]{2,1,0:T(8,128)(2,1)}, u32[]{:S(2)}) %copy-start.1) | copy-done | bytes 1048600
  6.5 1.2 %copy-done.3 = bf16[2,256,1024]{2,1,0:T(8,128)(2,1)S(1)} copy-done((bf16[2,256,1024]{2,1,0:T(8,128)(2,1)S(1)}, bf16[2,256,1024]{2,1,0:T(8,128)(2,1)}, u32[]{:S(2)}) %copy-start.3) | copy-done | bytes 1048600
  7.7 2.4 %shard_map.73.refs_0_ = bf16[512,256]{1,0:T(8,128)(2,1)S(1)} custom-call(f32[32,16]{1,0:T(8,128)S(1)} %copy.12.bias_ref, bf16[2,256,1024]{2,1,0:T(8,128)(2,1)S(1)} %copy-done, bf16[2,256,1024]{2,1,0:T(8,128)(2,1)S(1)} %copy-done.1, bf16[2,256,1024]{2,1,0:T(8,128)(2,1)S(1)} %copy-done.3), custom_call_target="tpu_custom_call" | custom-call | flops 134217728 | bytes 1048576 | tf_op jit(solution)/shard_map/pallas_call | solution.py:79
  10.1 2.4 %shard_map.74.refs_1_ = bf16[512,256]{1,0:T(8,128)(2,1)S(1)} custom-call(f32[32,16]{1,0:T(8,128)S(1)} %copy.12.bias_ref, bf16[2,256,1024]{2,1,0:T(8,128)(2,1)S(1)} %copy-done, bf16[2,256,1024]{2,1,0:T(8,128)(2,1)S(1)} %copy-done.1, bf16[2,256,1024]{2,1,0:T(8,128)(2,1)S(1)} %copy-done.3), custom_call_target="tpu_custom_call" | custom-call | flops 134217728 | bytes 1048576 | tf_op jit(solution)/shard_map/pallas_call | solution.py:79
  13.3 1.2 %collective-permute-done.refs_5_ = bf16[768,256]{1,0:T(8,128)(2,1)} collective-permute-done((bf16[768,256]{1,0:T(8,128)(2,1)}, bf16[768,256]{1,0:T(8,128)(2,1)}, u32[]{:S(2)}, u32[]{:S(2)}) %collective-permute-start) | collective-permute-done | bytes 393248 | tf_op jit(solution)/shard_map/ppermute | solution.py:238
  14.5 1.5 %collective-permute-done.1.refs_6_ = bf16[768,256]{1,0:T(8,128)(2,1)} collective-permute-done((bf16[768,256]{1,0:T(8,128)(2,1)}, bf16[768,256]{1,0:T(8,128)(2,1)}, u32[]{:S(2)}, u32[]{:S(2)}) %collective-permute-start.1) | collective-permute-done | bytes 393248 | tf_op jit(solution)/shard_map/ppermute | solution.py:238
  16.1 1.6 %collective-permute-start.2 = (bf16[768,256]{1,0:T(8,128)(2,1)}, bf16[768,256]{1,0:T(8,128)(2,1)}, u32[]{:S(2)}, u32[]{:S(2)}) collective-permute-start(bf16[768,256]{1,0:T(8,128)(2,1)} %collective-permute-done.refs_5_), channel_id=1, source_target_pairs={{0,4},{1,5},{4,8},{5,9},{8,12},{9,13},{12,14},{13,15},{14,10},{15,... | collective-permute-start | bytes 1179656 | tf_op jit(solution)/shard_map/ppermute | solution.py:238
  20.7 1.4 %collective-permute-start.4 = (bf16[512,256]{1,0:T(8,128)(2,1)}, bf16[512,256]{1,0:T(8,128)(2,1)}, u32[]{:S(2)}, u32[]{:S(2)}) collective-permute-start(bf16[512,256]{1,0:T(8,128)(2,1)} %pad_maximum_fusion), channel_id=1, source_target_pairs={{0,16},{1,17},{2,18},{3,19},{4,20},{5,21},{6,22},{7,23},{8,24},{9,... | collective-permute-start | bytes 786440 | tf_op jit(solution)/shard_map/ppermute | solution.py:238
  22.2 2.4 %shard_map.75.refs_2_ = bf16[512,256]{1,0:T(8,128)(2,1)S(1)} custom-call(f32[32,16]{1,0:T(8,128)S(1)} %copy.14.bias_ref, bf16[2,256,1024]{2,1,0:T(8,128)(2,1)S(1)} %copy-done, bf16[2,256,1024]{2,1,0:T(8,128)(2,1)S(1)} %copy-done.2, bf16[2,256,1024]{2,1,0:T(8,128)(2,1)S(1)} %copy-done.4), custom_call_target="tpu_custom_call" | custom-call | flops 134217728 | bytes 1048576 | tf_op jit(solution)/shard_map/pallas_call | solution.py:79
  24.6 2.4 %shard_map.76.refs_3_ = bf16[512,256]{1,0:T(8,128)(2,1)S(1)} custom-call(f32[32,16]{1,0:T(8,128)S(1)} %copy.14.bias_ref, bf16[2,256,1024]{2,1,0:T(8,128)(2,1)S(1)} %copy-done, bf16[2,256,1024]{2,1,0:T(8,128)(2,1)S(1)} %copy-done.2, bf16[2,256,1024]{2,1,0:T(8,128)(2,1)S(1)} %copy-done.4), custom_call_target="tpu_custom_call" | custom-call | flops 134217728 | bytes 1048576 | tf_op jit(solution)/shard_map/pallas_call | solution.py:79
  27.4 1.6 %collective-permute-start.5 = (bf16[768,256]{1,0:T(8,128)(2,1)}, bf16[768,256]{1,0:T(8,128)(2,1)S(1)}, u32[]{:S(2)}, u32[]{:S(2)}) collective-permute-start(bf16[768,256]{1,0:T(8,128)(2,1)} %collective-permute-done.2.refs_4_), channel_id=1, source_target_pairs={{0,4},{1,5},{4,8},{5,9},{8,12},{9,13},{12,14},{13,15},{14,10},{15,... | collective-permute-start | bytes 1179656 | tf_op jit(solution)/shard_map/ppermute | solution.py:238
  31.3 1.5 %collective-permute-start.7 = (bf16[512,256]{1,0:T(8,128)(2,1)S(1)}, bf16[512,256]{1,0:T(8,128)(2,1)S(1)}, u32[]{:S(2)}, u32[]{:S(2)}) collective-permute-start(bf16[512,256]{1,0:T(8,128)(2,1)S(1)} %pad_maximum_fusion.1), channel_id=1, source_target_pairs={{0,16},{1,17},{2,18},{3,19},{4,20},{5,21},{6,22},{7,23},{8,24},{9,... | collective-permute-start | bytes 786440 | tf_op jit(solution)/shard_map/ppermute | solution.py:238
  32.8 3.1 %shard_map.77 = (bf16[512,1024]{1,0:T(8,128)(2,1)S(1)}, bf16[512,1024]{1,0:T(8,128)(2,1)S(1)}) custom-call(bf16[512,256]{1,0:T(8,128)(2,1)S(1)} %shard_map.73.refs_0_, bf16[512,256]{1,0:T(8,128)(2,1)S(1)} %copy-done.7, bf16[512,256]{1,0:T(8,128)(2,1)S(1)} %shard_map.75.refs_2_, bf16[512,256]{1,0:T(8,128)(2,1)S(1)} %shard_map.76.refs_3_, ...), custom_call_target="tpu_custom_call" | custom-call | flops 805306368 | bytes 2359296 | tf_op jit(solution)/shard_map/pallas_call | solution.py:173
  35.9 2.8 %collective-permute-done.7.refs_6_ = bf16[512,256]{1,0:T(8,128)(2,1)S(1)} collective-permute-done((bf16[512,256]{1,0:T(8,128)(2,1)S(1)}, bf16[512,256]{1,0:T(8,128)(2,1)S(1)}, u32[]{:S(2)}, u32[]{:S(2)}) %collective-permute-start.7) | collective-permute-done | bytes 262176 | tf_op jit(solution)/shard_map/ppermute | solution.py:238
  38.8 1.6 %collective-permute-start.10 = (bf16[512,256]{1,0:T(8,128)(2,1)S(1)}, bf16[512,256]{1,0:T(8,128)(2,1)S(1)}, u32[]{:S(2)}, u32[]{:S(2)}) collective-permute-start(bf16[512,256]{1,0:T(8,128)(2,1)S(1)} %pad_maximum_fusion.2), channel_id=1, source_target_pairs={{0,16},{1,17},{2,18},{3,19},{4,20},{5,21},{6,22},{7,23},{8,24},{9,... | collective-permute-start | bytes 786440 | tf_op jit(solution)/shard_map/ppermute | solution.py:238
  40.8 1.7 %collective-permute-start.9 = (bf16[512,256]{1,0:T(8,128)(2,1)S(1)}, bf16[512,256]{1,0:T(8,128)(2,1)S(1)}, u32[]{:S(2)}, u32[]{:S(2)}) collective-permute-start(bf16[512,256]{1,0:T(8,128)(2,1)S(1)} %slice.37), channel_id=1, source_target_pairs={{0,2},{1,3},{4,0},{5,1},{8,4},{9,5},{12,8},{13,9},{14,12},{15,13},... | collective-permute-start | bytes 786440 | tf_op jit(solution)/shard_map/ppermute | solution.py:238
  42.5 2.6 %shard_map.78 = (bf16[512,1024]{1,0:T(8,128)(2,1)S(1)}, bf16[512,1024]{1,0:T(8,128)(2,1)S(1)}) custom-call(bf16[512,256]{1,0:T(8,128)(2,1)S(1)} %shard_map.73.refs_0_, bf16[512,256]{1,0:T(8,128)(2,1)S(1)} %copy-done.7, bf16[512,256]{1,0:T(8,128)(2,1)S(1)} %shard_map.75.refs_2_, ...), custom_call_target="tpu_custom_call", output_to_operand_aliasing={{0}: (7, {}), {1}: (8, {})} | custom-call | flops 536870912 | bytes 1572864 | tf_op jit(solution)/shard_map/pallas_call | solution.py:173
  45.3 1.5 %collective-permute-done.8.refs_7_ = bf16[512,256]{1,0:T(8,128)(2,1)S(1)} collective-permute-done((bf16[512,256]{1,0:T(8,128)(2,1)S(1)}, bf16[512,256]{1,0:T(8,128)(2,1)S(1)}, u32[]{:S(2)}, u32[]{:S(2)}) %collective-permute-start.8) | collective-permute-done | bytes 262176 | tf_op jit(solution)/shard_map/ppermute | solution.py:238
  47.2 2.0 %shard_map.79 = (bf16[512,1024]{1,0:T(8,128)(2,1)S(1)}, bf16[512,1024]{1,0:T(8,128)(2,1)S(1)}) custom-call(bf16[512,256]{1,0:T(8,128)(2,1)S(1)} %shard_map.73.refs_0_, bf16[512,256]{1,0:T(8,128)(2,1)S(1)} %copy-done.7, bf16[512,256]{1,0:T(8,128)(2,1)S(1)} %shard_map.75.refs_2_, ...), custom_call_target="tpu_custom_call", output_to_operand_aliasing={{0}: (9, {}), {1}: (10, {})} | custom-call | flops 805306368 | bytes 2359296 | tf_op jit(solution)/shard_map/pallas_call | solution.py:173
  49.2 1.0 %copy-done.5 = bf16[512,1024]{1,0:T(8,128)(2,1)} copy-done((bf16[512,1024]{1,0:T(8,128)(2,1)}, bf16[512,1024]{1,0:T(8,128)(2,1)S(1)}, u32[]{:S(2)}) %copy-start.5) | copy-done | bytes 1048600
  50.8 2.0 %collective-permute-done.11.other_ref = bf16[512,1024]{1,0:T(8,128)(2,1)S(1)} collective-permute-done((bf16[512,1024]{1,0:T(8,128)(2,1)S(1)}, bf16[512,1024]{1,0:T(8,128)(2,1)S(1)}, u32[]{:S(2)}, u32[]{:S(2)}) %collective-permute-start.11) | collective-permute-done | bytes 1048608 | tf_op jit(solution)/shard_map/ppermute | solution.py:238
  53.8 3.7 %shard_map.80 = bf16[2,256,1024]{2,1,0:T(8,128)(2,1)} custom-call(s32[1]{0:T(128)S(6)} %copy.20.counts_ref, s32[4]{0:T(128)} %donors_ref.1, bf16[512,1024]{1,0:T(8,128)(2,1)} %copy-done.5, bf16[512,1024]{1,0:T(8,128)(2,1)} %copy-done.9), custom_call_target="tpu_custom_call" | custom-call | tf_op jit(solution)/shard_map/pallas_call | solution.py:213
  (44 shorter events, 8.5 us)
Async XLA Ops:
  0.0 5.3 %copy-start = (bf16[2,256,1024]{2,1,0:T(8,128)(2,1)S(1)}, bf16[2,256,1024]{2,1,0:T(8,128)(2,1)}, u32[]{:S(2)}) copy-start(bf16[2,256,1024]{2,1,0:T(8,128)(2,1)} %query_ref.7) | copy-start | bytes 3145732
  0.0 5.2 %copy-start.10 = (f32[32,16]{0,1:T(8,128)S(1)}, f32[32,16]{0,1:T(8,128)}, u32[]{:S(2)}) copy-start(f32[32,16]{0,1:T(8,128)} %param.10) | copy-start | bytes 6148
  2.2 12.4 %collective-permute-start = (bf16[768,256]{1,0:T(8,128)(2,1)}, bf16[768,256]{1,0:T(8,128)(2,1)}, u32[]{:S(2)}, u32[]{:S(2)}) collective-permute-start(bf16[768,256]{1,0:T(8,128)(2,1)} %get-tuple-element.58), channel_id=1, source_target_pairs={{0,4},{1,5},{4,8},{5,9},{8,12},{9,13},{12,14},{13,15},{14,10},{15,... | collective-permute-start | bytes 1179656 | tf_op jit(solution)/shard_map/ppermute | solution.py:238
  5.2 10.9 %collective-permute-start.1 = (bf16[768,256]{1,0:T(8,128)(2,1)}, bf16[768,256]{1,0:T(8,128)(2,1)}, u32[]{:S(2)}, u32[]{:S(2)}) collective-permute-start(bf16[768,256]{1,0:T(8,128)(2,1)} %get-tuple-element.57), channel_id=1, source_target_pairs={{0,2},{1,3},{4,0},{5,1},{8,4},{9,5},{12,8},{13,9},{14,12},{15,13},... | collective-permute-start | bytes 1179656 | tf_op jit(solution)/shard_map/ppermute | solution.py:238
  5.3 1.2 %copy-start.1 = (bf16[2,256,1024]{2,1,0:T(8,128)(2,1)S(1)}, bf16[2,256,1024]{2,1,0:T(8,128)(2,1)}, u32[]{:S(2)}) copy-start(bf16[2,256,1024]{2,1,0:T(8,128)(2,1)} %key_ref.7) | copy-start | bytes 3145732
  6.5 1.2 %copy-start.3 = (bf16[2,256,1024]{2,1,0:T(8,128)(2,1)S(1)}, bf16[2,256,1024]{2,1,0:T(8,128)(2,1)}, u32[]{:S(2)}) copy-start(bf16[2,256,1024]{2,1,0:T(8,128)(2,1)} %value_ref.7) | copy-start | bytes 3145732
  10.1 12.0 %copy-start.4 = (bf16[2,256,1024]{2,1,0:T(8,128)(2,1)S(1)}, bf16[2,256,1024]{2,1,0:T(8,128)(2,1)}, u32[]{:S(2)}) copy-start(bf16[2,256,1024]{2,1,0:T(8,128)(2,1)} %value_ref.7) | copy-start | bytes 3145732
  12.6 0.7 %copy-start.6 = (bf16[512,256]{1,0:T(8,128)(2,1)}, bf16[512,256]{1,0:T(8,128)(2,1)S(1)}, u32[]{:S(2)}) copy-start(bf16[512,256]{1,0:T(8,128)(2,1)S(1)} %shard_map.74.refs_1_) | copy-start | bytes 786436
  13.3 8.9 %copy-start.2 = (bf16[2,256,1024]{2,1,0:T(8,128)(2,1)S(1)}, bf16[2,256,1024]{2,1,0:T(8,128)(2,1)}, u32[]{:S(2)}) copy-start(bf16[2,256,1024]{2,1,0:T(8,128)(2,1)} %key_ref.7) | copy-start | bytes 3145732
  16.1 11.3 %collective-permute-start.2 = (bf16[768,256]{1,0:T(8,128)(2,1)}, bf16[768,256]{1,0:T(8,128)(2,1)}, u32[]{:S(2)}, u32[]{:S(2)}) collective-permute-start(bf16[768,256]{1,0:T(8,128)(2,1)} %collective-permute-done.refs_5_), channel_id=1, source_target_pairs={{0,4},{1,5},{4,8},{5,9},{8,12},{9,13},{12,14},{13,15},{14,10},{15,... | collective-permute-start | bytes 1179656 | tf_op jit(solution)/shard_map/ppermute | solution.py:238
  17.7 9.7 %collective-permute-start.3 = (bf16[768,256]{1,0:T(8,128)(2,1)}, bf16[768,256]{1,0:T(8,128)(2,1)}, u32[]{:S(2)}, u32[]{:S(2)}) collective-permute-start(bf16[768,256]{1,0:T(8,128)(2,1)} %collective-permute-done.1.refs_6_), channel_id=1, source_target_pairs={{0,2},{1,3},{4,0},{5,1},{8,4},{9,5},{12,8},{13,9},{14,12},{15,13},... | collective-permute-start | bytes 1179656 | tf_op jit(solution)/shard_map/ppermute | solution.py:238
  20.7 6.7 %collective-permute-start.4 = (bf16[512,256]{1,0:T(8,128)(2,1)}, bf16[512,256]{1,0:T(8,128)(2,1)}, u32[]{:S(2)}, u32[]{:S(2)}) collective-permute-start(bf16[512,256]{1,0:T(8,128)(2,1)} %pad_maximum_fusion), channel_id=1, source_target_pairs={{0,16},{1,17},{2,18},{3,19},{4,20},{5,21},{6,22},{7,23},{8,24},{9,... | collective-permute-start | bytes 786440 | tf_op jit(solution)/shard_map/ppermute | solution.py:238
  27.0 5.7 %copy-start.8 = (bf16[1024,256]{1,0:T(8,128)(2,1)S(1)}, bf16[1024,256]{1,0:T(8,128)(2,1)}, u32[]{:S(2)}) copy-start(bf16[1024,256]{1,0:T(8,128)(2,1)} %refs_4_.1) | copy-start | bytes 1572868
  27.4 11.3 %collective-permute-start.5 = (bf16[768,256]{1,0:T(8,128)(2,1)}, bf16[768,256]{1,0:T(8,128)(2,1)S(1)}, u32[]{:S(2)}, u32[]{:S(2)}) collective-permute-start(bf16[768,256]{1,0:T(8,128)(2,1)} %collective-permute-done.2.refs_4_), channel_id=1, source_target_pairs={{0,4},{1,5},{4,8},{5,9},{8,12},{9,13},{12,14},{13,15},{14,10},{15,... | collective-permute-start | bytes 1179656 | tf_op jit(solution)/shard_map/ppermute | solution.py:238
  28.9 9.8 %collective-permute-start.6 = (bf16[768,256]{1,0:T(8,128)(2,1)}, bf16[768,256]{1,0:T(8,128)(2,1)S(1)}, u32[]{:S(2)}, u32[]{:S(2)}) collective-permute-start(bf16[768,256]{1,0:T(8,128)(2,1)} %collective-permute-done.3.refs_5_), channel_id=1, source_target_pairs={{0,2},{1,3},{4,0},{5,1},{8,4},{9,5},{12,8},{13,9},{14,12},{15,13},... | collective-permute-start | bytes 1179656 | tf_op jit(solution)/shard_map/ppermute | solution.py:238
  31.2 1.5 %copy-start.7 = (bf16[512,256]{1,0:T(8,128)(2,1)S(1)}, bf16[512,256]{1,0:T(8,128)(2,1)}, u32[]{:S(2)}) copy-start(bf16[512,256]{1,0:T(8,128)(2,1)} %copy-done.6) | copy-start | bytes 786436
  31.3 7.4 %collective-permute-start.7 = (bf16[512,256]{1,0:T(8,128)(2,1)S(1)}, bf16[512,256]{1,0:T(8,128)(2,1)S(1)}, u32[]{:S(2)}, u32[]{:S(2)}) collective-permute-start(bf16[512,256]{1,0:T(8,128)(2,1)S(1)} %pad_maximum_fusion.1), channel_id=1, source_target_pairs={{0,16},{1,17},{2,18},{3,19},{4,20},{5,21},{6,22},{7,23},{8,24},{9,... | collective-permute-start | bytes 786440 | tf_op jit(solution)/shard_map/ppermute | solution.py:238
  38.8 6.4 %collective-permute-start.10 = (bf16[512,256]{1,0:T(8,128)(2,1)S(1)}, bf16[512,256]{1,0:T(8,128)(2,1)S(1)}, u32[]{:S(2)}, u32[]{:S(2)}) collective-permute-start(bf16[512,256]{1,0:T(8,128)(2,1)S(1)} %pad_maximum_fusion.2), channel_id=1, source_target_pairs={{0,16},{1,17},{2,18},{3,19},{4,20},{5,21},{6,22},{7,23},{8,24},{9,... | collective-permute-start | bytes 786440 | tf_op jit(solution)/shard_map/ppermute | solution.py:238
  40.4 6.4 %collective-permute-start.8 = (bf16[512,256]{1,0:T(8,128)(2,1)S(1)}, bf16[512,256]{1,0:T(8,128)(2,1)S(1)}, u32[]{:S(2)}, u32[]{:S(2)}) collective-permute-start(bf16[512,256]{1,0:T(8,128)(2,1)S(1)} %slice.36), channel_id=1, source_target_pairs={{0,4},{1,5},{4,8},{5,9},{8,12},{9,13},{12,14},{13,15},{14,10},{15,... | collective-permute-start | bytes 786440 | tf_op jit(solution)/shard_map/ppermute | solution.py:238
  40.8 6.4 %collective-permute-start.9 = (bf16[512,256]{1,0:T(8,128)(2,1)S(1)}, bf16[512,256]{1,0:T(8,128)(2,1)S(1)}, u32[]{:S(2)}, u32[]{:S(2)}) collective-permute-start(bf16[512,256]{1,0:T(8,128)(2,1)S(1)} %slice.37), channel_id=1, source_target_pairs={{0,2},{1,3},{4,0},{5,1},{8,4},{9,5},{12,8},{13,9},{14,12},{15,13},... | collective-permute-start | bytes 786440 | tf_op jit(solution)/shard_map/ppermute | solution.py:238
  49.1 1.0 %copy-start.5 = (bf16[512,1024]{1,0:T(8,128)(2,1)}, bf16[512,1024]{1,0:T(8,128)(2,1)S(1)}, u32[]{:S(2)}) copy-start(bf16[512,1024]{1,0:T(8,128)(2,1)S(1)} %get-tuple-element.55.kept_ref) | copy-start | bytes 3145732
  50.2 2.7 %collective-permute-start.11 = (bf16[512,1024]{1,0:T(8,128)(2,1)S(1)}, bf16[512,1024]{1,0:T(8,128)(2,1)S(1)}, u32[]{:S(2)}, u32[]{:S(2)}) collective-permute-start(bf16[512,1024]{1,0:T(8,128)(2,1)S(1)} %get-tuple-element.56), channel_id=1, source_target_pairs={{0,1},{1,0},{2,3},{3,2},{4,5},{5,4},{6,7},{7,6},{8,9},{9,8},{10,11... | collective-permute-start | bytes 3145736 | tf_op jit(solution)/shard_map/ppermute | solution.py:238
  52.8 1.0 %copy-start.9 = (bf16[512,1024]{1,0:T(8,128)(2,1)}, bf16[512,1024]{1,0:T(8,128)(2,1)S(1)}, u32[]{:S(2)}) copy-start(bf16[512,1024]{1,0:T(8,128)(2,1)S(1)} %collective-permute-done.11.other_ref) | copy-start | bytes 3145732

commit v2 on v0

v2 whole, which is shorter than its diff:
```python
import functools

import jax
import jax.numpy as jnp
from jax import lax
from jax.experimental import pallas as pl
from jax.experimental.pallas import tpu as pltpu
from jax.sharding import PartitionSpec as P

HEAD_DIM = 64
PAIR = 2 * HEAD_DIM
CHUNK = 256
THRESHOLDS = (12, 16, 23, 32, 46, 64, 91)
AXES = ("rep", "dp", "tensor")


def bias_rows(position_bias, tokens):
    bucket_count = position_bias.shape[1]
    shape = (bucket_count, 2 * tokens)
    relative = lax.broadcasted_iota(jnp.int32, shape, 1) - (tokens - 1)
    distance = jnp.abs(relative)
    far = jnp.full(shape, 8, jnp.int32)
    for threshold in THRESHOLDS:
        far = far + jnp.where(distance >= threshold, 1, 0)
    bucket = jnp.where(distance < 8, distance, far) + jnp.where(relative > 0, 16, 0)
    one_hot = jnp.where(bucket == lax.broadcasted_iota(jnp.int32, shape, 0), 1.0, 0.0)
    return lax.dot_general(
        position_bias,
        one_hot,
        (((1,), (0,)), ((), ())),
        precision=lax.Precision.HIGHEST,
        preferred_element_type=jnp.float32,
    )


def attention_kernel(first, bias_ref, *refs):
    sources, (out_ref, held, sem) = refs[:3], refs[-3:]
    count, _, slots, tokens, width = held.shape
    copies = [
        [
            pltpu.make_async_copy(
                source.at[:, :, (first + chunk) * width : (first + chunk + 1) * width],
                held.at[chunk, at],
                sem.at[chunk, at],
            )
            for at, source in enumerate(sources)
        ]
        for chunk in range(count)
    ]
    for chunk in copies:
        for copy in chunk:
            copy.start()
    rows = bias_rows(bias_ref[...], tokens)
    lower = lax.broadcasted_iota(jnp.int32, (tokens, PAIR), 1) < HEAD_DIM
    for chunk in range(count):
        for copy in copies[chunk]:
            copy.wait()
        for pair in range(width // PAIR):
            columns = slice(pair * PAIR, (pair + 1) * PAIR)
            head = (first + chunk) * (width // HEAD_DIM) + 2 * pair
            terms = [toeplitz(rows[head + i : head + i + 1], tokens) for i in range(2)]
            for slot in range(slots):
                query, key, value = (held[chunk, at, slot, :, columns] for at in range(3))
                sums = []
                for i in range(2):
                    own = lower if i == 0 else jnp.logical_not(lower)
                    scores = lax.dot_general(
                        query,
                        jnp.where(own, key, 0),
                        (((1,), (1,)), ((), ())),
                        preferred_element_type=jnp.float32,
                    )
                    scores = scores + terms[i]
                    highest = jnp.max(scores, axis=-1, keepdims=True)
                    expd = jnp.exp(scores - highest).astype(jnp.bfloat16)
                    sums.append(
                        jnp.dot(expd, jnp.where(own, value, 1), preferred_element_type=jnp.float32)
                    )
                weighted = jnp.where(lower, sums[0], sums[1])
                total = pltpu.roll(jnp.where(lower, sums[1], sums[0]), HEAD_DIM, 1)
                at = slice(chunk * width + pair * PAIR, chunk * width + (pair + 1) * PAIR)
                out_ref[slot * tokens : (slot + 1) * tokens, at] = (weighted / total).astype(
                    jnp.bfloat16
                )


def toeplitz(row, tokens):
    spread = jnp.broadcast_to(row, (8, 2 * tokens))
    base = pltpu.roll(spread, tokens + 1, 1, stride=1, stride_axis=0)
    rolled = [base if i == 0 else pltpu.roll(base, 8 * i, 1) for i in range(16)]
    groups = []
    for group in range(tokens // 8):
        turned, whole = rolled[group % 16], group // 16 * 128
        if whole:
            turned = jnp.concatenate([turned[:, -whole:], turned[:, : tokens - whole]], axis=1)
        groups.append(turned[:, :tokens])
    return jnp.concatenate(groups, axis=0)


def attend(queries, key_rows, values, position_bias, first, count, after=()):
    slots, tokens, _ = queries.shape
    vmem = pl.BlockSpec(memory_space=pltpu.VMEM)
    away = pl.BlockSpec(memory_space=pltpu.HBM)
    scores = slots * (CHUNK // HEAD_DIM) * tokens * tokens * count
    return pl.pallas_call(
        functools.partial(attention_kernel, first),
        out_shape=jax.ShapeDtypeStruct((slots * tokens, CHUNK * count), jnp.bfloat16),
        in_specs=[vmem] + [away] * 3 + [pl.BlockSpec(memory_space=pl.ANY)] * len(after),
        out_specs=vmem,
        scratch_shapes=[
            pltpu.VMEM((count, 3, slots, tokens, CHUNK), jnp.bfloat16),
            pltpu.SemaphoreType.DMA((count, 3)),
        ],
        compiler_params=pltpu.CompilerParams(vmem_limit_bytes=14 << 20),
        cost_estimate=pl.CostEstimate(
            flops=4 * scores * HEAD_DIM,
            bytes_accessed=8 * slots * tokens * CHUNK * count,
            transcendentals=scores,
        ),
    )(position_bias.T, queries, key_rows, values, *after)


def device_index(rep, dp, tensor, dp_size):
    return (rep * dp_size + dp) * 2 + tensor


def ring_order(dp_size):
    half = dp_size // 2
    return [2 * i for i in range(half)] + [2 * i + 1 for i in reversed(range(half))]


def ring_pairs(reps, dp_size, way):
    order = ring_order(dp_size)
    pairs = []
    for rep in range(reps):
        step = way if rep == 0 else -way
        for place in range(dp_size):
            to = order[(place + step) % dp_size]
            for tensor in range(2):
                pairs.append(
                    (
                        device_index(rep, order[place], tensor, dp_size),
                        device_index(rep, to, tensor, dp_size),
                    )
                )
    return pairs


def block_of(distance):
    dp = lax.axis_index("dp")
    place = jnp.where(dp % 2 == 0, dp // 2, 7 - dp // 2)
    way = jnp.where(lax.axis_index("rep") == 0, 1, -1)
    place = (place - way * distance + 16) % 8
    return jnp.where(place < 4, 2 * place, 2 * (7 - place) + 1)


def project_kernel(plan, n_context, n_weights, *refs):
    context = refs[:n_context]
    weights = refs[n_context : n_context + n_weights]
    bases, out_ref = refs[n_context + n_weights : -1], refs[-1]
    for slot, pieces in enumerate(plan):
        total = bases[0][slot] if bases and slot < bases[0].shape[0] else None
        for weight, row, source, column, rows in pieces:
            part = jnp.dot(
                context[source][:, column : column + rows],
                weights[weight][row : row + rows],
                preferred_element_type=jnp.float32,
            )
            total = part if total is None else total + part
        out_ref[slot] = total.astype(out_ref.dtype)


def project(context, weights, plan, kind, bases=()):
    rows = context[0].shape[0]
    depth = sum(piece[-1] for pieces in plan for piece in pieces)
    vmem = pl.BlockSpec(memory_space=pltpu.VMEM)
    return pl.pallas_call(
        functools.partial(project_kernel, plan, len(context), len(weights)),
        out_shape=jax.ShapeDtypeStruct((len(plan), rows, CHUNK), kind),
        in_specs=[vmem] * (len(context) + len(weights) + len(bases)),
        out_specs=vmem,
        compiler_params=pltpu.CompilerParams(vmem_limit_bytes=12 << 20),
        cost_estimate=pl.CostEstimate(
            flops=2 * rows * depth * CHUNK,
            bytes_accessed=2 * (len(plan) * rows * CHUNK + depth * CHUNK),
            transcendentals=0,
        ),
    )(*context, *weights, *bases)


def finish_kernel(distances, counts_ref, donors_ref, *refs):
    n = len(distances)
    kept, other = refs[:n], refs[n : 2 * n]
    out_ref, buffer, sem = refs[-3:]
    slots, tokens = out_ref.shape[:2]
    my_group, tensor = lax.axis_index("dp"), lax.axis_index("tensor")
    second = donors_ref[0] == my_group
    for at in range(1, donors_ref.shape[0]):
        second = jnp.logical_or(second, donors_ref[at] == my_group)
    live = [jnp.where(counts_ref[0] >= 1, 1.0, 0.0), jnp.where(second, 1.0, 0.0)]
    at = 0
    steps = []
    for array, group in enumerate(distances):
        for slot, distance in enumerate(group):
            block = block_of(distance)
            column = pl.multiple_of(block % 4 * CHUNK, CHUNK)
            copy = pltpu.make_async_copy(
                buffer.at[at], out_ref.at[:, :, pl.ds(column, CHUNK)], sem.at[at]
            )
            steps.append((block // 4 == tensor, copy))

            @pl.when(block // 4 == tensor)
            def _():
                for passage in range(slots):
                    rows = slice(passage * tokens, (passage + 1) * tokens)
                    both = kept[array][slot, rows].astype(jnp.float32)
                    both = both + other[array][slot, rows].astype(jnp.float32)
                    buffer[at, passage] = (both * live[passage]).astype(jnp.bfloat16)
                copy.start()

            at += 1
    for mine, copy in steps:

        @pl.when(mine)
        def _():
            copy.wait()


def finish(kept, other, distances, counts, donors, slots, held=()):
    rows = kept[0].shape[1]
    tokens = rows // slots
    smem = pl.BlockSpec(memory_space=pltpu.SMEM)
    vmem = pl.BlockSpec(memory_space=pltpu.VMEM)
    away = pl.BlockSpec(memory_space=pl.ANY)
    blocks = sum(len(group) for group in distances)
    n_in = 2 + 2 * len(kept)
    return pl.pallas_call(
        functools.partial(finish_kernel, distances),
        out_shape=jax.ShapeDtypeStruct((slots, tokens, 4 * CHUNK), jnp.bfloat16),
        in_specs=[smem, smem] + [vmem] * (n_in - 2) + [away] * len(held),
        out_specs=away,
        scratch_shapes=[
            pltpu.VMEM((blocks, slots, tokens, CHUNK), jnp.bfloat16),
            pltpu.SemaphoreType.DMA((blocks,)),
        ],
        input_output_aliases={n_in: 0} if held else {},
        compiler_params=pltpu.CompilerParams(vmem_limit_bytes=12 << 20),
        cost_estimate=pl.CostEstimate(
            flops=blocks * rows * CHUNK,
            bytes_accessed=blocks * rows * CHUNK * 3,
            transcendentals=0,
        ),
    )(counts, donors, *kept, *other, *held)


def with_ring(queries, key_rows, values, position_bias, out_weight, counts, donors, reps, dp_size):
    slots = queries.shape[0]
    ahead = ring_pairs(reps, dp_size, 1)
    back = ring_pairs(reps, dp_size, -1)
    places = [(r, d, t) for r in range(2) for d in range(dp_size) for t in range(2)]
    across = [
        (device_index(r, d, t, dp_size), device_index(1 - r, d, t, dp_size)) for r, d, t in places
    ]
    cores = [
        (device_index(r, d, t, dp_size), device_index(r, d, 1 - t, dp_size)) for r, d, t in places
    ]
    send = lambda value, pairs: lax.ppermute(value, AXES, pairs)
    depth = out_weight.shape[0]
    cut, half = depth // 4, depth // 2
    edge = lambda p, q: jnp.concatenate([p[:cut], q[-cut:]], axis=0)
    barrier = lax.optimization_barrier

    p1, q1 = send(out_weight, ahead), send(out_weight, back)
    c0 = attend(queries, key_rows, values, position_bias, 0, 3)
    p1, q1, c0 = barrier((p1, q1, c0))

    p2, q2 = send(p1[:-cut], ahead), send(q1[cut:], back)
    c1 = attend(queries, key_rows, values, position_bias, 3, 1, (c0,))
    p2, q2, c1 = barrier((p2, q2, c1))
    context = (c0, c1)

    p3, q3, y2 = send(p2, ahead), send(q2, back), send(edge(p2, q2), across)
    whole = lambda w: [(w, 0, 0, 0, 3 * cut), (w, 3 * cut, 1, 0, cut)]
    e1 = project(context, (out_weight, p1, q1), [whole(i) for i in range(3)], jnp.bfloat16)
    p3, q3, y2, e1 = barrier((p3, q3, y2, e1))

    p4, q4 = send(p3[:half], ahead), send(q3[-half:], back)
    y3 = send(edge(p3, q3), across)
    x1 = send(e1, cores)
    p_part = lambda w: [(w, 0, 0, 0, 3 * cut)]
    q_part = lambda w: [(w, 0, 0, cut, 2 * cut), (w, 2 * cut, 1, 0, cut)]
    p_rest = lambda w: [(w, cut, 1, 0, cut)]
    q_rest = lambda w: [(w, 0, 0, 0, cut)]
    e2 = project(
        context, (p2, q2, y2), [p_part(0) + p_rest(2), q_part(1) + q_rest(2)], jnp.bfloat16
    )
    started = project(context, (p3, q3), [p_part(0), q_part(1)], jnp.float32)
    p4, q4, y3, e2, x1, started = barrier((p4, q4, y3, e2, x1, started))

    x2 = send(e2, cores)
    opposite = [(1, 0, 0, 0, half), (2, 0, 0, half, cut), (2, cut, 1, 0, cut)]
    e3 = project(
        context, (y3, p4, q4), [p_rest(0), q_rest(0), opposite], jnp.bfloat16, (started,)
    )
    x3 = send(e3, cores)
    early = finish((e1, e2), (x1, x2), ((0, 1, -1), (2, -2)), counts, donors, slots)
    x3, early = barrier((x3, early))
    return finish((e3,), (x3,), ((3, -3, 4),), counts, donors, slots, (early,))


def with_gather(queries, key_rows, values, position_bias, out_weight, counts, donors):
    slots, tokens, features = queries.shape
    whole = lax.all_gather(out_weight, "dp", axis=1, tiled=True)
    context = attend(queries, key_rows, values, position_bias, 0, features // CHUNK)
    product = jnp.dot(context, whole, preferred_element_type=jnp.float32).astype(jnp.bfloat16)
    merged = lax.psum_scatter(product, "tensor", scatter_dimension=1, tiled=True)
    first_live = counts[0] >= 1
    second_live = jnp.any(donors == lax.axis_index("dp"))
    live = jnp.stack([first_live, second_live]).astype(jnp.bfloat16)
    return merged.reshape(slots, tokens, merged.shape[1]) * live[:, None, None]


def solution(mesh):
    in_specs = (
        P(("rep", "dp"), None, "tensor"),
        P(("rep", "dp"), None, "tensor"),
        P(("rep", "dp"), None, "tensor"),
        P(None, "tensor"),
        P("tensor", "dp"),
        P(("rep", "dp")),
        P("rep"),
    )
    out_specs = P(("rep", "dp"), None, "tensor")
    reps, dp_size = mesh.shape["rep"], mesh.shape["dp"]
    if reps == 2 and dp_size == 8 and mesh.shape["tensor"] == 2:
        on_device = functools.partial(with_ring, reps=reps, dp_size=dp_size)
    else:
        on_device = with_gather
    return jax.shard_map(
        on_device, mesh=mesh, in_specs=in_specs, out_specs=out_specs, check_vma=False
    )
```

time: 111 us -> 53.6 us (0.48)
  waiting for transfers between devices: 61.9 us -> 19.4 us
  matrix products: 21 us -> 0 us
  Pallas kernels: 0 us -> 15.2 us
  between operations: 14.1 us -> 0.81 us
  starting transfers between devices: 0.04 us -> 12.9 us
  local copies, waits for them, and re-layouts: 9.27 us -> 4.51 us
  other arithmetic: 3.87 us -> 0.04 us
    all_gather x1 -> x0, waiting for transfers between devices: 55.3 us -> none  [on_device(): lax.all_gather(out_weight, 'dp', axis=1, tiled=True)]
    ppermute x0 -> x13, waiting for transfers between devices: none -> 19.4 us  [with_ring(): send = lambda value, pairs: lax.ppermute(value, AXES, pairs)]
    pallas_call x0 -> x8, Pallas kernels: none -> 15.2 us  [the longest x2 10 us: attend(): pl.pallas_call(functools.partial(attention_kernel, first), out_shape=jax....]
    dot_general x3 -> x0, matrix products: 14.4 us -> none  [the longest x1 5.92 us: on_device(): jnp.dot(row_block, lax.all_gather(out_weight, 'dp', axis=1, tiled=True),...]
    ppermute x0 -> x13, starting transfers between devices: none -> 12.9 us  [with_ring(): send = lambda value, pairs: lax.ppermute(value, AXES, pairs)]
    sub x1 -> x0, matrix products: 6.59 us -> none  [attend(): expd = jnp.exp(scores - highest)]
    reduce_scatter x1 -> x0, waiting for transfers between devices: 5.93 us -> none  [on_device(): lax.psum_scatter(jnp.dot(row_block, lax.all_gather(out_weight, 'dp', axis...]
    dot_general x1 -> x0, local copies, waits for them, and re-layouts: 5.39 us -> none  [attend(): jnp.einsum('ijb,bh->hij', one_hot, position_bias, precision=lax.Precision...]
  transfers between devices with their start and end apart: 2 -> 13, of which waited for: 2 -> 11; matrix products, arithmetic and copies ran while one was open for 23% -> 0% of each run, Pallas kernels for 0% -> 26%
where the time goes in v2:
time: 53.6 us; the launch traced here: 52.9 us
  waiting for transfers between devices  19.4 us (36%)
  Pallas kernels  15.2 us (28%)
  starting transfers between devices  12.9 us (24%)
  local copies, waits for them, and re-layouts  4.51 us (8%)
  between operations  0.81 us (2%)
    ppermute x13, waiting for transfers between devices, with_ring(): send = lambda value, pairs: lax.ppermute(value, AXES, pairs)  19.4 us
    ppermute x13, starting transfers between devices, with_ring(): send = lambda value, pairs: lax.ppermute(value, AXES, pairs)  12.9 us
    pallas_call x2, Pallas kernels, attend(): pl.pallas_call(functools.partial(attention_kernel, first), out_shape=jax....  10 us
    unnamed x12, local copies, waits for them, and re-layouts  4.38 us
    pallas_call x4, Pallas kernels, project(): pl.pallas_call(functools.partial(project_kernel, plan, len(context), len(...  2.87 us
    pallas_call x2, Pallas kernels, finish(): pl.pallas_call(functools.partial(finish_kernel, distances), out_shape=jax...  2.35 us
  transfers between devices with their start and end apart: 13, of which 11 were waited for; matrix products, arithmetic and copies ran while one was open for 0% of the time, Pallas kernels for 26%

profile of v2, /device:TPU:0, one launch (start us, length us, event | category | flops | bytes accessed | tf_op | source)
XLA Modules:
  0.0 52.9 jit_solution(11052464411985091405)
XLA Ops:
  0.0 3.0 %collective-permute-start = (bf16[1024,256]{1,0:T(8,128)(2,1)}, bf16[1024,256]{1,0:T(8,128)(2,1)S(1)}, u32[]{:S(2)}, u32[]{:S(2)}) collective-permute-start(bf16[1024,256]{1,0:T(8,128)(2,1)} %refs_2_.5), channel_id=1, source_target_pairs={{0,4},{1,5},{4,8},{5,9},{8,12},{9,13},{12,14},{13,15},{14,10},{15,... | collective-permute-start | bytes 1572872 | tf_op jit(solution)/shard_map/ppermute | solution.py:267
  3.0 1.2 %copy-done = bf16[2,256,1024]{2,1,0:T(8,128)(2,1)S(1)} copy-done((bf16[2,256,1024]{2,1,0:T(8,128)(2,1)S(1)}, bf16[2,256,1024]{2,1,0:T(8,128)(2,1)}, u32[]{:S(2)}) %copy-start) | copy-done | bytes 1048600
  4.3 1.2 %copy-done.1 = bf16[2,256,1024]{2,1,0:T(8,128)(2,1)S(1)} copy-done((bf16[2,256,1024]{2,1,0:T(8,128)(2,1)S(1)}, bf16[2,256,1024]{2,1,0:T(8,128)(2,1)}, u32[]{:S(2)}) %copy-start.1) | copy-done | bytes 1048600
  5.5 1.2 %copy-done.2 = bf16[2,256,1024]{2,1,0:T(8,128)(2,1)S(1)} copy-done((bf16[2,256,1024]{2,1,0:T(8,128)(2,1)S(1)}, bf16[2,256,1024]{2,1,0:T(8,128)(2,1)}, u32[]{:S(2)}) %copy-start.2) | copy-done | bytes 1048600
  6.7 0.7 %copy-done.4 = f32[32,16]{0,1:T(8,128)S(1)} copy-done((f32[32,16]{0,1:T(8,128)S(1)}, f32[32,16]{0,1:T(8,128)}, u32[]{:S(2)}) %copy-start.4) | copy-done | bytes 2072
  7.4 7.5 %shard_map.73.refs_3_.refs_0_ = bf16[512,768]{1,0:T(8,128)(2,1)S(1)} custom-call(f32[16,32]{1,0:T(8,128)S(1)} %bitcast.1, bf16[2,256,1024]{2,1,0:T(8,128)(2,1)S(1)} %copy-done, bf16[2,256,1024]{2,1,0:T(8,128)(2,1)S(1)} %copy-done.1, bf16[2,256,1024]{2,1,0:T(8,128)(2,1)S(1)} %copy-done.2), custom_call_target="tpu_custom_call" | custom-call | flops 402653184 | bytes 3145728 | tf_op jit(solution)/shard_map/pallas_call | solution.py:105
  15.1 1.5 %collective-permute-done.1.refs_4_ = bf16[1024,256]{1,0:T(8,128)(2,1)S(1)} collective-permute-done((bf16[1024,256]{1,0:T(8,128)(2,1)}, bf16[1024,256]{1,0:T(8,128)(2,1)S(1)}, u32[]{:S(2)}, u32[]{:S(2)}) %collective-permute-start.1) | collective-permute-done | bytes 524320 | tf_op jit(solution)/shard_map/ppermute | solution.py:267
  17.1 1.7 %collective-permute-start.2 = (bf16[768,256]{1,0:T(8,128)(2,1)S(1)}, bf16[768,256]{1,0:T(8,128)(2,1)S(1)}, u32[]{:S(2)}, u32[]{:S(2)}) collective-permute-start(bf16[768,256]{1,0:T(8,128)(2,1)S(1)} %slice.24), channel_id=1, source_target_pairs={{0,4},{1,5},{4,8},{5,9},{8,12},{9,13},{12,14},{13,15},{14,10},{15,... | collective-permute-start | bytes 1179656 | tf_op jit(solution)/shard_map/ppermute | solution.py:267
  18.8 2.6 %shard_map.74.refs_1_ = bf16[512,256]{1,0:T(8,128)(2,1)S(1)} custom-call(f32[16,32]{1,0:T(8,128)S(1)} %bitcast.2, bf16[2,256,1024]{2,1,0:T(8,128)(2,1)S(1)} %copy-done, bf16[2,256,1024]{2,1,0:T(8,128)(2,1)S(1)} %copy-done.1, bf16[2,256,1024]{2,1,0:T(8,128)(2,1)S(1)} %copy-done.2, bf16[512,768]{1,0:T(8,128)(2,1)S(1)} %shard_map.73.refs_3_.refs_0_), custom_call_target="tpu_custom_call" | custom-call | flops 134217728 | bytes 1048576 | tf_op jit(solution)/shard_map/pallas_call | solution.py:105
  21.3 5.1 %collective-permute-done.3.refs_3_ = bf16[768,256]{1,0:T(8,128)(2,1)S(1)} collective-permute-done((bf16[768,256]{1,0:T(8,128)(2,1)S(1)}, bf16[768,256]{1,0:T(8,128)(2,1)S(1)}, u32[]{:S(2)}, u32[]{:S(2)}) %collective-permute-start.3) | collective-permute-done | bytes 393248 | tf_op jit(solution)/shard_map/ppermute | solution.py:267
  27.0 1.2 %collective-permute-start.4 = (bf16[768,256]{1,0:T(8,128)(2,1)S(1)}, bf16[768,256]{1,0:T(8,128)(2,1)S(1)}, u32[]{:S(2)}, u32[]{:S(2)}) collective-permute-start(bf16[768,256]{1,0:T(8,128)(2,1)S(1)} %collective-permute-done.2.refs_2_), channel_id=1, source_target_pairs={{0,4},{1,5},{4,8},{5,9},{8,12},{9,13},{12,14},{13,15},{14,10},{15,... | collective-permute-start | bytes 1179656 | tf_op jit(solution)/shard_map/ppermute | solution.py:267
  28.1 0.9 %collective-permute-start.5 = (bf16[768,256]{1,0:T(8,128)(2,1)S(1)}, bf16[768,256]{1,0:T(8,128)(2,1)S(1)}, u32[]{:S(2)}, u32[]{:S(2)}) collective-permute-start(bf16[768,256]{1,0:T(8,128)(2,1)S(1)} %collective-permute-done.3.refs_3_), channel_id=1, source_target_pairs={{0,2},{1,3},{4,0},{5,1},{8,4},{9,5},{12,8},{13,9},{14,12},{15,13},... | collective-permute-start | bytes 1179656 | tf_op jit(solution)/shard_map/ppermute | solution.py:267
  29.1 1.7 %collective-permute-start.6 = (bf16[512,256]{1,0:T(8,128)(2,1)S(1)}, bf16[512,256]{1,0:T(8,128)(2,1)S(1)}, u32[]{:S(2)}, u32[]{:S(2)}) collective-permute-start(bf16[512,256]{1,0:T(8,128)(2,1)S(1)} %pad_maximum_fusion), channel_id=1, source_target_pairs={{0,16},{1,17},{2,18},{3,19},{4,20},{5,21},{6,22},{7,23},{8,24},{9,... | collective-permute-start | bytes 786440 | tf_op jit(solution)/shard_map/ppermute | solution.py:267
  30.7 1.0 %shard_map.75.refs_0_ = bf16[3,512,256]{2,1,0:T(8,128)(2,1)S(1)} custom-call(bf16[512,768]{1,0:T(8,128)(2,1)S(1)} %shard_map.73.refs_3_.refs_0_, bf16[512,256]{1,0:T(8,128)(2,1)S(1)} %shard_map.74.refs_1_, bf16[1024,256]{1,0:T(8,128)(2,1)S(1)} %copy-done.3, bf16[1024,256]{1,0:T(8,128)(2,1)S(1)} %collective-permute-done.refs_3_, ...), custom_call_target="tpu_custom_call" | custom-call | flops 805306368 | bytes 2359296 | tf_op jit(solution)/shard_map/pallas_call | solution.py:177
  31.7 3.8 %collective-permute-done.6.refs_4_ = bf16[512,256]{1,0:T(8,128)(2,1)S(1)} collective-permute-done((bf16[512,256]{1,0:T(8,128)(2,1)S(1)}, bf16[512,256]{1,0:T(8,128)(2,1)S(1)}, u32[]{:S(2)}, u32[]{:S(2)}) %collective-permute-start.6) | collective-permute-done | bytes 262176 | tf_op jit(solution)/shard_map/ppermute | solution.py:267
  36.5 1.3 %collective-permute-start.8 = (bf16[512,256]{1,0:T(8,128)(2,1)S(1)}, bf16[512,256]{1,0:T(8,128)(2,1)S(1)}, u32[]{:S(2)}, u32[]{:S(2)}) collective-permute-start(bf16[512,256]{1,0:T(8,128)(2,1)S(1)} %slice.29), channel_id=1, source_target_pairs={{0,2},{1,3},{4,0},{5,1},{8,4},{9,5},{12,8},{13,9},{14,12},{15,13},... | collective-permute-start | bytes 786440 | tf_op jit(solution)/shard_map/ppermute | solution.py:267
  37.9 0.7 %collective-permute-start.7 = (bf16[512,256]{1,0:T(8,128)(2,1)S(1)}, bf16[512,256]{1,0:T(8,128)(2,1)S(1)}, u32[]{:S(2)}, u32[]{:S(2)}) collective-permute-start(bf16[512,256]{1,0:T(8,128)(2,1)S(1)} %slice.28), channel_id=1, source_target_pairs={{0,4},{1,5},{4,8},{5,9},{8,12},{9,13},{12,14},{13,15},{14,10},{15,... | collective-permute-start | bytes 786440 | tf_op jit(solution)/shard_map/ppermute | solution.py:267
  38.6 1.5 %collective-permute-start.9 = (bf16[512,256]{1,0:T(8,128)(2,1)S(1)}, bf16[512,256]{1,0:T(8,128)(2,1)S(1)}, u32[]{:S(2)}, u32[]{:S(2)}) collective-permute-start(bf16[512,256]{1,0:T(8,128)(2,1)S(1)} %pad_maximum_fusion.1), channel_id=1, source_target_pairs={{0,16},{1,17},{2,18},{3,19},{4,20},{5,21},{6,22},{7,23},{8,24},{9,... | collective-permute-start | bytes 786440 | tf_op jit(solution)/shard_map/ppermute | solution.py:267
  40.7 0.7 %shard_map.76.refs_1_ = bf16[2,512,256]{2,1,0:T(8,128)(2,1)S(1)} custom-call(bf16[512,768]{1,0:T(8,128)(2,1)S(1)} %shard_map.73.refs_3_.refs_0_, bf16[512,256]{1,0:T(8,128)(2,1)S(1)} %shard_map.74.refs_1_, bf16[768,256]{1,0:T(8,128)(2,1)S(1)} %collective-permute-done.2.refs_2_, bf16[768,256]{1,0:T(8,128)(2,1)S(1)} %collective-permute-done.3.refs_3_, ...), custom_call_target="tpu_custom_call" | custom-call | flops 536870912 | bytes 1572864 | tf_op jit(solution)/shard_map/pallas_call | solution.py:177
  41.4 3.9 %collective-permute-done.8.refs_4_ = bf16[512,256]{1,0:T(8,128)(2,1)S(1)} collective-permute-done((bf16[512,256]{1,0:T(8,128)(2,1)S(1)}, bf16[512,256]{1,0:T(8,128)(2,1)S(1)}, u32[]{:S(2)}, u32[]{:S(2)}) %collective-permute-start.8) | collective-permute-done | bytes 262176 | tf_op jit(solution)/shard_map/ppermute | solution.py:267
  45.3 1.0 %collective-permute-done.7.refs_3_ = bf16[512,256]{1,0:T(8,128)(2,1)S(1)} collective-permute-done((bf16[512,256]{1,0:T(8,128)(2,1)S(1)}, bf16[512,256]{1,0:T(8,128)(2,1)S(1)}, u32[]{:S(2)}, u32[]{:S(2)}) %collective-permute-start.7) | collective-permute-done | bytes 262176 | tf_op jit(solution)/shard_map/ppermute | solution.py:267
  48.7 1.9 %collective-permute-done.12.refs_3_ = bf16[2,512,256]{2,1,0:T(8,128)(2,1)S(1)} collective-permute-done((bf16[2,512,256]{2,1,0:T(8,128)(2,1)S(1)}, bf16[2,512,256]{2,1,0:T(8,128)(2,1)S(1)}, u32[]{:S(2)}, u32[]{:S(2)}) %collective-permute-start.12) | collective-permute-done | bytes 524320 | tf_op jit(solution)/shard_map/ppermute | solution.py:267
  50.6 1.7 %shard_map.79.refs_2_ = bf16[2,256,1024]{2,1,0:T(8,128)(2,1)} custom-call(s32[1]{0:T(128)S(6)} %copy.10.counts_ref, s32[4]{0:T(128)S(1)} %copy-done.5, bf16[3,512,256]{2,1,0:T(8,128)(2,1)S(1)} %shard_map.75.refs_0_, bf16[2,512,256]{2,1,0:T(8,128)(2,1)S(1)} %shard_map.76.refs_1_, bf16[3,512,256]{2,1,0:T(8,128)(2,1)S(1)} %collective-permute-done.10.refs_2_, ...), custom_call_target="tpu_custom_call" | custom-call | flops 655360 | bytes 1966080 | tf_op jit(solution)/shard_map/pallas_call | solution.py:237
  52.3 0.7 %shard_map.80 = bf16[2,256,1024]{2,1,0:T(8,128)(2,1)} custom-call(s32[1]{0:T(128)S(6)} %copy.10.counts_ref, s32[4]{0:T(128)S(1)} %copy-done.5, bf16[3,512,256]{2,1,0:T(8,128)(2,1)S(1)} %shard_map.78.refs_0_, bf16[3,512,256]{2,1,0:T(8,128)(2,1)S(1)} %collective-permute-done.11.refs_1_, ...), custom_call_target="tpu_custom_call", output_to_operand_aliasing={{}: (4, {})} | custom-call | flops 393216 | bytes 1179648 | tf_op jit(solution)/shard_map/pallas_call | solution.py:237
  (32 shorter events, 4.6 us)
Async XLA Ops:
  0.0 15.1 %collective-permute-start = (bf16[1024,256]{1,0:T(8,128)(2,1)}, bf16[1024,256]{1,0:T(8,128)(2,1)S(1)}, u32[]{:S(2)}, u32[]{:S(2)}) collective-permute-start(bf16[1024,256]{1,0:T(8,128)(2,1)} %refs_2_.5), channel_id=1, source_target_pairs={{0,4},{1,5},{4,8},{5,9},{8,12},{9,13},{12,14},{13,15},{14,10},{15,... | collective-permute-start | bytes 1572872 | tf_op jit(solution)/shard_map/ppermute | solution.py:267
  3.0 13.6 %collective-permute-start.1 = (bf16[1024,256]{1,0:T(8,128)(2,1)}, bf16[1024,256]{1,0:T(8,128)(2,1)S(1)}, u32[]{:S(2)}, u32[]{:S(2)}) collective-permute-start(bf16[1024,256]{1,0:T(8,128)(2,1)} %refs_2_.5), channel_id=1, source_target_pairs={{0,2},{1,3},{4,0},{5,1},{8,4},{9,5},{12,8},{13,9},{14,12},{15,13},... | collective-permute-start | bytes 1572872 | tf_op jit(solution)/shard_map/ppermute | solution.py:267
  3.0 1.2 %copy-start = (bf16[2,256,1024]{2,1,0:T(8,128)(2,1)S(1)}, bf16[2,256,1024]{2,1,0:T(8,128)(2,1)}, u32[]{:S(2)}) copy-start(bf16[2,256,1024]{2,1,0:T(8,128)(2,1)} %refs_0_.3) | copy-start | bytes 3145732
  4.3 1.2 %copy-start.1 = (bf16[2,256,1024]{2,1,0:T(8,128)(2,1)S(1)}, bf16[2,256,1024]{2,1,0:T(8,128)(2,1)}, u32[]{:S(2)}) copy-start(bf16[2,256,1024]{2,1,0:T(8,128)(2,1)} %refs_1_.3) | copy-start | bytes 3145732
  5.5 1.2 %copy-start.2 = (bf16[2,256,1024]{2,1,0:T(8,128)(2,1)S(1)}, bf16[2,256,1024]{2,1,0:T(8,128)(2,1)}, u32[]{:S(2)}) copy-start(bf16[2,256,1024]{2,1,0:T(8,128)(2,1)} %refs_2_.4) | copy-start | bytes 3145732
  6.7 0.7 %copy-start.4 = (f32[32,16]{0,1:T(8,128)S(1)}, f32[32,16]{0,1:T(8,128)}, u32[]{:S(2)}) copy-start(f32[32,16]{0,1:T(8,128)} %param.10) | copy-start | bytes 6148
  16.7 9.7 %collective-permute-start.3 = (bf16[768,256]{1,0:T(8,128)(2,1)S(1)}, bf16[768,256]{1,0:T(8,128)(2,1)S(1)}, u32[]{:S(2)}, u32[]{:S(2)}) collective-permute-start(bf16[768,256]{1,0:T(8,128)(2,1)S(1)} %slice.25), channel_id=1, source_target_pairs={{0,2},{1,3},{4,0},{5,1},{8,4},{9,5},{12,8},{13,9},{14,12},{15,13},... | collective-permute-start | bytes 1179656 | tf_op jit(solution)/shard_map/ppermute | solution.py:267
  17.1 9.9 %collective-permute-start.2 = (bf16[768,256]{1,0:T(8,128)(2,1)S(1)}, bf16[768,256]{1,0:T(8,128)(2,1)S(1)}, u32[]{:S(2)}, u32[]{:S(2)}) collective-permute-start(bf16[768,256]{1,0:T(8,128)(2,1)S(1)} %slice.24), channel_id=1, source_target_pairs={{0,4},{1,5},{4,8},{5,9},{8,12},{9,13},{12,14},{13,15},{14,10},{15,... | collective-permute-start | bytes 1179656 | tf_op jit(solution)/shard_map/ppermute | solution.py:267
  21.3 9.4 %copy-start.3 = (bf16[1024,256]{1,0:T(8,128)(2,1)S(1)}, bf16[1024,256]{1,0:T(8,128)(2,1)}, u32[]{:S(2)}) copy-start(bf16[1024,256]{1,0:T(8,128)(2,1)} %refs_2_.5) | copy-start | bytes 1572868
  27.0 9.0 %collective-permute-start.4 = (bf16[768,256]{1,0:T(8,128)(2,1)S(1)}, bf16[768,256]{1,0:T(8,128)(2,1)S(1)}, u32[]{:S(2)}, u32[]{:S(2)}) collective-permute-start(bf16[768,256]{1,0:T(8,128)(2,1)S(1)} %collective-permute-done.2.refs_2_), channel_id=1, source_target_pairs={{0,4},{1,5},{4,8},{5,9},{8,12},{9,13},{12,14},{13,15},{14,10},{15,... | collective-permute-start | bytes 1179656 | tf_op jit(solution)/shard_map/ppermute | solution.py:267
  28.1 8.3 %collective-permute-start.5 = (bf16[768,256]{1,0:T(8,128)(2,1)S(1)}, bf16[768,256]{1,0:T(8,128)(2,1)S(1)}, u32[]{:S(2)}, u32[]{:S(2)}) collective-permute-start(bf16[768,256]{1,0:T(8,128)(2,1)S(1)} %collective-permute-done.3.refs_3_), channel_id=1, source_target_pairs={{0,2},{1,3},{4,0},{5,1},{8,4},{9,5},{12,8},{13,9},{14,12},{15,13},... | collective-permute-start | bytes 1179656 | tf_op jit(solution)/shard_map/ppermute | solution.py:267
  29.1 6.4 %collective-permute-start.6 = (bf16[512,256]{1,0:T(8,128)(2,1)S(1)}, bf16[512,256]{1,0:T(8,128)(2,1)S(1)}, u32[]{:S(2)}, u32[]{:S(2)}) collective-permute-start(bf16[512,256]{1,0:T(8,128)(2,1)S(1)} %pad_maximum_fusion), channel_id=1, source_target_pairs={{0,16},{1,17},{2,18},{3,19},{4,20},{5,21},{6,22},{7,23},{8,24},{9,... | collective-permute-start | bytes 786440 | tf_op jit(solution)/shard_map/ppermute | solution.py:267
  36.4 10.4 %collective-permute-start.10 = (bf16[3,512,256]{2,1,0:T(8,128)(2,1)S(1)}, bf16[3,512,256]{2,1,0:T(8,128)(2,1)S(1)}, u32[]{:S(2)}, u32[]{:S(2)}) collective-permute-start(bf16[3,512,256]{2,1,0:T(8,128)(2,1)S(1)} %shard_map.75.refs_0_), channel_id=1, source_target_pairs={{0,1},{1,0},{2,3},{3,2},{4,5},{5,4},{6,7},{7,6},{8,9},{9,8},{10,11... | collective-permute-start | bytes 2359304 | tf_op jit(solution)/shard_map/ppermute | solution.py:267
  36.5 8.8 %collective-permute-start.8 = (bf16[512,256]{1,0:T(8,128)(2,1)S(1)}, bf16[512,256]{1,0:T(8,128)(2,1)S(1)}, u32[]{:S(2)}, u32[]{:S(2)}) collective-permute-start(bf16[512,256]{1,0:T(8,128)(2,1)S(1)} %slice.29), channel_id=1, source_target_pairs={{0,2},{1,3},{4,0},{5,1},{8,4},{9,5},{12,8},{13,9},{14,12},{15,13},... | collective-permute-start | bytes 786440 | tf_op jit(solution)/shard_map/ppermute | solution.py:267
  37.9 8.4 %collective-permute-start.7 = (bf16[512,256]{1,0:T(8,128)(2,1)S(1)}, bf16[512,256]{1,0:T(8,128)(2,1)S(1)}, u32[]{:S(2)}, u32[]{:S(2)}) collective-permute-start(bf16[512,256]{1,0:T(8,128)(2,1)S(1)} %slice.28), channel_id=1, source_target_pairs={{0,4},{1,5},{4,8},{5,9},{8,12},{9,13},{12,14},{13,15},{14,10},{15,... | collective-permute-start | bytes 786440 | tf_op jit(solution)/shard_map/ppermute | solution.py:267
  38.6 8.2 %collective-permute-start.9 = (bf16[512,256]{1,0:T(8,128)(2,1)S(1)}, bf16[512,256]{1,0:T(8,128)(2,1)S(1)}, u32[]{:S(2)}, u32[]{:S(2)}) collective-permute-start(bf16[512,256]{1,0:T(8,128)(2,1)S(1)} %pad_maximum_fusion.1), channel_id=1, source_target_pairs={{0,16},{1,17},{2,18},{3,19},{4,20},{5,21},{6,22},{7,23},{8,24},{9,... | collective-permute-start | bytes 786440 | tf_op jit(solution)/shard_map/ppermute | solution.py:267
  47.5 3.1 %copy-start.5 = (s32[4]{0:T(128)S(1)}, s32[4]{0:T(128)}, u32[]{:S(2)}) copy-start(s32[4]{0:T(128)} %donors_ref.3) | copy-start | bytes 52
  47.5 4.8 %collective-permute-start.11 = (bf16[3,512,256]{2,1,0:T(8,128)(2,1)S(1)}, bf16[3,512,256]{2,1,0:T(8,128)(2,1)S(1)}, u32[]{:S(2)}, u32[]{:S(2)}) collective-permute-start(bf16[3,512,256]{2,1,0:T(8,128)(2,1)S(1)} %shard_map.78.refs_0_), channel_id=1, source_target_pairs={{0,1},{1,0},{2,3},{3,2},{4,5},{5,4},{6,7},{7,6},{8,9},{9,8},{10,11... | collective-permute-start | bytes 2359304 | tf_op jit(solution)/shard_map/ppermute | solution.py:267
  47.6 3.0 %collective-permute-start.12 = (bf16[2,512,256]{2,1,0:T(8,128)(2,1)S(1)}, bf16[2,512,256]{2,1,0:T(8,128)(2,1)S(1)}, u32[]{:S(2)}, u32[]{:S(2)}) collective-permute-start(bf16[2,512,256]{2,1,0:T(8,128)(2,1)S(1)} %shard_map.76.refs_1_), channel_id=1, source_target_pairs={{0,1},{1,0},{2,3},{3,2},{4,5},{5,4},{6,7},{7,6},{8,9},{9,8},{10,11... | collective-permute-start | bytes 1572872 | tf_op jit(solution)/shard_map/ppermute | solution.py:267

commit v3 on v2

--- a/solution.py
+++ b/solution.py
@@ -266,46 +266,48 @@
     ]
     send = lambda value, pairs: lax.ppermute(value, AXES, pairs)
     depth = out_weight.shape[0]
-    cut, half = depth // 4, depth // 2
+    cut, half = 3 * depth // 8, depth // 2
+    over = half - cut
     edge = lambda p, q: jnp.concatenate([p[:cut], q[-cut:]], axis=0)
     barrier = lax.optimization_barrier
 
-    p1, q1 = send(out_weight, ahead), send(out_weight, back)
-    c0 = attend(queries, key_rows, values, position_bias, 0, 3)
+    upper, lower = out_weight[:-cut], out_weight[cut:]
+    p1, q1 = send(upper, ahead), send(lower, back)
+    c0 = attend(queries, key_rows, values, position_bias, 0, 2)
     p1, q1, c0 = barrier((p1, q1, c0))
 
-    p2, q2 = send(p1[:-cut], ahead), send(q1[cut:], back)
-    c1 = attend(queries, key_rows, values, position_bias, 3, 1, (c0,))
-    p2, q2, c1 = barrier((p2, q2, c1))
+    y1 = send(edge(p1, q1), across)
+    p2, q2 = send(p1, ahead), send(q1, back)
+    c1 = attend(queries, key_rows, values, position_bias, 2, 2, (c0,))
+    p2, q2, y1, c1 = barrier((p2, q2, y1, c1))
     context = (c0, c1)
-
-    p3, q3, y2 = send(p2, ahead), send(q2, back), send(edge(p2, q2), across)
-    whole = lambda w: [(w, 0, 0, 0, 3 * cut), (w, 3 * cut, 1, 0, cut)]
-    e1 = project(context, (out_weight, p1, q1), [whole(i) for i in range(3)], jnp.bfloat16)
+    p_part = lambda w: [(w, 0, 0, 0, half), (w, half, 1, 0, over)]
+    q_part = lambda w: [(w, 0, 0, cut, over), (w, over, 1, 0, half)]
+    p_rest = lambda w: [(w, cut, 1, over, cut)]
+    q_rest = lambda w: [(w, 0, 0, 0, cut)]
+    pair = lambda p, q, y: [p_part(p) + p_rest(y), q_part(q) + q_rest(y)]
+    own = [(0, 0, 0, 0, half), (0, half, 1, 0, half)]
+
+    y2 = send(edge(p2, q2), across)
+    p3, q3 = send(p2, ahead), send(q2, back)
+    e1 = project(context, (out_weight, p1, q1, y1), [own] + pair(1, 2, 3), jnp.bfloat16)
     p3, q3, y2, e1 = barrier((p3, q3, y2, e1))
 
+    y3 = send(edge(p3, q3), across)
     p4, q4 = send(p3[:half], ahead), send(q3[-half:], back)
-    y3 = send(edge(p3, q3), across)
-    x1 = send(e1, cores)
-    p_part = lambda w: [(w, 0, 0, 0, 3 * cut)]
-    q_part = lambda w: [(w, 0, 0, cut, 2 * cut), (w, 2 * cut, 1, 0, cut)]
-    p_rest = lambda w: [(w, cut, 1, 0, cut)]
-    q_rest = lambda w: [(w, 0, 0, 0, cut)]
-    e2 = project(
-        context, (p2, q2, y2), [p_part(0) + p_rest(2), q_part(1) + q_rest(2)], jnp.bfloat16
-    )
+    e2 = project(context, (p2, q2, y2), pair(0, 1, 2), jnp.bfloat16)
     started = project(context, (p3, q3), [p_part(0), q_part(1)], jnp.float32)
-    p4, q4, y3, e2, x1, started = barrier((p4, q4, y3, e2, x1, started))
-
-    x2 = send(e2, cores)
-    opposite = [(1, 0, 0, 0, half), (2, 0, 0, half, cut), (2, cut, 1, 0, cut)]
+    p4, q4, y3, e1, e2, started = barrier((p4, q4, y3, e1, e2, started))
+
+    x1, x2 = send(e1, cores), send(e2, cores)
+    opposite = [(1, 0, 0, 0, half), (2, 0, 1, 0, half)]
     e3 = project(
         context, (y3, p4, q4), [p_rest(0), q_rest(0), opposite], jnp.bfloat16, (started,)
     )
     x3 = send(e3, cores)
-    early = finish((e1, e2), (x1, x2), ((0, 1, -1), (2, -2)), counts, donors, slots)
-    x3, early = barrier((x3, early))
-    return finish((e3,), (x3,), ((3, -3, 4),), counts, donors, slots, (early,))
+    early = finish((e1,), (x1,), ((0, 1, -1),), counts, donors, slots)
+    x2, x3, early = barrier((x2, x3, early))
+    return finish((e2, e3), (x2, x3), ((2, -2), (3, -3, 4)), counts, donors, slots, (early,))
 
 
 def with_gather(queries, key_rows, values, position_bias, out_weight, counts, donors):

time: 53.6 us -> 48.6 us (0.907)
  waiting for transfers between devices: 19.4 us -> 15.3 us
  Pallas kernels: 15.2 us -> 16.2 us
  local copies, waits for them, and re-layouts: 4.51 us -> 3.8 us
  starting transfers between devices: 12.9 us -> 12.2 us
    ppermute x13 -> x14, waiting for transfers between devices: 19.4 us -> 15.3 us  [with_ring(): send = lambda value, pairs: lax.ppermute(value, AXES, pairs)]
    unnamed x12, local copies, waits for them, and re-layouts: 4.38 us -> 2.47 us
    slice x2 -> x1, local copies, waits for them, and re-layouts: 0.05 us -> 1.2 us  [with_ring(): upper, lower = (out_weight[:-cut], out_weight[cut:])]
    ppermute x13 -> x14, starting transfers between devices: 12.9 us -> 12.2 us  [with_ring(): send = lambda value, pairs: lax.ppermute(value, AXES, pairs)]
    pallas_call x2, Pallas kernels: 2.35 us -> 2.98 us  [finish(): pl.pallas_call(functools.partial(finish_kernel, distances), out_shape=jax...]
  transfers between devices with their start and end apart: 13 -> 14, of which waited for: 11 -> 10; matrix products, arithmetic and copies ran while one was open for 0% -> 0% of each run, Pallas kernels for 26% -> 31%
where the time goes in v3:
time: 48.6 us; the launch traced here: 48.4 us
  Pallas kernels  16.2 us (33%)
  waiting for transfers between devices  15.3 us (31%)
  starting transfers between devices  12.2 us (25%)
  local copies, waits for them, and re-layouts  3.8 us (8%)
  between operations  0.83 us (2%)
    ppermute x14, waiting for transfers between devices, with_ring(): send = lambda value, pairs: lax.ppermute(value, AXES, pairs)  15.3 us
    ppermute x14, starting transfers between devices, with_ring(): send = lambda value, pairs: lax.ppermute(value, AXES, pairs)  12.2 us
    pallas_call x2, Pallas kernels, attend(): pl.pallas_call(functools.partial(attention_kernel, first), out_shape=jax....  10 us
    pallas_call x4, Pallas kernels, project(): pl.pallas_call(functools.partial(project_kernel, plan, len(context), len(...  3.2 us
    pallas_call x2, Pallas kernels, finish(): pl.pallas_call(functools.partial(finish_kernel, distances), out_shape=jax...  2.98 us
    unnamed x12, local copies, waits for them, and re-layouts  2.47 us
    slice x1, local copies, waits for them, and re-layouts, with_ring(): upper, lower = (out_weight[:-cut], out_weight[cut:])  1.2 us
  transfers between devices with their start and end apart: 14, of which 10 were waited for; matrix products, arithmetic and copies ran while one was open for 0% of the time, Pallas kernels for 31%

profile of v3, /device:TPU:0, one launch (start us, length us, event | category | flops | bytes accessed | tf_op | source)
XLA Modules:
  0.0 48.4 jit_solution(5332068967872818101)
XLA Ops:
  0.0 1.2 %fusion = (bf16[640,256]{1,0:T(8,128)(2,1)S(1)}, bf16[640,256]{1,0:T(8,128)(2,1)S(1)}) fusion(bf16[1024,256]{1,0:T(8,128)(2,1)} %refs_2_.5), kind=kLoop, calls=%fused_computation.3 | loop fusion | bytes 1310720 | tf_op jit(solution)/shard_map/slice | solution.py:274
  1.2 3.0 %collective-permute-start.1 = (bf16[640,256]{1,0:T(8,128)(2,1)S(1)}, bf16[640,256]{1,0:T(8,128)(2,1)S(1)}, u32[]{:S(2)}, u32[]{:S(2)}) collective-permute-start(bf16[640,256]{1,0:T(8,128)(2,1)S(1)} %get-tuple-element.45), channel_id=1, source_target_pairs={{0,2},{1,3},{4,0},{5,1},{8,4},{9,5},{12,8},{13,9},{14,12},{15,13},... | collective-permute-start | bytes 983048 | tf_op jit(solution)/shard_map/ppermute | solution.py:267
  4.4 1.2 %copy-done.1 = bf16[2,256,1024]{2,1,0:T(8,128)(2,1)S(1)} copy-done((bf16[2,256,1024]{2,1,0:T(8,128)(2,1)S(1)}, bf16[2,256,1024]{2,1,0:T(8,128)(2,1)}, u32[]{:S(2)}) %copy-start.1) | copy-done | bytes 1048600
  5.6 1.2 %copy-done.2 = bf16[2,256,1024]{2,1,0:T(8,128)(2,1)S(1)} copy-done((bf16[2,256,1024]{2,1,0:T(8,128)(2,1)S(1)}, bf16[2,256,1024]{2,1,0:T(8,128)(2,1)}, u32[]{:S(2)}) %copy-start.2) | copy-done | bytes 1048600
  6.8 5.0 %shard_map.73.refs_3_.refs_0_ = bf16[512,512]{1,0:T(8,128)(2,1)S(1)} custom-call(f32[16,32]{1,0:T(8,128)S(1)} %bitcast.1, bf16[2,256,1024]{2,1,0:T(8,128)(2,1)S(1)} %copy-done, bf16[2,256,1024]{2,1,0:T(8,128)(2,1)S(1)} %copy-done.1, bf16[2,256,1024]{2,1,0:T(8,128)(2,1)S(1)} %copy-done.2), custom_call_target="tpu_custom_call" | custom-call | flops 268435456 | bytes 2097152 | tf_op jit(solution)/shard_map/pallas_call | solution.py:105
  12.0 1.4 %collective-permute-done.refs_3_ = bf16[640,256]{1,0:T(8,128)(2,1)S(1)} collective-permute-done((bf16[640,256]{1,0:T(8,128)(2,1)S(1)}, bf16[640,256]{1,0:T(8,128)(2,1)S(1)}, u32[]{:S(2)}, u32[]{:S(2)}) %collective-permute-start) | collective-permute-done | bytes 327712 | tf_op jit(solution)/shard_map/ppermute | solution.py:267
  13.4 1.7 %collective-permute-start.4 = (bf16[768,256]{1,0:T(8,128)(2,1)S(1)}, bf16[768,256]{1,0:T(8,128)(2,1)S(1)}, u32[]{:S(2)}, u32[]{:S(2)}) collective-permute-start(bf16[768,256]{1,0:T(8,128)(2,1)S(1)} %pad_maximum_fusion), channel_id=1, source_target_pairs={{0,16},{1,17},{2,18},{3,19},{4,20},{5,21},{6,22},{7,23},{8,24},{9,... | collective-permute-start | bytes 1179656 | tf_op jit(solution)/shard_map/ppermute | solution.py:267
  15.1 1.6 %collective-permute-start.2 = (bf16[640,256]{1,0:T(8,128)(2,1)S(1)}, bf16[640,256]{1,0:T(8,128)(2,1)S(1)}, u32[]{:S(2)}, u32[]{:S(2)}) collective-permute-start(bf16[640,256]{1,0:T(8,128)(2,1)S(1)} %collective-permute-done.refs_3_), channel_id=1, source_target_pairs={{0,4},{1,5},{4,8},{5,9},{8,12},{9,13},{12,14},{13,15},{14,10},{15,... | collective-permute-start | bytes 983048 | tf_op jit(solution)/shard_map/ppermute | solution.py:267
  17.1 5.0 %shard_map.74.refs_1_ = bf16[512,512]{1,0:T(8,128)(2,1)S(1)} custom-call(f32[16,32]{1,0:T(8,128)S(1)} %bitcast.2, bf16[2,256,1024]{2,1,0:T(8,128)(2,1)S(1)} %copy-done, bf16[2,256,1024]{2,1,0:T(8,128)(2,1)S(1)} %copy-done.1, bf16[2,256,1024]{2,1,0:T(8,128)(2,1)S(1)} %copy-done.2, bf16[512,512]{1,0:T(8,128)(2,1)S(1)} %shard_map.73.refs_3_.refs_0_), custom_call_target="tpu_custom_call" | custom-call | flops 268435456 | bytes 2097152 | tf_op jit(solution)/shard_map/pallas_call | solution.py:105
  22.2 0.9 %collective-permute-done.2.refs_2_ = bf16[640,256]{1,0:T(8,128)(2,1)S(1)} collective-permute-done((bf16[640,256]{1,0:T(8,128)(2,1)S(1)}, bf16[640,256]{1,0:T(8,128)(2,1)S(1)}, u32[]{:S(2)}, u32[]{:S(2)}) %collective-permute-start.2) | collective-permute-done | bytes 327712 | tf_op jit(solution)/shard_map/ppermute | solution.py:267
  23.1 1.3 %collective-permute-done.3.refs_3_ = bf16[640,256]{1,0:T(8,128)(2,1)S(1)} collective-permute-done((bf16[640,256]{1,0:T(8,128)(2,1)S(1)}, bf16[640,256]{1,0:T(8,128)(2,1)S(1)}, u32[]{:S(2)}, u32[]{:S(2)}) %collective-permute-start.3) | collective-permute-done | bytes 327712 | tf_op jit(solution)/shard_map/ppermute | solution.py:267
  25.0 1.5 %collective-permute-start.5 = (bf16[640,256]{1,0:T(8,128)(2,1)S(1)}, bf16[640,256]{1,0:T(8,128)(2,1)S(1)}, u32[]{:S(2)}, u32[]{:S(2)}) collective-permute-start(bf16[640,256]{1,0:T(8,128)(2,1)S(1)} %collective-permute-done.2.refs_2_), channel_id=1, source_target_pairs={{0,4},{1,5},{4,8},{5,9},{8,12},{9,13},{12,14},{13,15},{14,10},{15,... | collective-permute-start | bytes 983048 | tf_op jit(solution)/shard_map/ppermute | solution.py:267
  27.0 1.1 %shard_map.75.refs_0_ = bf16[3,512,256]{2,1,0:T(8,128)(2,1)S(1)} custom-call(bf16[512,512]{1,0:T(8,128)(2,1)S(1)} %shard_map.73.refs_3_.refs_0_, bf16[512,512]{1,0:T(8,128)(2,1)S(1)} %shard_map.74.refs_1_, bf16[1024,256]{1,0:T(8,128)(2,1)S(1)} %copy-done.3, bf16[640,256]{1,0:T(8,128)(2,1)S(1)} %collective-permute-done.refs_3_, ...), custom_call_target="tpu_custom_call" | custom-call | flops 805306368 | bytes 2359296 | tf_op jit(solution)/shard_map/pallas_call | solution.py:177
  28.1 3.9 %collective-permute-done.5.refs_2_ = bf16[640,256]{1,0:T(8,128)(2,1)S(1)} collective-permute-done((bf16[640,256]{1,0:T(8,128)(2,1)S(1)}, bf16[640,256]{1,0:T(8,128)(2,1)S(1)}, u32[]{:S(2)}, u32[]{:S(2)}) %collective-permute-start.5) | collective-permute-done | bytes 327712 | tf_op jit(solution)/shard_map/ppermute | solution.py:267
  32.1 2.1 %collective-permute-done.6.refs_3_ = bf16[640,256]{1,0:T(8,128)(2,1)S(1)} collective-permute-done((bf16[640,256]{1,0:T(8,128)(2,1)S(1)}, bf16[640,256]{1,0:T(8,128)(2,1)S(1)}, u32[]{:S(2)}, u32[]{:S(2)}) %collective-permute-start.6) | collective-permute-done | bytes 327712 | tf_op jit(solution)/shard_map/ppermute | solution.py:267
  34.3 2.1 %collective-permute-start.9 = (bf16[512,256]{1,0:T(8,128)(2,1)S(1)}, bf16[512,256]{1,0:T(8,128)(2,1)S(1)}, u32[]{:S(2)}, u32[]{:S(2)}) collective-permute-start(bf16[512,256]{1,0:T(8,128)(2,1)S(1)} %slice.37), channel_id=1, source_target_pairs={{0,2},{1,3},{4,0},{5,1},{8,4},{9,5},{12,8},{13,9},{14,12},{15,13},... | collective-permute-start | bytes 786440 | tf_op jit(solution)/shard_map/ppermute | solution.py:267
  36.4 0.6 %shard_map.77.refs_5_ = f32[2,512,256]{2,1,0:T(8,128)S(1)} custom-call(bf16[512,512]{1,0:T(8,128)(2,1)S(1)} %shard_map.73.refs_3_.refs_0_, bf16[512,512]{1,0:T(8,128)(2,1)S(1)} %shard_map.74.refs_1_, bf16[640,256]{1,0:T(8,128)(2,1)S(1)} %collective-permute-done.5.refs_2_, bf16[640,256]{1,0:T(8,128)(2,1)S(1)} %collective-permute-done.6.refs_3_), custom_call_target="tpu_custom_call" | custom-call | flops 335544320 | bytes 1179648 | tf_op jit(solution)/shard_map/pallas_call | solution.py:177
  37.0 0.8 %shard_map.76.refs_0_ = bf16[2,512,256]{2,1,0:T(8,128)(2,1)S(1)} custom-call(bf16[512,512]{1,0:T(8,128)(2,1)S(1)} %shard_map.73.refs_3_.refs_0_, bf16[512,512]{1,0:T(8,128)(2,1)S(1)} %shard_map.74.refs_1_, bf16[640,256]{1,0:T(8,128)(2,1)S(1)} %collective-permute-done.2.refs_2_, bf16[640,256]{1,0:T(8,128)(2,1)S(1)} %collective-permute-done.3.refs_3_, ...), custom_call_target="tpu_custom_call" | custom-call | flops 536870912 | bytes 1572864 | tf_op jit(solution)/shard_map/pallas_call | solution.py:177
  37.8 2.9 %collective-permute-done.9.refs_4_ = bf16[512,256]{1,0:T(8,128)(2,1)S(1)} collective-permute-done((bf16[512,256]{1,0:T(8,128)(2,1)S(1)}, bf16[512,256]{1,0:T(8,128)(2,1)S(1)}, u32[]{:S(2)}, u32[]{:S(2)}) %collective-permute-start.9) | collective-permute-done | bytes 262176 | tf_op jit(solution)/shard_map/ppermute | solution.py:267
  40.7 2.0 %collective-permute-done.8.refs_3_ = bf16[512,256]{1,0:T(8,128)(2,1)S(1)} collective-permute-done((bf16[512,256]{1,0:T(8,128)(2,1)S(1)}, bf16[512,256]{1,0:T(8,128)(2,1)S(1)}, u32[]{:S(2)}, u32[]{:S(2)}) %collective-permute-start.8) | collective-permute-done | bytes 262176 | tf_op jit(solution)/shard_map/ppermute | solution.py:267
  42.8 0.7 %shard_map.78.refs_1_ = bf16[3,512,256]{2,1,0:T(8,128)(2,1)S(1)} custom-call(bf16[512,512]{1,0:T(8,128)(2,1)S(1)} %shard_map.73.refs_3_.refs_0_, bf16[512,512]{1,0:T(8,128)(2,1)S(1)} %shard_map.74.refs_1_, bf16[768,256]{1,0:T(8,128)(2,1)S(1)} %collective-permute-done.10.refs_2_, bf16[512,256]{1,0:T(8,128)(2,1)S(1)} %collective-permute-done.8.refs_3_, ...), custom_call_target="tpu_custom_call" | custom-call | flops 469762048 | bytes 1703936 | tf_op jit(solution)/shard_map/pallas_call | solution.py:177
  43.5 0.6 %collective-permute-start.12 = (bf16[3,512,256]{2,1,0:T(8,128)(2,1)S(1)}, bf16[3,512,256]{2,1,0:T(8,128)(2,1)S(1)}, u32[]{:S(2)}, u32[]{:S(2)}) collective-permute-start(bf16[3,512,256]{2,1,0:T(8,128)(2,1)S(1)} %shard_map.78.refs_1_), channel_id=1, source_target_pairs={{0,1},{1,0},{2,3},{3,2},{4,5},{5,4},{6,7},{7,6},{8,9},{9,8},{10,11... | collective-permute-start | bytes 2359304 | tf_op jit(solution)/shard_map/ppermute | solution.py:267
  45.1 1.6 %shard_map.79.refs_4_ = bf16[2,256,1024]{2,1,0:T(8,128)(2,1)} custom-call(s32[1]{0:T(128)S(6)} %copy.10.counts_ref, s32[4]{0:T(128)S(1)} %copy-done.5, bf16[3,512,256]{2,1,0:T(8,128)(2,1)S(1)} %shard_map.75.refs_0_, bf16[3,512,256]{2,1,0:T(8,128)(2,1)S(1)} %collective-permute-done.13.refs_1_), custom_call_target="tpu_custom_call" | custom-call | flops 393216 | bytes 1179648 | tf_op jit(solution)/shard_map/pallas_call | solution.py:237
  47.0 1.4 %shard_map.80 = bf16[2,256,1024]{2,1,0:T(8,128)(2,1)} custom-call(s32[1]{0:T(128)S(6)} %copy.10.counts_ref, s32[4]{0:T(128)S(1)} %copy-done.5, bf16[2,512,256]{2,1,0:T(8,128)(2,1)S(1)} %shard_map.76.refs_0_, bf16[3,512,256]{2,1,0:T(8,128)(2,1)S(1)} %shard_map.78.refs_1_, ...), custom_call_target="tpu_custom_call", output_to_operand_aliasing={{}: (6, {})} | custom-call | flops 655360 | bytes 1966080 | tf_op jit(solution)/shard_map/pallas_call | solution.py:237
  (36 shorter events, 2.7 us)
Async XLA Ops:
  0.0 4.4 %copy-start = (bf16[2,256,1024]{2,1,0:T(8,128)(2,1)S(1)}, bf16[2,256,1024]{2,1,0:T(8,128)(2,1)}, u32[]{:S(2)}) copy-start(bf16[2,256,1024]{2,1,0:T(8,128)(2,1)} %refs_0_.3) | copy-start | bytes 3145732
  0.0 4.4 %copy-start.4 = (f32[32,16]{0,1:T(8,128)S(1)}, f32[32,16]{0,1:T(8,128)}, u32[]{:S(2)}) copy-start(f32[32,16]{0,1:T(8,128)} %param.10) | copy-start | bytes 6148
  1.2 10.8 %collective-permute-start.1 = (bf16[640,256]{1,0:T(8,128)(2,1)S(1)}, bf16[640,256]{1,0:T(8,128)(2,1)S(1)}, u32[]{:S(2)}, u32[]{:S(2)}) collective-permute-start(bf16[640,256]{1,0:T(8,128)(2,1)S(1)} %get-tuple-element.45), channel_id=1, source_target_pairs={{0,2},{1,3},{4,0},{5,1},{8,4},{9,5},{12,8},{13,9},{14,12},{15,13},... | collective-permute-start | bytes 983048 | tf_op jit(solution)/shard_map/ppermute | solution.py:267
  4.2 9.2 %collective-permute-start = (bf16[640,256]{1,0:T(8,128)(2,1)S(1)}, bf16[640,256]{1,0:T(8,128)(2,1)S(1)}, u32[]{:S(2)}, u32[]{:S(2)}) collective-permute-start(bf16[640,256]{1,0:T(8,128)(2,1)S(1)} %get-tuple-element.46), channel_id=1, source_target_pairs={{0,4},{1,5},{4,8},{5,9},{8,12},{9,13},{12,14},{13,15},{14,10},{15,... | collective-permute-start | bytes 983048 | tf_op jit(solution)/shard_map/ppermute | solution.py:267
  4.4 1.2 %copy-start.1 = (bf16[2,256,1024]{2,1,0:T(8,128)(2,1)S(1)}, bf16[2,256,1024]{2,1,0:T(8,128)(2,1)}, u32[]{:S(2)}) copy-start(bf16[2,256,1024]{2,1,0:T(8,128)(2,1)} %refs_1_.3) | copy-start | bytes 3145732
  5.6 1.2 %copy-start.2 = (bf16[2,256,1024]{2,1,0:T(8,128)(2,1)S(1)}, bf16[2,256,1024]{2,1,0:T(8,128)(2,1)}, u32[]{:S(2)}) copy-start(bf16[2,256,1024]{2,1,0:T(8,128)(2,1)} %refs_2_.4) | copy-start | bytes 3145732
  13.4 11.0 %collective-permute-start.4 = (bf16[768,256]{1,0:T(8,128)(2,1)S(1)}, bf16[768,256]{1,0:T(8,128)(2,1)S(1)}, u32[]{:S(2)}, u32[]{:S(2)}) collective-permute-start(bf16[768,256]{1,0:T(8,128)(2,1)S(1)} %pad_maximum_fusion), channel_id=1, source_target_pairs={{0,16},{1,17},{2,18},{3,19},{4,20},{5,21},{6,22},{7,23},{8,24},{9,... | collective-permute-start | bytes 1179656 | tf_op jit(solution)/shard_map/ppermute | solution.py:267
  15.1 8.0 %collective-permute-start.2 = (bf16[640,256]{1,0:T(8,128)(2,1)S(1)}, bf16[640,256]{1,0:T(8,128)(2,1)S(1)}, u32[]{:S(2)}, u32[]{:S(2)}) collective-permute-start(bf16[640,256]{1,0:T(8,128)(2,1)S(1)} %collective-permute-done.refs_3_), channel_id=1, source_target_pairs={{0,4},{1,5},{4,8},{5,9},{8,12},{9,13},{12,14},{13,15},{14,10},{15,... | collective-permute-start | bytes 983048 | tf_op jit(solution)/shard_map/ppermute | solution.py:267
  16.7 7.7 %collective-permute-start.3 = (bf16[640,256]{1,0:T(8,128)(2,1)S(1)}, bf16[640,256]{1,0:T(8,128)(2,1)S(1)}, u32[]{:S(2)}, u32[]{:S(2)}) collective-permute-start(bf16[640,256]{1,0:T(8,128)(2,1)S(1)} %collective-permute-done.1.refs_4_), channel_id=1, source_target_pairs={{0,2},{1,3},{4,0},{5,1},{8,4},{9,5},{12,8},{13,9},{14,12},{15,13},... | collective-permute-start | bytes 983048 | tf_op jit(solution)/shard_map/ppermute | solution.py:267
  24.4 2.6 %copy-start.3 = (bf16[1024,256]{1,0:T(8,128)(2,1)S(1)}, bf16[1024,256]{1,0:T(8,128)(2,1)}, u32[]{:S(2)}) copy-start(bf16[1024,256]{1,0:T(8,128)(2,1)} %refs_2_.5) | copy-start | bytes 1572868
  24.5 9.6 %collective-permute-start.7 = (bf16[768,256]{1,0:T(8,128)(2,1)S(1)}, bf16[768,256]{1,0:T(8,128)(2,1)S(1)}, u32[]{:S(2)}, u32[]{:S(2)}) collective-permute-start(bf16[768,256]{1,0:T(8,128)(2,1)S(1)} %pad_maximum_fusion.1), channel_id=1, source_target_pairs={{0,16},{1,17},{2,18},{3,19},{4,20},{5,21},{6,22},{7,23},{8,24},{9,... | collective-permute-start | bytes 1179656 | tf_op jit(solution)/shard_map/ppermute | solution.py:267
  25.0 7.1 %collective-permute-start.5 = (bf16[640,256]{1,0:T(8,128)(2,1)S(1)}, bf16[640,256]{1,0:T(8,128)(2,1)S(1)}, u32[]{:S(2)}, u32[]{:S(2)}) collective-permute-start(bf16[640,256]{1,0:T(8,128)(2,1)S(1)} %collective-permute-done.2.refs_2_), channel_id=1, source_target_pairs={{0,4},{1,5},{4,8},{5,9},{8,12},{9,13},{12,14},{13,15},{14,10},{15,... | collective-permute-start | bytes 983048 | tf_op jit(solution)/shard_map/ppermute | solution.py:267
  26.5 7.6 %collective-permute-start.6 = (bf16[640,256]{1,0:T(8,128)(2,1)S(1)}, bf16[640,256]{1,0:T(8,128)(2,1)S(1)}, u32[]{:S(2)}, u32[]{:S(2)}) collective-permute-start(bf16[640,256]{1,0:T(8,128)(2,1)S(1)} %collective-permute-done.3.refs_3_), channel_id=1, source_target_pairs={{0,2},{1,3},{4,0},{5,1},{8,4},{9,5},{12,8},{13,9},{14,12},{15,13},... | collective-permute-start | bytes 983048 | tf_op jit(solution)/shard_map/ppermute | solution.py:267
  34.2 8.6 %collective-permute-start.10 = (bf16[768,256]{1,0:T(8,128)(2,1)S(1)}, bf16[768,256]{1,0:T(8,128)(2,1)S(1)}, u32[]{:S(2)}, u32[]{:S(2)}) collective-permute-start(bf16[768,256]{1,0:T(8,128)(2,1)S(1)} %pad_maximum_fusion.2), channel_id=1, source_target_pairs={{0,16},{1,17},{2,18},{3,19},{4,20},{5,21},{6,22},{7,23},{8,24},{9,... | collective-permute-start | bytes 1179656 | tf_op jit(solution)/shard_map/ppermute | solution.py:267
  34.3 6.4 %collective-permute-start.9 = (bf16[512,256]{1,0:T(8,128)(2,1)S(1)}, bf16[512,256]{1,0:T(8,128)(2,1)S(1)}, u32[]{:S(2)}, u32[]{:S(2)}) collective-permute-start(bf16[512,256]{1,0:T(8,128)(2,1)S(1)} %slice.37), channel_id=1, source_target_pairs={{0,2},{1,3},{4,0},{5,1},{8,4},{9,5},{12,8},{13,9},{14,12},{15,13},... | collective-permute-start | bytes 786440 | tf_op jit(solution)/shard_map/ppermute | solution.py:267
  36.4 6.4 %collective-permute-start.8 = (bf16[512,256]{1,0:T(8,128)(2,1)S(1)}, bf16[512,256]{1,0:T(8,128)(2,1)S(1)}, u32[]{:S(2)}, u32[]{:S(2)}) collective-permute-start(bf16[512,256]{1,0:T(8,128)(2,1)S(1)} %slice.36), channel_id=1, source_target_pairs={{0,4},{1,5},{4,8},{5,9},{8,12},{9,13},{12,14},{13,15},{14,10},{15,... | collective-permute-start | bytes 786440 | tf_op jit(solution)/shard_map/ppermute | solution.py:267
  42.8 2.3 %collective-permute-start.13 = (bf16[3,512,256]{2,1,0:T(8,128)(2,1)S(1)}, bf16[3,512,256]{2,1,0:T(8,128)(2,1)S(1)}, u32[]{:S(2)}, u32[]{:S(2)}) collective-permute-start(bf16[3,512,256]{2,1,0:T(8,128)(2,1)S(1)} %shard_map.75.refs_0_), channel_id=1, source_target_pairs={{0,1},{1,0},{2,3},{3,2},{4,5},{5,4},{6,7},{7,6},{8,9},{9,8},{10,11... | collective-permute-start | bytes 2359304 | tf_op jit(solution)/shard_map/ppermute | solution.py:267
  43.5 1.6 %copy-start.5 = (s32[4]{0:T(128)S(1)}, s32[4]{0:T(128)}, u32[]{:S(2)}) copy-start(s32[4]{0:T(128)} %donors_ref.3) | copy-start | bytes 52
  43.5 3.4 %collective-permute-start.12 = (bf16[3,512,256]{2,1,0:T(8,128)(2,1)S(1)}, bf16[3,512,256]{2,1,0:T(8,128)(2,1)S(1)}, u32[]{:S(2)}, u32[]{:S(2)}) collective-permute-start(bf16[3,512,256]{2,1,0:T(8,128)(2,1)S(1)} %shard_map.78.refs_1_), channel_id=1, source_target_pairs={{0,1},{1,0},{2,3},{3,2},{4,5},{5,4},{6,7},{7,6},{8,9},{9,8},{10,11... | collective-permute-start | bytes 2359304 | tf_op jit(solution)/shard_map/ppermute | solution.py:267
  44.1 2.9 %collective-permute-start.11 = (bf16[2,512,256]{2,1,0:T(8,128)(2,1)S(1)}, bf16[2,512,256]{2,1,0:T(8,128)(2,1)S(1)}, u32[]{:S(2)}, u32[]{:S(2)}) collective-permute-start(bf16[2,512,256]{2,1,0:T(8,128)(2,1)S(1)} %shard_map.76.refs_0_), channel_id=1, source_target_pairs={{0,1},{1,0},{2,3},{3,2},{4,5},{5,4},{6,7},{7,6},{8,9},{9,8},{10,11... | collective-permute-start | bytes 1572872 | tf_op jit(solution)/shard_map/ppermute | solution.py:267

commit v4 on v3

--- a/solution.py
+++ b/solution.py
@@ -158,12 +158,14 @@
     context = refs[:n_context]
     weights = refs[n_context : n_context + n_weights]
     bases, out_ref = refs[n_context + n_weights : -1], refs[-1]
-    for slot, pieces in enumerate(plan):
+    for slot, products in enumerate(plan):
         total = bases[0][slot] if bases and slot < bases[0].shape[0] else None
-        for weight, row, source, column, rows in pieces:
+        for source, column, pieces in products:
+            parts = [weights[weight][row : row + rows] for weight, row, rows in pieces]
+            rows = parts[0] if len(parts) == 1 else jnp.concatenate(parts, axis=0)
             part = jnp.dot(
-                context[source][:, column : column + rows],
-                weights[weight][row : row + rows],
+                context[source][:, column : column + rows.shape[0]],
+                rows,
                 preferred_element_type=jnp.float32,
             )
             total = part if total is None else total + part
@@ -172,7 +174,7 @@
 
 def project(context, weights, plan, kind, bases=()):
     rows = context[0].shape[0]
-    depth = sum(piece[-1] for pieces in plan for piece in pieces)
+    depth = sum(piece[-1] for block in plan for product in block for piece in product[-1])
     vmem = pl.BlockSpec(memory_space=pltpu.VMEM)
     return pl.pallas_call(
         functools.partial(project_kernel, plan, len(context), len(weights)),
@@ -197,7 +199,9 @@
     second = donors_ref[0] == my_group
     for at in range(1, donors_ref.shape[0]):
         second = jnp.logical_or(second, donors_ref[at] == my_group)
-    live = [jnp.where(counts_ref[0] >= 1, 1.0, 0.0), jnp.where(second, 1.0, 0.0)]
+    live = [
+        jnp.where(lives, 1.0, 0.0).astype(jnp.bfloat16) for lives in (counts_ref[0] >= 1, second)
+    ]
     at = 0
     steps = []
     for array, group in enumerate(distances):
@@ -213,9 +217,8 @@
             def _():
                 for passage in range(slots):
                     rows = slice(passage * tokens, (passage + 1) * tokens)
-                    both = kept[array][slot, rows].astype(jnp.float32)
-                    both = both + other[array][slot, rows].astype(jnp.float32)
-                    buffer[at, passage] = (both * live[passage]).astype(jnp.bfloat16)
+                    both = kept[array][slot, rows] + other[array][slot, rows]
+                    buffer[at, passage] = both * live[passage]
                 copy.start()
 
             at += 1
@@ -266,43 +269,46 @@
     ]
     send = lambda value, pairs: lax.ppermute(value, AXES, pairs)
     depth = out_weight.shape[0]
-    cut, half = 3 * depth // 8, depth // 2
+    half, cut = depth // 2, 11 * depth // 32
     over = half - cut
+    lead = over // 128 * 128
+    spill = over - lead
     edge = lambda p, q: jnp.concatenate([p[:cut], q[-cut:]], axis=0)
     barrier = lax.optimization_barrier
 
-    upper, lower = out_weight[:-cut], out_weight[cut:]
-    p1, q1 = send(upper, ahead), send(lower, back)
+    p1, q1 = send(out_weight[:-cut], ahead), send(out_weight[cut:], back)
     c0 = attend(queries, key_rows, values, position_bias, 0, 2)
-    p1, q1, c0 = barrier((p1, q1, c0))
-
-    y1 = send(edge(p1, q1), across)
-    p2, q2 = send(p1, ahead), send(q1, back)
+    p1, c0 = barrier((p1, c0))
+
+    p2, q2, y1 = send(p1, ahead), send(q1, back), send(edge(p1, q1), across)
     c1 = attend(queries, key_rows, values, position_bias, 2, 2, (c0,))
-    p2, q2, y1, c1 = barrier((p2, q2, y1, c1))
+    p2, c1 = barrier((p2, c1))
     context = (c0, c1)
-    p_part = lambda w: [(w, 0, 0, 0, half), (w, half, 1, 0, over)]
-    q_part = lambda w: [(w, 0, 0, cut, over), (w, over, 1, 0, half)]
-    p_rest = lambda w: [(w, cut, 1, over, cut)]
-    q_rest = lambda w: [(w, 0, 0, 0, cut)]
-    pair = lambda p, q, y: [p_part(p) + p_rest(y), q_part(q) + q_rest(y)]
-    own = [(0, 0, 0, 0, half), (0, half, 1, 0, half)]
-
-    y2 = send(edge(p2, q2), across)
-    p3, q3 = send(p2, ahead), send(q2, back)
-    e1 = project(context, (out_weight, p1, q1, y1), [own] + pair(1, 2, 3), jnp.bfloat16)
-    p3, q3, y2, e1 = barrier((p3, q3, y2, e1))
-
+
+    p3, q3, y2 = send(p2, ahead), send(q2, back), send(edge(p2, q2), across)
+    p3, q3, y1 = barrier((p3, q3, y1))
+
+    own = [(0, 0, [(0, 0, half)]), (1, 0, [(0, half, half)])]
+    p_block = lambda p, y: [(0, 0, [(p, 0, half)]), (1, 0, [(p, half, over), (y, cut, cut)])]
+    q_block = lambda q, y: [(0, 0, [(y, 0, cut), (q, 0, over)]), (1, 0, [(q, over, half)])]
+    p_part = [(0, 0, [(0, 0, half)]), (1, 0, [(0, half, lead)])]
+    q_part = [(0, half - lead, [(1, spill, lead)]), (1, 0, [(1, over, half)])]
+    p_rest = [(1, lead, [(0, half + lead, spill), (2, cut, cut)])]
+    q_rest = [(0, 0, [(2, 0, cut), (1, 0, spill)])]
+    opposite = [(0, 0, [(3, 0, half)]), (1, 0, [(4, 0, half)])]
+
+    p4, q4 = send(p3[:half], ahead), send(q3[-half:], back)
     y3 = send(edge(p3, q3), across)
-    p4, q4 = send(p3[:half], ahead), send(q3[-half:], back)
-    e2 = project(context, (p2, q2, y2), pair(0, 1, 2), jnp.bfloat16)
-    started = project(context, (p3, q3), [p_part(0), q_part(1)], jnp.float32)
+    e1 = project(
+        context, (out_weight, p1, q1, y1), [own, p_block(1, 3), q_block(2, 3)], jnp.bfloat16
+    )
+    e2 = project(context, (p2, q2, y2), [p_block(0, 2), q_block(1, 2)], jnp.bfloat16)
+    started = project(context, (p3, q3), [p_part, q_part], jnp.float32)
     p4, q4, y3, e1, e2, started = barrier((p4, q4, y3, e1, e2, started))
 
     x1, x2 = send(e1, cores), send(e2, cores)
-    opposite = [(1, 0, 0, 0, half), (2, 0, 1, 0, half)]
     e3 = project(
-        context, (y3, p4, q4), [p_rest(0), q_rest(0), opposite], jnp.bfloat16, (started,)
+        context, (p3, q3, y3, p4, q4), [p_rest, q_rest, opposite], jnp.bfloat16, (started,)
     )
     x3 = send(e3, cores)
     early = finish((e1,), (x1,), ((0, 1, -1),), counts, donors, slots)

time: 48.6 us -> 46.2 us (0.951)
  waiting for transfers between devices: 15.3 us -> 10.8 us
  starting transfers between devices: 12.2 us -> 14.6 us
    ppermute x14, waiting for transfers between devices: 15.3 us -> 10.8 us  [with_ring(): send = lambda value, pairs: lax.ppermute(value, AXES, pairs)]
    ppermute x14, starting transfers between devices: 12.2 us -> 14.6 us  [with_ring(): send = lambda value, pairs: lax.ppermute(value, AXES, pairs)]
  transfers between devices with their start and end apart: 14 -> 14, of which waited for: 10 -> 9; matrix products, arithmetic and copies ran while one was open for 0% -> 0% of each run, Pallas kernels for 31% -> 31%
where the time goes in v4:
time: 46.2 us; the launch traced here: 46 us
  Pallas kernels  15.8 us (34%)
  starting transfers between devices  14.6 us (32%)
  waiting for transfers between devices  10.8 us (23%)
  local copies, waits for them, and re-layouts  3.8 us (8%)
  between operations  0.84 us (2%)
    ppermute x14, starting transfers between devices, with_ring(): send = lambda value, pairs: lax.ppermute(value, AXES, pairs)  14.6 us
    ppermute x14, waiting for transfers between devices, with_ring(): send = lambda value, pairs: lax.ppermute(value, AXES, pairs)  10.8 us
    pallas_call x2, Pallas kernels, attend(): pl.pallas_call(functools.partial(attention_kernel, first), out_shape=jax....  10 us
    pallas_call x4, Pallas kernels, project(): pl.pallas_call(functools.partial(project_kernel, plan, len(context), len(...  2.95 us
    pallas_call x2, Pallas kernels, finish(): pl.pallas_call(functools.partial(finish_kernel, distances), out_shape=jax...  2.86 us
    unnamed x12, local copies, waits for them, and re-layouts  2.46 us
    slice x1, local copies, waits for them, and re-layouts, with_ring(): p1, q1 = (send(out_weight[:-cut], ahead), send(out_weight[cut:], back))  1.22 us
  transfers between devices with their start and end apart: 14, of which 9 were waited for; matrix products, arithmetic and copies ran while one was open for 0% of the time, Pallas kernels for 31%

profile of v4, /device:TPU:0, one launch (start us, length us, event | category | flops | bytes accessed | tf_op | source)
XLA Modules:
  0.0 46.0 jit_solution(269462178420500090)
XLA Ops:
  0.0 1.2 %fusion = (bf16[672,256]{1,0:T(8,128)(2,1)S(1)}, bf16[672,256]{1,0:T(8,128)(2,1)S(1)}) fusion(bf16[1024,256]{1,0:T(8,128)(2,1)} %refs_2_.5), kind=kLoop, calls=%fused_computation.3 | loop fusion | bytes 1376256 | tf_op jit(solution)/shard_map/slice | solution.py:279
  1.2 3.1 %collective-permute-start = (bf16[672,256]{1,0:T(8,128)(2,1)S(1)}, bf16[672,256]{1,0:T(8,128)(2,1)S(1)}, u32[]{:S(2)}, u32[]{:S(2)}) collective-permute-start(bf16[672,256]{1,0:T(8,128)(2,1)S(1)} %get-tuple-element.38), channel_id=1, source_target_pairs={{0,4},{1,5},{4,8},{5,9},{8,12},{9,13},{12,14},{13,15},{14,10},{15,... | collective-permute-start | bytes 1032200 | tf_op jit(solution)/shard_map/ppermute | solution.py:270
  4.3 1.2 %copy-done.1 = bf16[2,256,1024]{2,1,0:T(8,128)(2,1)S(1)} copy-done((bf16[2,256,1024]{2,1,0:T(8,128)(2,1)S(1)}, bf16[2,256,1024]{2,1,0:T(8,128)(2,1)}, u32[]{:S(2)}) %copy-start.1) | copy-done | bytes 1048600
  5.5 1.2 %copy-done.2 = bf16[2,256,1024]{2,1,0:T(8,128)(2,1)S(1)} copy-done((bf16[2,256,1024]{2,1,0:T(8,128)(2,1)S(1)}, bf16[2,256,1024]{2,1,0:T(8,128)(2,1)}, u32[]{:S(2)}) %copy-start.2) | copy-done | bytes 1048600
  6.8 5.0 %shard_map.73.refs_3_.refs_0_ = bf16[512,512]{1,0:T(8,128)(2,1)S(1)} custom-call(f32[16,32]{1,0:T(8,128)S(1)} %bitcast.1, bf16[2,256,1024]{2,1,0:T(8,128)(2,1)S(1)} %copy-done, bf16[2,256,1024]{2,1,0:T(8,128)(2,1)S(1)} %copy-done.1, bf16[2,256,1024]{2,1,0:T(8,128)(2,1)S(1)} %copy-done.2), custom_call_target="tpu_custom_call" | custom-call | flops 268435456 | bytes 2097152 | tf_op jit(solution)/shard_map/pallas_call | solution.py:105
  12.3 1.8 %collective-permute-start.1 = (bf16[672,256]{1,0:T(8,128)(2,1)S(1)}, bf16[672,256]{1,0:T(8,128)(2,1)S(1)}, u32[]{:S(2)}, u32[]{:S(2)}) collective-permute-start(bf16[672,256]{1,0:T(8,128)(2,1)S(1)} %collective-permute-done.refs_3_), channel_id=1, source_target_pairs={{0,4},{1,5},{4,8},{5,9},{8,12},{9,13},{12,14},{13,15},{14,10},{15,... | collective-permute-start | bytes 1032200 | tf_op jit(solution)/shard_map/ppermute | solution.py:270
  14.4 1.8 %collective-permute-start.6 = (bf16[704,256]{1,0:T(8,128)(2,1)S(1)}, bf16[704,256]{1,0:T(8,128)(2,1)S(1)}, u32[]{:S(2)}, u32[]{:S(2)}) collective-permute-start(bf16[704,256]{1,0:T(8,128)(2,1)S(1)} %pad_maximum_fusion), channel_id=1, source_target_pairs={{0,16},{1,17},{2,18},{3,19},{4,20},{5,21},{6,22},{7,23},{8,24},{9,... | collective-permute-start | bytes 1081352 | tf_op jit(solution)/shard_map/ppermute | solution.py:270
  16.2 5.0 %shard_map.74.refs_1_ = bf16[512,512]{1,0:T(8,128)(2,1)S(1)} custom-call(f32[16,32]{1,0:T(8,128)S(1)} %bitcast.2, bf16[2,256,1024]{2,1,0:T(8,128)(2,1)S(1)} %copy-done, bf16[2,256,1024]{2,1,0:T(8,128)(2,1)S(1)} %copy-done.1, bf16[2,256,1024]{2,1,0:T(8,128)(2,1)S(1)} %copy-done.2, bf16[512,512]{1,0:T(8,128)(2,1)S(1)} %shard_map.73.refs_3_.refs_0_), custom_call_target="tpu_custom_call" | custom-call | flops 268435456 | bytes 2097152 | tf_op jit(solution)/shard_map/pallas_call | solution.py:105
  21.5 1.3 %collective-permute-done.4.refs_3_ = bf16[672,256]{1,0:T(8,128)(2,1)S(1)} collective-permute-done((bf16[672,256]{1,0:T(8,128)(2,1)S(1)}, bf16[672,256]{1,0:T(8,128)(2,1)S(1)}, u32[]{:S(2)}, u32[]{:S(2)}) %collective-permute-start.4) | collective-permute-done | bytes 344096 | tf_op jit(solution)/shard_map/ppermute | solution.py:270
  23.3 1.6 %collective-permute-start.2 = (bf16[672,256]{1,0:T(8,128)(2,1)S(1)}, bf16[672,256]{1,0:T(8,128)(2,1)S(1)}, u32[]{:S(2)}, u32[]{:S(2)}) collective-permute-start(bf16[672,256]{1,0:T(8,128)(2,1)S(1)} %collective-permute-done.1.refs_2_), channel_id=1, source_target_pairs={{0,4},{1,5},{4,8},{5,9},{8,12},{9,13},{12,14},{13,15},{14,10},{15,... | collective-permute-start | bytes 1032200 | tf_op jit(solution)/shard_map/ppermute | solution.py:270
  24.9 1.5 %collective-permute-start.10 = (bf16[704,256]{1,0:T(8,128)(2,1)S(1)}, bf16[704,256]{1,0:T(8,128)(2,1)S(1)}, u32[]{:S(2)}, u32[]{:S(2)}) collective-permute-start(bf16[704,256]{1,0:T(8,128)(2,1)S(1)} %pad_maximum_fusion.2), channel_id=1, source_target_pairs={{0,16},{1,17},{2,18},{3,19},{4,20},{5,21},{6,22},{7,23},{8,24},{9,... | collective-permute-start | bytes 1081352 | tf_op jit(solution)/shard_map/ppermute | solution.py:270
  26.4 4.2 %collective-permute-done.5.refs_3_ = bf16[672,256]{1,0:T(8,128)(2,1)S(1)} collective-permute-done((bf16[672,256]{1,0:T(8,128)(2,1)S(1)}, bf16[672,256]{1,0:T(8,128)(2,1)S(1)}, u32[]{:S(2)}, u32[]{:S(2)}) %collective-permute-start.5) | collective-permute-done | bytes 344096 | tf_op jit(solution)/shard_map/ppermute | solution.py:270
  31.1 1.5 %collective-permute-start.9 = (bf16[704,256]{1,0:T(8,128)(2,1)S(1)}, bf16[704,256]{1,0:T(8,128)(2,1)S(1)}, u32[]{:S(2)}, u32[]{:S(2)}) collective-permute-start(bf16[704,256]{1,0:T(8,128)(2,1)S(1)} %pad_maximum_fusion.1), channel_id=1, source_target_pairs={{0,16},{1,17},{2,18},{3,19},{4,20},{5,21},{6,22},{7,23},{8,24},{9,... | collective-permute-start | bytes 1081352 | tf_op jit(solution)/shard_map/ppermute | solution.py:270
  32.6 1.4 %collective-permute-start.8 = (bf16[512,256]{1,0:T(8,128)(2,1)S(1)}, bf16[512,256]{1,0:T(8,128)(2,1)S(1)}, u32[]{:S(2)}, u32[]{:S(2)}) collective-permute-start(bf16[512,256]{1,0:T(8,128)(2,1)S(1)} %slice.35), channel_id=1, source_target_pairs={{0,2},{1,3},{4,0},{5,1},{8,4},{9,5},{12,8},{13,9},{14,12},{15,13},... | collective-permute-start | bytes 786440 | tf_op jit(solution)/shard_map/ppermute | solution.py:270
  34.1 0.6 %collective-permute-start.7 = (bf16[512,256]{1,0:T(8,128)(2,1)S(1)}, bf16[512,256]{1,0:T(8,128)(2,1)S(1)}, u32[]{:S(2)}, u32[]{:S(2)}) collective-permute-start(bf16[512,256]{1,0:T(8,128)(2,1)S(1)} %slice.34), channel_id=1, source_target_pairs={{0,4},{1,5},{4,8},{5,9},{8,12},{9,13},{12,14},{13,15},{14,10},{15,... | collective-permute-start | bytes 786440 | tf_op jit(solution)/shard_map/ppermute | solution.py:270
  34.7 0.6 %shard_map.77.refs_7_ = f32[2,512,256]{2,1,0:T(8,128)S(1)} custom-call(bf16[512,512]{1,0:T(8,128)(2,1)S(1)} %shard_map.73.refs_3_.refs_0_, bf16[512,512]{1,0:T(8,128)(2,1)S(1)} %shard_map.74.refs_1_, bf16[672,256]{1,0:T(8,128)(2,1)S(1)} %collective-permute-done.2.refs_2_, bf16[672,256]{1,0:T(8,128)(2,1)S(1)} %collective-permute-done.5.refs_3_), custom_call_target="tpu_custom_call" | custom-call | flops 335544320 | bytes 1179648 | tf_op jit(solution)/shard_map/pallas_call | solution.py:179
  35.3 1.0 %shard_map.75.refs_0_ = bf16[3,512,256]{2,1,0:T(8,128)(2,1)S(1)} custom-call(bf16[512,512]{1,0:T(8,128)(2,1)S(1)} %shard_map.73.refs_3_.refs_0_, bf16[512,512]{1,0:T(8,128)(2,1)S(1)} %shard_map.74.refs_1_, bf16[1024,256]{1,0:T(8,128)(2,1)S(1)} %copy-done.3, bf16[672,256]{1,0:T(8,128)(2,1)S(1)} %collective-permute-done.refs_3_, ...), custom_call_target="tpu_custom_call" | custom-call | flops 805306368 | bytes 2359296 | tf_op jit(solution)/shard_map/pallas_call | solution.py:179
  36.3 0.7 %shard_map.76.refs_0_ = bf16[2,512,256]{2,1,0:T(8,128)(2,1)S(1)} custom-call(bf16[512,512]{1,0:T(8,128)(2,1)S(1)} %shard_map.73.refs_3_.refs_0_, bf16[512,512]{1,0:T(8,128)(2,1)S(1)} %shard_map.74.refs_1_, bf16[672,256]{1,0:T(8,128)(2,1)S(1)} %collective-permute-done.1.refs_2_, bf16[672,256]{1,0:T(8,128)(2,1)S(1)} %collective-permute-done.4.refs_3_, ...), custom_call_target="tpu_custom_call" | custom-call | flops 536870912 | bytes 1572864 | tf_op jit(solution)/shard_map/pallas_call | solution.py:179
  37.0 2.1 %collective-permute-done.8.refs_6_ = bf16[512,256]{1,0:T(8,128)(2,1)S(1)} collective-permute-done((bf16[512,256]{1,0:T(8,128)(2,1)S(1)}, bf16[512,256]{1,0:T(8,128)(2,1)S(1)}, u32[]{:S(2)}, u32[]{:S(2)}) %collective-permute-start.8) | collective-permute-done | bytes 262176 | tf_op jit(solution)/shard_map/ppermute | solution.py:270
  39.1 1.4 %collective-permute-done.7.refs_5_ = bf16[512,256]{1,0:T(8,128)(2,1)S(1)} collective-permute-done((bf16[512,256]{1,0:T(8,128)(2,1)S(1)}, bf16[512,256]{1,0:T(8,128)(2,1)S(1)}, u32[]{:S(2)}, u32[]{:S(2)}) %collective-permute-start.7) | collective-permute-done | bytes 262176 | tf_op jit(solution)/shard_map/ppermute | solution.py:270
  40.5 0.7 %shard_map.78.refs_1_ = bf16[3,512,256]{2,1,0:T(8,128)(2,1)S(1)} custom-call(bf16[512,512]{1,0:T(8,128)(2,1)S(1)} %shard_map.73.refs_3_.refs_0_, bf16[512,512]{1,0:T(8,128)(2,1)S(1)} %shard_map.74.refs_1_, bf16[672,256]{1,0:T(8,128)(2,1)S(1)} %collective-permute-done.2.refs_2_, bf16[672,256]{1,0:T(8,128)(2,1)S(1)} %collective-permute-done.5.refs_3_, ...), custom_call_target="tpu_custom_call" | custom-call | flops 469762048 | bytes 1703936 | tf_op jit(solution)/shard_map/pallas_call | solution.py:179
  41.2 0.6 %collective-permute-start.12 = (bf16[3,512,256]{2,1,0:T(8,128)(2,1)S(1)}, bf16[3,512,256]{2,1,0:T(8,128)(2,1)S(1)}, u32[]{:S(2)}, u32[]{:S(2)}) collective-permute-start(bf16[3,512,256]{2,1,0:T(8,128)(2,1)S(1)} %shard_map.78.refs_1_), channel_id=1, source_target_pairs={{0,1},{1,0},{2,3},{3,2},{4,5},{5,4},{6,7},{7,6},{8,9},{9,8},{10,11... | collective-permute-start | bytes 2359304 | tf_op jit(solution)/shard_map/ppermute | solution.py:270
  42.7 1.5 %shard_map.79.refs_4_ = bf16[2,256,1024]{2,1,0:T(8,128)(2,1)} custom-call(s32[1]{0:T(128)S(6)} %copy.10.counts_ref, s32[4]{0:T(128)S(1)} %copy-done.5, bf16[3,512,256]{2,1,0:T(8,128)(2,1)S(1)} %shard_map.75.refs_0_, bf16[3,512,256]{2,1,0:T(8,128)(2,1)S(1)} %collective-permute-done.13.refs_1_), custom_call_target="tpu_custom_call" | custom-call | flops 393216 | bytes 1179648 | tf_op jit(solution)/shard_map/pallas_call | solution.py:240
  44.6 1.4 %shard_map.80 = bf16[2,256,1024]{2,1,0:T(8,128)(2,1)} custom-call(s32[1]{0:T(128)S(6)} %copy.10.counts_ref, s32[4]{0:T(128)S(1)} %copy-done.5, bf16[2,512,256]{2,1,0:T(8,128)(2,1)S(1)} %shard_map.76.refs_0_, bf16[3,512,256]{2,1,0:T(8,128)(2,1)S(1)} %shard_map.78.refs_1_, ...), custom_call_target="tpu_custom_call", output_to_operand_aliasing={{}: (6, {})} | custom-call | flops 655360 | bytes 1966080 | tf_op jit(solution)/shard_map/pallas_call | solution.py:240
  (36 shorter events, 2.8 us)
Async XLA Ops:
  0.0 4.3 %copy-start = (bf16[2,256,1024]{2,1,0:T(8,128)(2,1)S(1)}, bf16[2,256,1024]{2,1,0:T(8,128)(2,1)}, u32[]{:S(2)}) copy-start(bf16[2,256,1024]{2,1,0:T(8,128)(2,1)} %refs_0_.3) | copy-start | bytes 3145732
  0.0 4.3 %copy-start.4 = (f32[32,16]{0,1:T(8,128)S(1)}, f32[32,16]{0,1:T(8,128)}, u32[]{:S(2)}) copy-start(f32[32,16]{0,1:T(8,128)} %param.10) | copy-start | bytes 6148
  1.2 11.1 %collective-permute-start = (bf16[672,256]{1,0:T(8,128)(2,1)S(1)}, bf16[672,256]{1,0:T(8,128)(2,1)S(1)}, u32[]{:S(2)}, u32[]{:S(2)}) collective-permute-start(bf16[672,256]{1,0:T(8,128)(2,1)S(1)} %get-tuple-element.38), channel_id=1, source_target_pairs={{0,4},{1,5},{4,8},{5,9},{8,12},{9,13},{12,14},{13,15},{14,10},{15,... | collective-permute-start | bytes 1032200 | tf_op jit(solution)/shard_map/ppermute | solution.py:270
  4.3 9.8 %collective-permute-start.3 = (bf16[672,256]{1,0:T(8,128)(2,1)S(1)}, bf16[672,256]{1,0:T(8,128)(2,1)S(1)}, u32[]{:S(2)}, u32[]{:S(2)}) collective-permute-start(bf16[672,256]{1,0:T(8,128)(2,1)S(1)} %get-tuple-element.37), channel_id=1, source_target_pairs={{0,2},{1,3},{4,0},{5,1},{8,4},{9,5},{12,8},{13,9},{14,12},{15,13},... | collective-permute-start | bytes 1032200 | tf_op jit(solution)/shard_map/ppermute | solution.py:270
  4.3 1.2 %copy-start.1 = (bf16[2,256,1024]{2,1,0:T(8,128)(2,1)S(1)}, bf16[2,256,1024]{2,1,0:T(8,128)(2,1)}, u32[]{:S(2)}) copy-start(bf16[2,256,1024]{2,1,0:T(8,128)(2,1)} %refs_1_.3) | copy-start | bytes 3145732
  5.5 1.2 %copy-start.2 = (bf16[2,256,1024]{2,1,0:T(8,128)(2,1)S(1)}, bf16[2,256,1024]{2,1,0:T(8,128)(2,1)}, u32[]{:S(2)}) copy-start(bf16[2,256,1024]{2,1,0:T(8,128)(2,1)} %refs_2_.4) | copy-start | bytes 3145732
  12.3 9.2 %collective-permute-start.1 = (bf16[672,256]{1,0:T(8,128)(2,1)S(1)}, bf16[672,256]{1,0:T(8,128)(2,1)S(1)}, u32[]{:S(2)}, u32[]{:S(2)}) collective-permute-start(bf16[672,256]{1,0:T(8,128)(2,1)S(1)} %collective-permute-done.refs_3_), channel_id=1, source_target_pairs={{0,4},{1,5},{4,8},{5,9},{8,12},{9,13},{12,14},{13,15},{14,10},{15,... | collective-permute-start | bytes 1032200 | tf_op jit(solution)/shard_map/ppermute | solution.py:270
  14.1 8.7 %collective-permute-start.4 = (bf16[672,256]{1,0:T(8,128)(2,1)S(1)}, bf16[672,256]{1,0:T(8,128)(2,1)S(1)}, u32[]{:S(2)}, u32[]{:S(2)}) collective-permute-start(bf16[672,256]{1,0:T(8,128)(2,1)S(1)} %collective-permute-done.3.refs_4_), channel_id=1, source_target_pairs={{0,2},{1,3},{4,0},{5,1},{8,4},{9,5},{12,8},{13,9},{14,12},{15,13},... | collective-permute-start | bytes 1032200 | tf_op jit(solution)/shard_map/ppermute | solution.py:270
  14.4 12.1 %collective-permute-start.6 = (bf16[704,256]{1,0:T(8,128)(2,1)S(1)}, bf16[704,256]{1,0:T(8,128)(2,1)S(1)}, u32[]{:S(2)}, u32[]{:S(2)}) collective-permute-start(bf16[704,256]{1,0:T(8,128)(2,1)S(1)} %pad_maximum_fusion), channel_id=1, source_target_pairs={{0,16},{1,17},{2,18},{3,19},{4,20},{5,21},{6,22},{7,23},{8,24},{9,... | collective-permute-start | bytes 1081352 | tf_op jit(solution)/shard_map/ppermute | solution.py:270
  22.8 7.8 %collective-permute-start.5 = (bf16[672,256]{1,0:T(8,128)(2,1)S(1)}, bf16[672,256]{1,0:T(8,128)(2,1)S(1)}, u32[]{:S(2)}, u32[]{:S(2)}) collective-permute-start(bf16[672,256]{1,0:T(8,128)(2,1)S(1)} %collective-permute-done.4.refs_3_), channel_id=1, source_target_pairs={{0,2},{1,3},{4,0},{5,1},{8,4},{9,5},{12,8},{13,9},{14,12},{15,13},... | collective-permute-start | bytes 1032200 | tf_op jit(solution)/shard_map/ppermute | solution.py:270
  23.3 7.8 %collective-permute-start.2 = (bf16[672,256]{1,0:T(8,128)(2,1)S(1)}, bf16[672,256]{1,0:T(8,128)(2,1)S(1)}, u32[]{:S(2)}, u32[]{:S(2)}) collective-permute-start(bf16[672,256]{1,0:T(8,128)(2,1)S(1)} %collective-permute-done.1.refs_2_), channel_id=1, source_target_pairs={{0,4},{1,5},{4,8},{5,9},{8,12},{9,13},{12,14},{13,15},{14,10},{15,... | collective-permute-start | bytes 1032200 | tf_op jit(solution)/shard_map/ppermute | solution.py:270
  24.9 11.3 %collective-permute-start.10 = (bf16[704,256]{1,0:T(8,128)(2,1)S(1)}, bf16[704,256]{1,0:T(8,128)(2,1)S(1)}, u32[]{:S(2)}, u32[]{:S(2)}) collective-permute-start(bf16[704,256]{1,0:T(8,128)(2,1)S(1)} %pad_maximum_fusion.2), channel_id=1, source_target_pairs={{0,16},{1,17},{2,18},{3,19},{4,20},{5,21},{6,22},{7,23},{8,24},{9,... | collective-permute-start | bytes 1081352 | tf_op jit(solution)/shard_map/ppermute | solution.py:270
  31.1 9.3 %collective-permute-start.9 = (bf16[704,256]{1,0:T(8,128)(2,1)S(1)}, bf16[704,256]{1,0:T(8,128)(2,1)S(1)}, u32[]{:S(2)}, u32[]{:S(2)}) collective-permute-start(bf16[704,256]{1,0:T(8,128)(2,1)S(1)} %pad_maximum_fusion.1), channel_id=1, source_target_pairs={{0,16},{1,17},{2,18},{3,19},{4,20},{5,21},{6,22},{7,23},{8,24},{9,... | collective-permute-start | bytes 1081352 | tf_op jit(solution)/shard_map/ppermute | solution.py:270
  32.6 2.7 %copy-start.3 = (bf16[1024,256]{1,0:T(8,128)(2,1)S(1)}, bf16[1024,256]{1,0:T(8,128)(2,1)}, u32[]{:S(2)}) copy-start(bf16[1024,256]{1,0:T(8,128)(2,1)} %refs_2_.5) | copy-start | bytes 1572868
  32.6 6.4 %collective-permute-start.8 = (bf16[512,256]{1,0:T(8,128)(2,1)S(1)}, bf16[512,256]{1,0:T(8,128)(2,1)S(1)}, u32[]{:S(2)}, u32[]{:S(2)}) collective-permute-start(bf16[512,256]{1,0:T(8,128)(2,1)S(1)} %slice.35), channel_id=1, source_target_pairs={{0,2},{1,3},{4,0},{5,1},{8,4},{9,5},{12,8},{13,9},{14,12},{15,13},... | collective-permute-start | bytes 786440 | tf_op jit(solution)/shard_map/ppermute | solution.py:270
  34.1 6.4 %collective-permute-start.7 = (bf16[512,256]{1,0:T(8,128)(2,1)S(1)}, bf16[512,256]{1,0:T(8,128)(2,1)S(1)}, u32[]{:S(2)}, u32[]{:S(2)}) collective-permute-start(bf16[512,256]{1,0:T(8,128)(2,1)S(1)} %slice.34), channel_id=1, source_target_pairs={{0,4},{1,5},{4,8},{5,9},{8,12},{9,13},{12,14},{13,15},{14,10},{15,... | collective-permute-start | bytes 786440 | tf_op jit(solution)/shard_map/ppermute | solution.py:270
  40.4 2.3 %collective-permute-start.13 = (bf16[3,512,256]{2,1,0:T(8,128)(2,1)S(1)}, bf16[3,512,256]{2,1,0:T(8,128)(2,1)S(1)}, u32[]{:S(2)}, u32[]{:S(2)}) collective-permute-start(bf16[3,512,256]{2,1,0:T(8,128)(2,1)S(1)} %shard_map.75.refs_0_), channel_id=1, source_target_pairs={{0,1},{1,0},{2,3},{3,2},{4,5},{5,4},{6,7},{7,6},{8,9},{9,8},{10,11... | collective-permute-start | bytes 2359304 | tf_op jit(solution)/shard_map/ppermute | solution.py:270
  41.2 1.6 %copy-start.5 = (s32[4]{0:T(128)S(1)}, s32[4]{0:T(128)}, u32[]{:S(2)}) copy-start(s32[4]{0:T(128)} %donors_ref.3) | copy-start | bytes 52
  41.2 3.4 %collective-permute-start.12 = (bf16[3,512,256]{2,1,0:T(8,128)(2,1)S(1)}, bf16[3,512,256]{2,1,0:T(8,128)(2,1)S(1)}, u32[]{:S(2)}, u32[]{:S(2)}) collective-permute-start(bf16[3,512,256]{2,1,0:T(8,128)(2,1)S(1)} %shard_map.78.refs_1_), channel_id=1, source_target_pairs={{0,1},{1,0},{2,3},{3,2},{4,5},{5,4},{6,7},{7,6},{8,9},{9,8},{10,11... | collective-permute-start | bytes 2359304 | tf_op jit(solution)/shard_map/ppermute | solution.py:270
  41.7 2.9 %collective-permute-start.11 = (bf16[2,512,256]{2,1,0:T(8,128)(2,1)S(1)}, bf16[2,512,256]{2,1,0:T(8,128)(2,1)S(1)}, u32[]{:S(2)}, u32[]{:S(2)}) collective-permute-start(bf16[2,512,256]{2,1,0:T(8,128)(2,1)S(1)} %shard_map.76.refs_0_), channel_id=1, source_target_pairs={{0,1},{1,0},{2,3},{3,2},{4,5},{5,4},{6,7},{7,6},{8,9},{9,8},{10,11... | collective-permute-start | bytes 1572872 | tf_op jit(solution)/shard_map/ppermute | solution.py:270

commit v5 on v4

--- a/solution.py
+++ b/solution.py
@@ -34,7 +34,13 @@
 
 
 def attention_kernel(first, bias_ref, *refs):
-    sources, (out_ref, held, sem) = refs[:3], refs[-3:]
+    sources, (out_ref, held, sem, counts_ref, donors_ref, live_sem) = refs[:3], refs[-6:]
+    live_copies = [
+        pltpu.make_async_copy(source, target, live_sem.at[at])
+        for at, (source, target) in enumerate(zip(refs[3:5], (counts_ref, donors_ref)))
+    ]
+    for copy in live_copies:
+        copy.start()
     count, _, slots, tokens, width = held.shape
     copies = [
         [
@@ -52,6 +58,13 @@
             copy.start()
     rows = bias_rows(bias_ref[...], tokens)
     lower = lax.broadcasted_iota(jnp.int32, (tokens, PAIR), 1) < HEAD_DIM
+    for copy in live_copies:
+        copy.wait()
+    my_group = lax.axis_index("dp")
+    second = donors_ref[0] == my_group
+    for at in range(1, donors_ref.shape[0]):
+        second = jnp.logical_or(second, donors_ref[at] == my_group)
+    live = [jnp.where(lives, 1.0, 0.0) for lives in (counts_ref[0] >= 1, second)]
     for chunk in range(count):
         for copy in copies[chunk]:
             copy.wait()
@@ -79,9 +92,9 @@
                 weighted = jnp.where(lower, sums[0], sums[1])
                 total = pltpu.roll(jnp.where(lower, sums[1], sums[0]), HEAD_DIM, 1)
                 at = slice(chunk * width + pair * PAIR, chunk * width + (pair + 1) * PAIR)
-                out_ref[slot * tokens : (slot + 1) * tokens, at] = (weighted / total).astype(
-                    jnp.bfloat16
-                )
+                out_ref[slot * tokens : (slot + 1) * tokens, at] = (
+                    weighted / total * live[slot]
+                ).astype(jnp.bfloat16)
 
 
 def toeplitz(row, tokens):
@@ -97,7 +110,7 @@
     return jnp.concatenate(groups, axis=0)
 
 
-def attend(queries, key_rows, values, position_bias, first, count, after=()):
+def attend(queries, key_rows, values, position_bias, counts, donors, first, count, after=()):
     slots, tokens, _ = queries.shape
     vmem = pl.BlockSpec(memory_space=pltpu.VMEM)
     away = pl.BlockSpec(memory_space=pltpu.HBM)
@@ -105,11 +118,14 @@
     return pl.pallas_call(
         functools.partial(attention_kernel, first),
         out_shape=jax.ShapeDtypeStruct((slots * tokens, CHUNK * count), jnp.bfloat16),
-        in_specs=[vmem] + [away] * 3 + [pl.BlockSpec(memory_space=pl.ANY)] * len(after),
+        in_specs=[vmem] + [away] * 5 + [pl.BlockSpec(memory_space=pl.ANY)] * len(after),
         out_specs=vmem,
         scratch_shapes=[
             pltpu.VMEM((count, 3, slots, tokens, CHUNK), jnp.bfloat16),
             pltpu.SemaphoreType.DMA((count, 3)),
+            pltpu.SMEM(counts.shape, counts.dtype),
+            pltpu.SMEM(donors.shape, donors.dtype),
+            pltpu.SemaphoreType.DMA((2,)),
         ],
         compiler_params=pltpu.CompilerParams(vmem_limit_bytes=14 << 20),
         cost_estimate=pl.CostEstimate(
@@ -117,7 +133,7 @@
             bytes_accessed=8 * slots * tokens * CHUNK * count,
             transcendentals=scores,
         ),
-    )(position_bias.T, queries, key_rows, values, *after)
+    )(position_bias.T, queries, key_rows, values, counts, donors, *after)
 
 
 def device_index(rep, dp, tensor, dp_size):
@@ -190,22 +206,16 @@
     )(*context, *weights, *bases)
 
 
-def finish_kernel(distances, counts_ref, donors_ref, *refs):
+def finish_kernel(distances, *refs):
     n = len(distances)
     kept, other = refs[:n], refs[n : 2 * n]
     out_ref, buffer, sem = refs[-3:]
     slots, tokens = out_ref.shape[:2]
-    my_group, tensor = lax.axis_index("dp"), lax.axis_index("tensor")
-    second = donors_ref[0] == my_group
-    for at in range(1, donors_ref.shape[0]):
-        second = jnp.logical_or(second, donors_ref[at] == my_group)
-    live = [
-        jnp.where(lives, 1.0, 0.0).astype(jnp.bfloat16) for lives in (counts_ref[0] >= 1, second)
-    ]
-    at = 0
+    tensor = lax.axis_index("tensor")
     steps = []
     for array, group in enumerate(distances):
         for slot, distance in enumerate(group):
+            at = len(steps)
             block = block_of(distance)
             column = pl.multiple_of(block % 4 * CHUNK, CHUNK)
             copy = pltpu.make_async_copy(
@@ -217,11 +227,9 @@
             def _():
                 for passage in range(slots):
                     rows = slice(passage * tokens, (passage + 1) * tokens)
-                    both = kept[array][slot, rows] + other[array][slot, rows]
-                    buffer[at, passage] = both * live[passage]
+                    buffer[at, passage] = kept[array][slot, rows] + other[array][slot, rows]
                 copy.start()
 
-            at += 1
     for mine, copy in steps:
 
         @pl.when(mine)
@@ -229,18 +237,17 @@
             copy.wait()
 
 
-def finish(kept, other, distances, counts, donors, slots, held=()):
+def finish(kept, other, distances, slots, held=()):
     rows = kept[0].shape[1]
     tokens = rows // slots
-    smem = pl.BlockSpec(memory_space=pltpu.SMEM)
     vmem = pl.BlockSpec(memory_space=pltpu.VMEM)
     away = pl.BlockSpec(memory_space=pl.ANY)
     blocks = sum(len(group) for group in distances)
-    n_in = 2 + 2 * len(kept)
+    n_in = 2 * len(kept)
     return pl.pallas_call(
         functools.partial(finish_kernel, distances),
         out_shape=jax.ShapeDtypeStruct((slots, tokens, 4 * CHUNK), jnp.bfloat16),
-        in_specs=[smem, smem] + [vmem] * (n_in - 2) + [away] * len(held),
+        in_specs=[vmem] * n_in + [away] * len(held),
         out_specs=away,
         scratch_shapes=[
             pltpu.VMEM((blocks, slots, tokens, CHUNK), jnp.bfloat16),
@@ -253,7 +260,7 @@
             bytes_accessed=blocks * rows * CHUNK * 3,
             transcendentals=0,
         ),
-    )(counts, donors, *kept, *other, *held)
+    )(*kept, *other, *held)
 
 
 def with_ring(queries, key_rows, values, position_bias, out_weight, counts, donors, reps, dp_size):
@@ -277,11 +284,11 @@
     barrier = lax.optimization_barrier
 
     p1, q1 = send(out_weight[:-cut], ahead), send(out_weight[cut:], back)
-    c0 = attend(queries, key_rows, values, position_bias, 0, 2)
+    c0 = attend(queries, key_rows, values, position_bias, counts, donors, 0, 2)
     p1, c0 = barrier((p1, c0))
 
     p2, q2, y1 = send(p1, ahead), send(q1, back), send(edge(p1, q1), across)
-    c1 = attend(queries, key_rows, values, position_bias, 2, 2, (c0,))
+    c1 = attend(queries, key_rows, values, position_bias, counts, donors, 2, 2, (c0,))
     p2, c1 = barrier((p2, c1))
     context = (c0, c1)
 
@@ -304,28 +311,25 @@
     )
     e2 = project(context, (p2, q2, y2), [p_block(0, 2), q_block(1, 2)], jnp.bfloat16)
     started = project(context, (p3, q3), [p_part, q_part], jnp.float32)
-    p4, q4, y3, e1, e2, started = barrier((p4, q4, y3, e1, e2, started))
+    p4, q4, y3, e2, started = barrier((p4, q4, y3, e2, started))
 
     x1, x2 = send(e1, cores), send(e2, cores)
     e3 = project(
         context, (p3, q3, y3, p4, q4), [p_rest, q_rest, opposite], jnp.bfloat16, (started,)
     )
     x3 = send(e3, cores)
-    early = finish((e1,), (x1,), ((0, 1, -1),), counts, donors, slots)
-    x2, x3, early = barrier((x2, x3, early))
-    return finish((e2, e3), (x2, x3), ((2, -2), (3, -3, 4)), counts, donors, slots, (early,))
+    early = finish((e1, e2), (x1, x2), ((0, 1, -1), (2, -2)), slots)
+    x3, early = barrier((x3, early))
+    return finish((e3,), (x3,), ((3, -3, 4),), slots, (early,))
 
 
 def with_gather(queries, key_rows, values, position_bias, out_weight, counts, donors):
     slots, tokens, features = queries.shape
     whole = lax.all_gather(out_weight, "dp", axis=1, tiled=True)
-    context = attend(queries, key_rows, values, position_bias, 0, features // CHUNK)
+    context = attend(queries, key_rows, values, position_bias, counts, donors, 0, features // CHUNK)
     product = jnp.dot(context, whole, preferred_element_type=jnp.float32).astype(jnp.bfloat16)
     merged = lax.psum_scatter(product, "tensor", scatter_dimension=1, tiled=True)
-    first_live = counts[0] >= 1
-    second_live = jnp.any(donors == lax.axis_index("dp"))
-    live = jnp.stack([first_live, second_live]).astype(jnp.bfloat16)
-    return merged.reshape(slots, tokens, merged.shape[1]) * live[:, None, None]
+    return merged.reshape(slots, tokens, merged.shape[1])
 
 
 def solution(mesh):

time: 46.2 us -> 46.7 us (1.011)
  Pallas kernels: 15.8 us -> 14.5 us
  local copies, waits for them, and re-layouts: 3.8 us -> 4.42 us
  starting transfers between devices: 14.6 us -> 15.2 us
    pallas_call x2, Pallas kernels: 2.86 us -> 1.15 us  [finish(): pl.pallas_call(functools.partial(finish_kernel, distances), out_shape=jax...]
    unnamed x12, local copies, waits for them, and re-layouts: 2.46 us -> 3.09 us
    ppermute x14, starting transfers between devices: 14.6 us -> 15.2 us  [with_ring(): send = lambda value, pairs: lax.ppermute(value, AXES, pairs)]
  transfers between devices with their start and end apart: 14 -> 14, of which waited for: 9 -> 6; matrix products, arithmetic and copies ran while one was open for 0% -> 0% of each run, Pallas kernels for 31% -> 31%
where the time goes in v5:
time: 46.7 us; the launch traced here: 46.2 us
  starting transfers between devices  15.2 us (33%)
  Pallas kernels  14.5 us (31%)
  waiting for transfers between devices  11.2 us (24%)
  local copies, waits for them, and re-layouts  4.42 us (9%)
  between operations  0.86 us (2%)
    ppermute x14, starting transfers between devices, with_ring(): send = lambda value, pairs: lax.ppermute(value, AXES, pairs)  15.2 us
    ppermute x14, waiting for transfers between devices, with_ring(): send = lambda value, pairs: lax.ppermute(value, AXES, pairs)  11.2 us
    pallas_call x2, Pallas kernels, attend(): pl.pallas_call(functools.partial(attention_kernel, first), out_shape=jax....  10.4 us
    unnamed x12, local copies, waits for them, and re-layouts  3.09 us
    pallas_call x4, Pallas kernels, project(): pl.pallas_call(functools.partial(project_kernel, plan, len(context), len(...  2.97 us
    slice x1, local copies, waits for them, and re-layouts, with_ring(): p1, q1 = (send(out_weight[:-cut], ahead), send(out_weight[cut:], back))  1.22 us
    pallas_call x2, Pallas kernels, finish(): pl.pallas_call(functools.partial(finish_kernel, distances), out_shape=jax...  1.15 us
  transfers between devices with their start and end apart: 14, of which 6 were waited for; matrix products, arithmetic and copies ran while one was open for 0% of the time, Pallas kernels for 31%

profile of v5, /device:TPU:0, one launch (start us, length us, event | category | flops | bytes accessed | tf_op | source)
XLA Modules:
  0.0 46.2 jit_solution(698819410743202326)
XLA Ops:
  0.0 1.2 %fusion = (bf16[672,256]{1,0:T(8,128)(2,1)S(1)}, bf16[672,256]{1,0:T(8,128)(2,1)S(1)}) fusion(bf16[1024,256]{1,0:T(8,128)(2,1)} %refs_2_.5), kind=kLoop, calls=%fused_computation.3 | loop fusion | bytes 1376256 | tf_op jit(solution)/shard_map/slice | solution.py:286
  1.2 3.1 %collective-permute-start = (bf16[672,256]{1,0:T(8,128)(2,1)S(1)}, bf16[672,256]{1,0:T(8,128)(2,1)S(1)}, u32[]{:S(2)}, u32[]{:S(2)}) collective-permute-start(bf16[672,256]{1,0:T(8,128)(2,1)S(1)} %get-tuple-element.34), channel_id=1, source_target_pairs={{0,4},{1,5},{4,8},{5,9},{8,12},{9,13},{12,14},{13,15},{14,10},{15,... | collective-permute-start | bytes 1032200 | tf_op jit(solution)/shard_map/ppermute | solution.py:277
  5.0 0.6 %copy-done.5 = s32[4]{0:T(128)S(1)} copy-done((s32[4]{0:T(128)S(1)}, s32[4]{0:T(128)}, u32[]{:S(2)}) %copy-start.5) | copy-done | bytes 40
  5.6 1.2 %copy-done.1 = bf16[2,256,1024]{2,1,0:T(8,128)(2,1)S(1)} copy-done((bf16[2,256,1024]{2,1,0:T(8,128)(2,1)S(1)}, bf16[2,256,1024]{2,1,0:T(8,128)(2,1)}, u32[]{:S(2)}) %copy-start.1) | copy-done | bytes 1048600
  6.8 1.2 %copy-done.2 = bf16[2,256,1024]{2,1,0:T(8,128)(2,1)S(1)} copy-done((bf16[2,256,1024]{2,1,0:T(8,128)(2,1)S(1)}, bf16[2,256,1024]{2,1,0:T(8,128)(2,1)}, u32[]{:S(2)}) %copy-start.2) | copy-done | bytes 1048600
  8.1 5.2 %shard_map.73.refs_5_.refs_0_ = bf16[512,512]{1,0:T(8,128)(2,1)S(1)} custom-call(f32[16,32]{1,0:T(8,128)S(1)} %bitcast.1, bf16[2,256,1024]{2,1,0:T(8,128)(2,1)S(1)} %copy-done, bf16[2,256,1024]{2,1,0:T(8,128)(2,1)S(1)} %copy-done.1, bf16[2,256,1024]{2,1,0:T(8,128)(2,1)S(1)} %copy-done.2, s32[1]{0:T(128)S(6)} %copy.10.refs_3_, s32[4]{0:T(128)S(1)} %copy-done.5), custom_call_target="tpu_custom_call" | custom-call | flops 268435456 | bytes 2097152 | tf_op jit(solution)/shard_map/pallas_call | solution.py:118
  13.3 2.1 %collective-permute-start.1 = (bf16[672,256]{1,0:T(8,128)(2,1)S(1)}, bf16[672,256]{1,0:T(8,128)(2,1)S(1)}, u32[]{:S(2)}, u32[]{:S(2)}) collective-permute-start(bf16[672,256]{1,0:T(8,128)(2,1)S(1)} %collective-permute-done.refs_3_), channel_id=1, source_target_pairs={{0,4},{1,5},{4,8},{5,9},{8,12},{9,13},{12,14},{13,15},{14,10},{15,... | collective-permute-start | bytes 1032200 | tf_op jit(solution)/shard_map/ppermute | solution.py:277
  15.4 2.0 %collective-permute-start.6 = (bf16[704,256]{1,0:T(8,128)(2,1)S(1)}, bf16[704,256]{1,0:T(8,128)(2,1)S(1)}, u32[]{:S(2)}, u32[]{:S(2)}) collective-permute-start(bf16[704,256]{1,0:T(8,128)(2,1)S(1)} %pad_maximum_fusion), channel_id=1, source_target_pairs={{0,16},{1,17},{2,18},{3,19},{4,20},{5,21},{6,22},{7,23},{8,24},{9,... | collective-permute-start | bytes 1081352 | tf_op jit(solution)/shard_map/ppermute | solution.py:277
  17.5 5.2 %shard_map.74.refs_1_ = bf16[512,512]{1,0:T(8,128)(2,1)S(1)} custom-call(f32[16,32]{1,0:T(8,128)S(1)} %bitcast.2, bf16[2,256,1024]{2,1,0:T(8,128)(2,1)S(1)} %copy-done, bf16[2,256,1024]{2,1,0:T(8,128)(2,1)S(1)} %copy-done.1, bf16[2,256,1024]{2,1,0:T(8,128)(2,1)S(1)} %copy-done.2, s32[1]{0:T(128)S(6)} %copy.10.refs_3_, s32[4]{0:T(128)S(1)} %copy-done.5, ...), custom_call_target="tpu_custom_call" | custom-call | flops 268435456 | bytes 2097152 | tf_op jit(solution)/shard_map/pallas_call | solution.py:118
  22.9 1.7 %collective-permute-start.2 = (bf16[672,256]{1,0:T(8,128)(2,1)S(1)}, bf16[672,256]{1,0:T(8,128)(2,1)S(1)}, u32[]{:S(2)}, u32[]{:S(2)}) collective-permute-start(bf16[672,256]{1,0:T(8,128)(2,1)S(1)} %collective-permute-done.1.refs_2_), channel_id=1, source_target_pairs={{0,4},{1,5},{4,8},{5,9},{8,12},{9,13},{12,14},{13,15},{14,10},{15,... | collective-permute-start | bytes 1032200 | tf_op jit(solution)/shard_map/ppermute | solution.py:277
  25.0 1.7 %collective-permute-start.10 = (bf16[704,256]{1,0:T(8,128)(2,1)S(1)}, bf16[704,256]{1,0:T(8,128)(2,1)S(1)}, u32[]{:S(2)}, u32[]{:S(2)}) collective-permute-start(bf16[704,256]{1,0:T(8,128)(2,1)S(1)} %pad_maximum_fusion.2), channel_id=1, source_target_pairs={{0,16},{1,17},{2,18},{3,19},{4,20},{5,21},{6,22},{7,23},{8,24},{9,... | collective-permute-start | bytes 1081352 | tf_op jit(solution)/shard_map/ppermute | solution.py:277
  26.7 4.8 %collective-permute-done.2.refs_2_ = bf16[672,256]{1,0:T(8,128)(2,1)S(1)} collective-permute-done((bf16[672,256]{1,0:T(8,128)(2,1)S(1)}, bf16[672,256]{1,0:T(8,128)(2,1)S(1)}, u32[]{:S(2)}, u32[]{:S(2)}) %collective-permute-start.2) | collective-permute-done | bytes 344096 | tf_op jit(solution)/shard_map/ppermute | solution.py:277
  31.5 1.2 %collective-permute-done.5.refs_3_ = bf16[672,256]{1,0:T(8,128)(2,1)S(1)} collective-permute-done((bf16[672,256]{1,0:T(8,128)(2,1)S(1)}, bf16[672,256]{1,0:T(8,128)(2,1)S(1)}, u32[]{:S(2)}, u32[]{:S(2)}) %collective-permute-start.5) | collective-permute-done | bytes 344096 | tf_op jit(solution)/shard_map/ppermute | solution.py:277
  32.7 1.5 %collective-permute-start.9 = (bf16[704,256]{1,0:T(8,128)(2,1)S(1)}, bf16[704,256]{1,0:T(8,128)(2,1)S(1)}, u32[]{:S(2)}, u32[]{:S(2)}) collective-permute-start(bf16[704,256]{1,0:T(8,128)(2,1)S(1)} %pad_maximum_fusion.1), channel_id=1, source_target_pairs={{0,16},{1,17},{2,18},{3,19},{4,20},{5,21},{6,22},{7,23},{8,24},{9,... | collective-permute-start | bytes 1081352 | tf_op jit(solution)/shard_map/ppermute | solution.py:277
  34.3 0.6 %collective-permute-start.7 = (bf16[512,256]{1,0:T(8,128)(2,1)S(1)}, bf16[512,256]{1,0:T(8,128)(2,1)S(1)}, u32[]{:S(2)}, u32[]{:S(2)}) collective-permute-start(bf16[512,256]{1,0:T(8,128)(2,1)S(1)} %slice.34), channel_id=1, source_target_pairs={{0,4},{1,5},{4,8},{5,9},{8,12},{9,13},{12,14},{13,15},{14,10},{15,... | collective-permute-start | bytes 786440 | tf_op jit(solution)/shard_map/ppermute | solution.py:277
  34.9 1.5 %collective-permute-start.8 = (bf16[512,256]{1,0:T(8,128)(2,1)S(1)}, bf16[512,256]{1,0:T(8,128)(2,1)S(1)}, u32[]{:S(2)}, u32[]{:S(2)}) collective-permute-start(bf16[512,256]{1,0:T(8,128)(2,1)S(1)} %slice.35), channel_id=1, source_target_pairs={{0,2},{1,3},{4,0},{5,1},{8,4},{9,5},{12,8},{13,9},{14,12},{15,13},... | collective-permute-start | bytes 786440 | tf_op jit(solution)/shard_map/ppermute | solution.py:277
  36.4 1.0 %shard_map.78.refs_0_ = bf16[3,512,256]{2,1,0:T(8,128)(2,1)S(1)} custom-call(bf16[512,512]{1,0:T(8,128)(2,1)S(1)} %shard_map.73.refs_5_.refs_0_, bf16[512,512]{1,0:T(8,128)(2,1)S(1)} %shard_map.74.refs_1_, bf16[1024,256]{1,0:T(8,128)(2,1)S(1)} %copy-done.3, bf16[672,256]{1,0:T(8,128)(2,1)S(1)} %collective-permute-done.refs_3_, ...), custom_call_target="tpu_custom_call" | custom-call | flops 805306368 | bytes 2359296 | tf_op jit(solution)/shard_map/pallas_call | solution.py:195
  37.4 0.6 %shard_map.76.refs_7_ = f32[2,512,256]{2,1,0:T(8,128)S(1)} custom-call(bf16[512,512]{1,0:T(8,128)(2,1)S(1)} %shard_map.73.refs_5_.refs_0_, bf16[512,512]{1,0:T(8,128)(2,1)S(1)} %shard_map.74.refs_1_, bf16[672,256]{1,0:T(8,128)(2,1)S(1)} %collective-permute-done.2.refs_2_, bf16[672,256]{1,0:T(8,128)(2,1)S(1)} %collective-permute-done.5.refs_3_), custom_call_target="tpu_custom_call" | custom-call | flops 335544320 | bytes 1179648 | tf_op jit(solution)/shard_map/pallas_call | solution.py:195
  38.0 0.7 %shard_map.75.refs_1_ = bf16[2,512,256]{2,1,0:T(8,128)(2,1)S(1)} custom-call(bf16[512,512]{1,0:T(8,128)(2,1)S(1)} %shard_map.73.refs_5_.refs_0_, bf16[512,512]{1,0:T(8,128)(2,1)S(1)} %shard_map.74.refs_1_, bf16[672,256]{1,0:T(8,128)(2,1)S(1)} %collective-permute-done.1.refs_2_, bf16[672,256]{1,0:T(8,128)(2,1)S(1)} %collective-permute-done.4.refs_3_, ...), custom_call_target="tpu_custom_call" | custom-call | flops 536870912 | bytes 1572864 | tf_op jit(solution)/shard_map/pallas_call | solution.py:195
  38.7 2.0 %collective-permute-done.7.refs_5_ = bf16[512,256]{1,0:T(8,128)(2,1)S(1)} collective-permute-done((bf16[512,256]{1,0:T(8,128)(2,1)S(1)}, bf16[512,256]{1,0:T(8,128)(2,1)S(1)}, u32[]{:S(2)}, u32[]{:S(2)}) %collective-permute-start.7) | collective-permute-done | bytes 262176 | tf_op jit(solution)/shard_map/ppermute | solution.py:277
  40.7 0.5 %collective-permute-done.8.refs_6_ = bf16[512,256]{1,0:T(8,128)(2,1)S(1)} collective-permute-done((bf16[512,256]{1,0:T(8,128)(2,1)S(1)}, bf16[512,256]{1,0:T(8,128)(2,1)S(1)}, u32[]{:S(2)}, u32[]{:S(2)}) %collective-permute-start.8) | collective-permute-done | bytes 262176 | tf_op jit(solution)/shard_map/ppermute | solution.py:277
  41.2 0.7 %shard_map.77.refs_0_ = bf16[3,512,256]{2,1,0:T(8,128)(2,1)S(1)} custom-call(bf16[512,512]{1,0:T(8,128)(2,1)S(1)} %shard_map.73.refs_5_.refs_0_, bf16[512,512]{1,0:T(8,128)(2,1)S(1)} %shard_map.74.refs_1_, bf16[672,256]{1,0:T(8,128)(2,1)S(1)} %collective-permute-done.2.refs_2_, bf16[672,256]{1,0:T(8,128)(2,1)S(1)} %collective-permute-done.5.refs_3_, ...), custom_call_target="tpu_custom_call" | custom-call | flops 469762048 | bytes 1703936 | tf_op jit(solution)/shard_map/pallas_call | solution.py:195
  42.5 2.5 %collective-permute-done.13.refs_3_ = bf16[2,512,256]{2,1,0:T(8,128)(2,1)S(1)} collective-permute-done((bf16[2,512,256]{2,1,0:T(8,128)(2,1)S(1)}, bf16[2,512,256]{2,1,0:T(8,128)(2,1)S(1)}, u32[]{:S(2)}, u32[]{:S(2)}) %collective-permute-start.13) | collective-permute-done | bytes 524320 | tf_op jit(solution)/shard_map/ppermute | solution.py:277
  45.1 1.0 %shard_map.79.refs_2_ = bf16[2,256,1024]{2,1,0:T(8,128)(2,1)} custom-call(bf16[3,512,256]{2,1,0:T(8,128)(2,1)S(1)} %shard_map.78.refs_0_, bf16[2,512,256]{2,1,0:T(8,128)(2,1)S(1)} %shard_map.75.refs_1_, bf16[3,512,256]{2,1,0:T(8,128)(2,1)S(1)} %collective-permute-done.12.refs_2_, bf16[2,512,256]{2,1,0:T(8,128)(2,1)S(1)} %collective-permute-done.13.refs_3_), custom_call_target="tpu_custom_call" | custom-call | flops 655360 | bytes 1966080 | tf_op jit(solution)/shard_map/pallas_call | solution.py:247
  (36 shorter events, 1.5 us)
Async XLA Ops:
  0.0 5.0 %copy-start = (bf16[2,256,1024]{2,1,0:T(8,128)(2,1)S(1)}, bf16[2,256,1024]{2,1,0:T(8,128)(2,1)}, u32[]{:S(2)}) copy-start(bf16[2,256,1024]{2,1,0:T(8,128)(2,1)} %refs_0_.3) | copy-start | bytes 3145732
  0.0 5.0 %copy-start.4 = (f32[32,16]{0,1:T(8,128)S(1)}, f32[32,16]{0,1:T(8,128)}, u32[]{:S(2)}) copy-start(f32[32,16]{0,1:T(8,128)} %param.10) | copy-start | bytes 6148
  1.2 12.1 %collective-permute-start = (bf16[672,256]{1,0:T(8,128)(2,1)S(1)}, bf16[672,256]{1,0:T(8,128)(2,1)S(1)}, u32[]{:S(2)}, u32[]{:S(2)}) collective-permute-start(bf16[672,256]{1,0:T(8,128)(2,1)S(1)} %get-tuple-element.34), channel_id=1, source_target_pairs={{0,4},{1,5},{4,8},{5,9},{8,12},{9,13},{12,14},{13,15},{14,10},{15,... | collective-permute-start | bytes 1032200 | tf_op jit(solution)/shard_map/ppermute | solution.py:277
  4.3 11.1 %collective-permute-start.3 = (bf16[672,256]{1,0:T(8,128)(2,1)S(1)}, bf16[672,256]{1,0:T(8,128)(2,1)S(1)}, u32[]{:S(2)}, u32[]{:S(2)}) collective-permute-start(bf16[672,256]{1,0:T(8,128)(2,1)S(1)} %get-tuple-element.33), channel_id=1, source_target_pairs={{0,2},{1,3},{4,0},{5,1},{8,4},{9,5},{12,8},{13,9},{14,12},{15,13},... | collective-permute-start | bytes 1032200 | tf_op jit(solution)/shard_map/ppermute | solution.py:277
  5.0 0.7 %copy-start.5 = (s32[4]{0:T(128)S(1)}, s32[4]{0:T(128)}, u32[]{:S(2)}) copy-start(s32[4]{0:T(128)} %refs_4_.3) | copy-start | bytes 52
  5.6 1.2 %copy-start.1 = (bf16[2,256,1024]{2,1,0:T(8,128)(2,1)S(1)}, bf16[2,256,1024]{2,1,0:T(8,128)(2,1)}, u32[]{:S(2)}) copy-start(bf16[2,256,1024]{2,1,0:T(8,128)(2,1)} %refs_1_.3) | copy-start | bytes 3145732
  6.8 1.2 %copy-start.2 = (bf16[2,256,1024]{2,1,0:T(8,128)(2,1)S(1)}, bf16[2,256,1024]{2,1,0:T(8,128)(2,1)}, u32[]{:S(2)}) copy-start(bf16[2,256,1024]{2,1,0:T(8,128)(2,1)} %refs_2_.4) | copy-start | bytes 3145732
  13.3 9.6 %collective-permute-start.1 = (bf16[672,256]{1,0:T(8,128)(2,1)S(1)}, bf16[672,256]{1,0:T(8,128)(2,1)S(1)}, u32[]{:S(2)}, u32[]{:S(2)}) collective-permute-start(bf16[672,256]{1,0:T(8,128)(2,1)S(1)} %collective-permute-done.refs_3_), channel_id=1, source_target_pairs={{0,4},{1,5},{4,8},{5,9},{8,12},{9,13},{12,14},{13,15},{14,10},{15,... | collective-permute-start | bytes 1032200 | tf_op jit(solution)/shard_map/ppermute | solution.py:277
  15.4 9.2 %collective-permute-start.4 = (bf16[672,256]{1,0:T(8,128)(2,1)S(1)}, bf16[672,256]{1,0:T(8,128)(2,1)S(1)}, u32[]{:S(2)}, u32[]{:S(2)}) collective-permute-start(bf16[672,256]{1,0:T(8,128)(2,1)S(1)} %collective-permute-done.3.refs_4_), channel_id=1, source_target_pairs={{0,2},{1,3},{4,0},{5,1},{8,4},{9,5},{12,8},{13,9},{14,12},{15,13},... | collective-permute-start | bytes 1032200 | tf_op jit(solution)/shard_map/ppermute | solution.py:277
  15.4 11.3 %collective-permute-start.6 = (bf16[704,256]{1,0:T(8,128)(2,1)S(1)}, bf16[704,256]{1,0:T(8,128)(2,1)S(1)}, u32[]{:S(2)}, u32[]{:S(2)}) collective-permute-start(bf16[704,256]{1,0:T(8,128)(2,1)S(1)} %pad_maximum_fusion), channel_id=1, source_target_pairs={{0,16},{1,17},{2,18},{3,19},{4,20},{5,21},{6,22},{7,23},{8,24},{9,... | collective-permute-start | bytes 1081352 | tf_op jit(solution)/shard_map/ppermute | solution.py:277
  22.9 8.6 %collective-permute-start.2 = (bf16[672,256]{1,0:T(8,128)(2,1)S(1)}, bf16[672,256]{1,0:T(8,128)(2,1)S(1)}, u32[]{:S(2)}, u32[]{:S(2)}) collective-permute-start(bf16[672,256]{1,0:T(8,128)(2,1)S(1)} %collective-permute-done.1.refs_2_), channel_id=1, source_target_pairs={{0,4},{1,5},{4,8},{5,9},{8,12},{9,13},{12,14},{13,15},{14,10},{15,... | collective-permute-start | bytes 1032200 | tf_op jit(solution)/shard_map/ppermute | solution.py:277
  24.6 8.0 %collective-permute-start.5 = (bf16[672,256]{1,0:T(8,128)(2,1)S(1)}, bf16[672,256]{1,0:T(8,128)(2,1)S(1)}, u32[]{:S(2)}, u32[]{:S(2)}) collective-permute-start(bf16[672,256]{1,0:T(8,128)(2,1)S(1)} %collective-permute-done.4.refs_3_), channel_id=1, source_target_pairs={{0,2},{1,3},{4,0},{5,1},{8,4},{9,5},{12,8},{13,9},{14,12},{15,13},... | collective-permute-start | bytes 1032200 | tf_op jit(solution)/shard_map/ppermute | solution.py:277
  25.0 13.0 %collective-permute-start.10 = (bf16[704,256]{1,0:T(8,128)(2,1)S(1)}, bf16[704,256]{1,0:T(8,128)(2,1)S(1)}, u32[]{:S(2)}, u32[]{:S(2)}) collective-permute-start(bf16[704,256]{1,0:T(8,128)(2,1)S(1)} %pad_maximum_fusion.2), channel_id=1, source_target_pairs={{0,16},{1,17},{2,18},{3,19},{4,20},{5,21},{6,22},{7,23},{8,24},{9,... | collective-permute-start | bytes 1081352 | tf_op jit(solution)/shard_map/ppermute | solution.py:277
  32.7 3.6 %copy-start.3 = (bf16[1024,256]{1,0:T(8,128)(2,1)S(1)}, bf16[1024,256]{1,0:T(8,128)(2,1)}, u32[]{:S(2)}) copy-start(bf16[1024,256]{1,0:T(8,128)(2,1)} %refs_2_.5) | copy-start | bytes 1572868
  32.7 8.5 %collective-permute-start.9 = (bf16[704,256]{1,0:T(8,128)(2,1)S(1)}, bf16[704,256]{1,0:T(8,128)(2,1)S(1)}, u32[]{:S(2)}, u32[]{:S(2)}) collective-permute-start(bf16[704,256]{1,0:T(8,128)(2,1)S(1)} %pad_maximum_fusion.1), channel_id=1, source_target_pairs={{0,16},{1,17},{2,18},{3,19},{4,20},{5,21},{6,22},{7,23},{8,24},{9,... | collective-permute-start | bytes 1081352 | tf_op jit(solution)/shard_map/ppermute | solution.py:277
  34.3 6.4 %collective-permute-start.7 = (bf16[512,256]{1,0:T(8,128)(2,1)S(1)}, bf16[512,256]{1,0:T(8,128)(2,1)S(1)}, u32[]{:S(2)}, u32[]{:S(2)}) collective-permute-start(bf16[512,256]{1,0:T(8,128)(2,1)S(1)} %slice.34), channel_id=1, source_target_pairs={{0,4},{1,5},{4,8},{5,9},{8,12},{9,13},{12,14},{13,15},{14,10},{15,... | collective-permute-start | bytes 786440 | tf_op jit(solution)/shard_map/ppermute | solution.py:277
  34.9 6.4 %collective-permute-start.8 = (bf16[512,256]{1,0:T(8,128)(2,1)S(1)}, bf16[512,256]{1,0:T(8,128)(2,1)S(1)}, u32[]{:S(2)}, u32[]{:S(2)}) collective-permute-start(bf16[512,256]{1,0:T(8,128)(2,1)S(1)} %slice.35), channel_id=1, source_target_pairs={{0,2},{1,3},{4,0},{5,1},{8,4},{9,5},{12,8},{13,9},{14,12},{15,13},... | collective-permute-start | bytes 786440 | tf_op jit(solution)/shard_map/ppermute | solution.py:277
  37.4 5.2 %collective-permute-start.12 = (bf16[3,512,256]{2,1,0:T(8,128)(2,1)S(1)}, bf16[3,512,256]{2,1,0:T(8,128)(2,1)S(1)}, u32[]{:S(2)}, u32[]{:S(2)}) collective-permute-start(bf16[3,512,256]{2,1,0:T(8,128)(2,1)S(1)} %shard_map.78.refs_0_), channel_id=1, source_target_pairs={{0,1},{1,0},{2,3},{3,2},{4,5},{5,4},{6,7},{7,6},{8,9},{9,8},{10,11... | collective-permute-start | bytes 2359304 | tf_op jit(solution)/shard_map/ppermute | solution.py:277
  42.0 4.1 %collective-permute-start.11 = (bf16[3,512,256]{2,1,0:T(8,128)(2,1)S(1)}, bf16[3,512,256]{2,1,0:T(8,128)(2,1)S(1)}, u32[]{:S(2)}, u32[]{:S(2)}) collective-permute-start(bf16[3,512,256]{2,1,0:T(8,128)(2,1)S(1)} %shard_map.77.refs_0_), channel_id=1, source_target_pairs={{0,1},{1,0},{2,3},{3,2},{4,5},{5,4},{6,7},{7,6},{8,9},{9,8},{10,11... | collective-permute-start | bytes 2359304 | tf_op jit(solution)/shard_map/ppermute | solution.py:277
  42.0 3.0 %collective-permute-start.13 = (bf16[2,512,256]{2,1,0:T(8,128)(2,1)S(1)}, bf16[2,512,256]{2,1,0:T(8,128)(2,1)S(1)}, u32[]{:S(2)}, u32[]{:S(2)}) collective-permute-start(bf16[2,512,256]{2,1,0:T(8,128)(2,1)S(1)} %shard_map.75.refs_1_), channel_id=1, source_target_pairs={{0,1},{1,0},{2,3},{3,2},{4,5},{5,4},{6,7},{7,6},{8,9},{9,8},{10,11... | collective-permute-start | bytes 1572872 | tf_op jit(solution)/shard_map/ppermute | solution.py:277

commit v6 on v4

--- a/solution.py
+++ b/solution.py
@@ -33,9 +33,10 @@
     )
 
 
-def attention_kernel(first, bias_ref, *refs):
+def attention_kernel(first, joined, bias_ref, *refs):
     sources, (out_ref, held, sem) = refs[:3], refs[-3:]
     count, _, slots, tokens, width = held.shape
+    offset = out_ref.shape[1] - count * width
     copies = [
         [
             pltpu.make_async_copy(
@@ -50,6 +51,8 @@
     for chunk in copies:
         for copy in chunk:
             copy.start()
+    if joined:
+        out_ref[:, :offset] = refs[3][...]
     rows = bias_rows(bias_ref[...], tokens)
     lower = lax.broadcasted_iota(jnp.int32, (tokens, PAIR), 1) < HEAD_DIM
     for chunk in range(count):
@@ -78,7 +81,8 @@
                     )
                 weighted = jnp.where(lower, sums[0], sums[1])
                 total = pltpu.roll(jnp.where(lower, sums[1], sums[0]), HEAD_DIM, 1)
-                at = slice(chunk * width + pair * PAIR, chunk * width + (pair + 1) * PAIR)
+                at = offset + chunk * width + pair * PAIR
+                at = slice(at, at + PAIR)
                 out_ref[slot * tokens : (slot + 1) * tokens, at] = (weighted / total).astype(
                     jnp.bfloat16
                 )
@@ -97,15 +101,17 @@
     return jnp.concatenate(groups, axis=0)
 
 
-def attend(queries, key_rows, values, position_bias, first, count, after=()):
+def attend(queries, key_rows, values, position_bias, first, count, after=(), joined=False):
     slots, tokens, _ = queries.shape
     vmem = pl.BlockSpec(memory_space=pltpu.VMEM)
     away = pl.BlockSpec(memory_space=pltpu.HBM)
+    last = vmem if joined else pl.BlockSpec(memory_space=pl.ANY)
+    columns = CHUNK * count + (after[0].shape[1] if joined else 0)
     scores = slots * (CHUNK // HEAD_DIM) * tokens * tokens * count
     return pl.pallas_call(
-        functools.partial(attention_kernel, first),
-        out_shape=jax.ShapeDtypeStruct((slots * tokens, CHUNK * count), jnp.bfloat16),
-        in_specs=[vmem] + [away] * 3 + [pl.BlockSpec(memory_space=pl.ANY)] * len(after),
+        functools.partial(attention_kernel, first, joined),
+        out_shape=jax.ShapeDtypeStruct((slots * tokens, columns), jnp.bfloat16),
+        in_specs=[vmem] + [away] * 3 + [last] * len(after),
         out_specs=vmem,
         scratch_shapes=[
             pltpu.VMEM((count, 3, slots, tokens, CHUNK), jnp.bfloat16),
@@ -154,10 +160,11 @@
     return jnp.where(place < 4, 2 * place, 2 * (7 - place) + 1)
 
 
-def project_kernel(plan, n_context, n_weights, *refs):
+def project_kernel(plan, n_context, n_weights, choice, *refs):
     context = refs[:n_context]
     weights = refs[n_context : n_context + n_weights]
-    bases, out_ref = refs[n_context + n_weights : -1], refs[-1]
+    n_out = 2 if choice else 1
+    bases, out_ref = refs[n_context + n_weights : -n_out], refs[-n_out]
     for slot, products in enumerate(plan):
         total = bases[0][slot] if bases and slot < bases[0].shape[0] else None
         for source, column, pieces in products:
@@ -170,17 +177,25 @@
             )
             total = part if total is None else total + part
         out_ref[slot] = total.astype(out_ref.dtype)
-
-
-def project(context, weights, plan, kind, bases=()):
+        if choice:
+
+            @pl.when(block_of(choice[slot]) // 4 != lax.axis_index("tensor"))
+            def _():
+                refs[-1][0] = total.astype(out_ref.dtype)
+
+
+def project(context, weights, plan, kind, bases=(), choice=None):
     rows = context[0].shape[0]
     depth = sum(piece[-1] for block in plan for product in block for piece in product[-1])
     vmem = pl.BlockSpec(memory_space=pltpu.VMEM)
     return pl.pallas_call(
-        functools.partial(project_kernel, plan, len(context), len(weights)),
-        out_shape=jax.ShapeDtypeStruct((len(plan), rows, CHUNK), kind),
+        functools.partial(project_kernel, plan, len(context), len(weights), choice),
+        out_shape=[
+            jax.ShapeDtypeStruct((blocks, rows, CHUNK), kind)
+            for blocks in ((len(plan), 1) if choice else (len(plan),))
+        ],
         in_specs=[vmem] * (len(context) + len(weights) + len(bases)),
-        out_specs=vmem,
+        out_specs=[vmem] * (2 if choice else 1),
         compiler_params=pltpu.CompilerParams(vmem_limit_bytes=12 << 20),
         cost_estimate=pl.CostEstimate(
             flops=2 * rows * depth * CHUNK,
@@ -205,6 +220,7 @@
     at = 0
     steps = []
     for array, group in enumerate(distances):
+        several = other[array].shape[0] > 1
         for slot, distance in enumerate(group):
             block = block_of(distance)
             column = pl.multiple_of(block % 4 * CHUNK, CHUNK)
@@ -217,7 +233,7 @@
             def _():
                 for passage in range(slots):
                     rows = slice(passage * tokens, (passage + 1) * tokens)
-                    both = kept[array][slot, rows] + other[array][slot, rows]
+                    both = kept[array][slot, rows] + other[array][slot if several else 0, rows]
                     buffer[at, passage] = both * live[passage]
                 copy.start()
 
@@ -281,12 +297,13 @@
     p1, c0 = barrier((p1, c0))
 
     p2, q2, y1 = send(p1, ahead), send(q1, back), send(edge(p1, q1), across)
-    c1 = attend(queries, key_rows, values, position_bias, 2, 2, (c0,))
+    c1 = attend(queries, key_rows, values, position_bias, 2, 1, (c0,))
     p2, c1 = barrier((p2, c1))
+
+    p3, q3, y2 = send(p2, ahead), send(q2, back), send(edge(p2, q2), across)
+    c1 = attend(queries, key_rows, values, position_bias, 3, 1, (c1,), joined=True)
+    p3, q3, y1, c1 = barrier((p3, q3, y1, c1))
     context = (c0, c1)
-
-    p3, q3, y2 = send(p2, ahead), send(q2, back), send(edge(p2, q2), across)
-    p3, q3, y1 = barrier((p3, q3, y1))
 
     own = [(0, 0, [(0, 0, half)]), (1, 0, [(0, half, half)])]
     p_block = lambda p, y: [(0, 0, [(p, 0, half)]), (1, 0, [(p, half, over), (y, cut, cut)])]
@@ -299,15 +316,17 @@
 
     p4, q4 = send(p3[:half], ahead), send(q3[-half:], back)
     y3 = send(edge(p3, q3), across)
-    e1 = project(
+    (e1,) = project(
         context, (out_weight, p1, q1, y1), [own, p_block(1, 3), q_block(2, 3)], jnp.bfloat16
     )
-    e2 = project(context, (p2, q2, y2), [p_block(0, 2), q_block(1, 2)], jnp.bfloat16)
-    started = project(context, (p3, q3), [p_part, q_part], jnp.float32)
-    p4, q4, y3, e1, e2, started = barrier((p4, q4, y3, e1, e2, started))
-
-    x1, x2 = send(e1, cores), send(e2, cores)
-    e3 = project(
+    e2, s2 = project(
+        context, (p2, q2, y2), [p_block(0, 2), q_block(1, 2)], jnp.bfloat16, choice=(2, -2)
+    )
+    (started,) = project(context, (p3, q3), [p_part, q_part], jnp.float32)
+    p4, q4, y3, e2, s2, started = barrier((p4, q4, y3, e2, s2, started))
+
+    x1, x2 = send(e1, cores), send(s2, cores)
+    (e3,) = project(
         context, (p3, q3, y3, p4, q4), [p_rest, q_rest, opposite], jnp.bfloat16, (started,)
     )
     x3 = send(e3, cores)

time: 46.2 us -> 45.5 us (0.985)
  waiting for transfers between devices: 10.8 us -> 9.3 us
  Pallas kernels: 15.8 us -> 16.6 us
    ppermute x14, waiting for transfers between devices: 10.8 us -> 9.3 us  [with_ring(): send = lambda value, pairs: lax.ppermute(value, AXES, pairs)]
    pallas_call x4, Pallas kernels: 2.95 us -> 3.62 us  [project(): pl.pallas_call(functools.partial(project_kernel, plan, len(context), len(...]
    pallas_call x2 -> x3, Pallas kernels: 10 us -> 10.1 us  [attend(): pl.pallas_call(functools.partial(attention_kernel, first, joined), out_sh...]
  transfers between devices with their start and end apart: 14 -> 14, of which waited for: 9 -> 7; matrix products, arithmetic and copies ran while one was open for 0% -> 0% of each run, Pallas kernels for 31% -> 34%
where the time goes in v6:
time: 45.5 us; the launch traced here: 45.3 us
  Pallas kernels  16.6 us (36%)
  starting transfers between devices  14.6 us (32%)
  waiting for transfers between devices  9.3 us (20%)
  local copies, waits for them, and re-layouts  3.8 us (8%)
  between operations  0.89 us (2%)
    ppermute x14, starting transfers between devices, with_ring(): send = lambda value, pairs: lax.ppermute(value, AXES, pairs)  14.6 us
    pallas_call x3, Pallas kernels, attend(): pl.pallas_call(functools.partial(attention_kernel, first, joined), out_sh...  10.1 us
    ppermute x14, waiting for transfers between devices, with_ring(): send = lambda value, pairs: lax.ppermute(value, AXES, pairs)  9.3 us
    pallas_call x4, Pallas kernels, project(): pl.pallas_call(functools.partial(project_kernel, plan, len(context), len(...  3.62 us
    pallas_call x2, Pallas kernels, finish(): pl.pallas_call(functools.partial(finish_kernel, distances), out_shape=jax...  2.86 us
    unnamed x12, local copies, waits for them, and re-layouts  2.46 us
    slice x1, local copies, waits for them, and re-layouts, with_ring(): p1, q1 = (send(out_weight[:-cut], ahead), send(out_weight[cut:], back))  1.22 us
  transfers between devices with their start and end apart: 14, of which 7 were waited for; matrix products, arithmetic and copies ran while one was open for 0% of the time, Pallas kernels for 34%

profile of v6, /device:TPU:0, one launch (start us, length us, event | category | flops | bytes accessed | tf_op | source)
XLA Modules:
  0.0 45.3 jit_solution(4257877551108711869)
XLA Ops:
  0.0 1.2 %fusion = (bf16[672,256]{1,0:T(8,128)(2,1)S(1)}, bf16[672,256]{1,0:T(8,128)(2,1)S(1)}) fusion(bf16[1024,256]{1,0:T(8,128)(2,1)} %refs_2_.7), kind=kLoop, calls=%fused_computation.3 | loop fusion | bytes 1376256 | tf_op jit(solution)/shard_map/slice | solution.py:295
  1.2 3.1 %collective-permute-start = (bf16[672,256]{1,0:T(8,128)(2,1)S(1)}, bf16[672,256]{1,0:T(8,128)(2,1)S(1)}, u32[]{:S(2)}, u32[]{:S(2)}) collective-permute-start(bf16[672,256]{1,0:T(8,128)(2,1)S(1)} %get-tuple-element.44), channel_id=1, source_target_pairs={{0,4},{1,5},{4,8},{5,9},{8,12},{9,13},{12,14},{13,15},{14,10},{15,... | collective-permute-start | bytes 1032200 | tf_op jit(solution)/shard_map/ppermute | solution.py:286
  4.3 1.2 %copy-done.1 = bf16[2,256,1024]{2,1,0:T(8,128)(2,1)S(1)} copy-done((bf16[2,256,1024]{2,1,0:T(8,128)(2,1)S(1)}, bf16[2,256,1024]{2,1,0:T(8,128)(2,1)}, u32[]{:S(2)}) %copy-start.1) | copy-done | bytes 1048600
  5.5 1.2 %copy-done.2 = bf16[2,256,1024]{2,1,0:T(8,128)(2,1)S(1)} copy-done((bf16[2,256,1024]{2,1,0:T(8,128)(2,1)S(1)}, bf16[2,256,1024]{2,1,0:T(8,128)(2,1)}, u32[]{:S(2)}) %copy-start.2) | copy-done | bytes 1048600
  6.8 5.0 %shard_map.73.refs_3_.refs_0_ = bf16[512,512]{1,0:T(8,128)(2,1)S(1)} custom-call(f32[16,32]{1,0:T(8,128)S(1)} %bitcast.1, bf16[2,256,1024]{2,1,0:T(8,128)(2,1)S(1)} %copy-done, bf16[2,256,1024]{2,1,0:T(8,128)(2,1)S(1)} %copy-done.1, bf16[2,256,1024]{2,1,0:T(8,128)(2,1)S(1)} %copy-done.2), custom_call_target="tpu_custom_call" | custom-call | flops 268435456 | bytes 2097152 | tf_op jit(solution)/shard_map/pallas_call | solution.py:111
  12.3 1.8 %collective-permute-start.1 = (bf16[672,256]{1,0:T(8,128)(2,1)S(1)}, bf16[672,256]{1,0:T(8,128)(2,1)S(1)}, u32[]{:S(2)}, u32[]{:S(2)}) collective-permute-start(bf16[672,256]{1,0:T(8,128)(2,1)S(1)} %collective-permute-done.refs_3_), channel_id=1, source_target_pairs={{0,4},{1,5},{4,8},{5,9},{8,12},{9,13},{12,14},{13,15},{14,10},{15,... | collective-permute-start | bytes 1032200 | tf_op jit(solution)/shard_map/ppermute | solution.py:286
  14.4 1.8 %collective-permute-start.6 = (bf16[704,256]{1,0:T(8,128)(2,1)S(1)}, bf16[704,256]{1,0:T(8,128)(2,1)S(1)}, u32[]{:S(2)}, u32[]{:S(2)}) collective-permute-start(bf16[704,256]{1,0:T(8,128)(2,1)S(1)} %pad_maximum_fusion), channel_id=1, source_target_pairs={{0,16},{1,17},{2,18},{3,19},{4,20},{5,21},{6,22},{7,23},{8,24},{9,... | collective-permute-start | bytes 1081352 | tf_op jit(solution)/shard_map/ppermute | solution.py:286
  16.2 2.6 %shard_map.74.refs_3_ = bf16[512,256]{1,0:T(8,128)(2,1)S(1)} custom-call(f32[16,32]{1,0:T(8,128)S(1)} %bitcast.2, bf16[2,256,1024]{2,1,0:T(8,128)(2,1)S(1)} %copy-done, bf16[2,256,1024]{2,1,0:T(8,128)(2,1)S(1)} %copy-done.1, bf16[2,256,1024]{2,1,0:T(8,128)(2,1)S(1)} %copy-done.2, bf16[512,512]{1,0:T(8,128)(2,1)S(1)} %shard_map.73.refs_3_.refs_0_), custom_call_target="tpu_custom_call" | custom-call | flops 134217728 | bytes 1048576 | tf_op jit(solution)/shard_map/pallas_call | solution.py:111
  18.8 2.7 %collective-permute-done.1.refs_2_ = bf16[672,256]{1,0:T(8,128)(2,1)S(1)} collective-permute-done((bf16[672,256]{1,0:T(8,128)(2,1)S(1)}, bf16[672,256]{1,0:T(8,128)(2,1)S(1)}, u32[]{:S(2)}, u32[]{:S(2)}) %collective-permute-start.1) | collective-permute-done | bytes 344096 | tf_op jit(solution)/shard_map/ppermute | solution.py:286
  21.5 1.3 %collective-permute-done.4.refs_3_ = bf16[672,256]{1,0:T(8,128)(2,1)S(1)} collective-permute-done((bf16[672,256]{1,0:T(8,128)(2,1)S(1)}, bf16[672,256]{1,0:T(8,128)(2,1)S(1)}, u32[]{:S(2)}, u32[]{:S(2)}) %collective-permute-start.4) | collective-permute-done | bytes 344096 | tf_op jit(solution)/shard_map/ppermute | solution.py:286
  23.3 1.6 %collective-permute-start.2 = (bf16[672,256]{1,0:T(8,128)(2,1)S(1)}, bf16[672,256]{1,0:T(8,128)(2,1)S(1)}, u32[]{:S(2)}, u32[]{:S(2)}) collective-permute-start(bf16[672,256]{1,0:T(8,128)(2,1)S(1)} %collective-permute-done.1.refs_2_), channel_id=1, source_target_pairs={{0,4},{1,5},{4,8},{5,9},{8,12},{9,13},{12,14},{13,15},{14,10},{15,... | collective-permute-start | bytes 1032200 | tf_op jit(solution)/shard_map/ppermute | solution.py:286
  24.9 1.5 %collective-permute-start.10 = (bf16[704,256]{1,0:T(8,128)(2,1)S(1)}, bf16[704,256]{1,0:T(8,128)(2,1)S(1)}, u32[]{:S(2)}, u32[]{:S(2)}) collective-permute-start(bf16[704,256]{1,0:T(8,128)(2,1)S(1)} %pad_maximum_fusion.2), channel_id=1, source_target_pairs={{0,16},{1,17},{2,18},{3,19},{4,20},{5,21},{6,22},{7,23},{8,24},{9,... | collective-permute-start | bytes 1081352 | tf_op jit(solution)/shard_map/ppermute | solution.py:286
  26.4 2.6 %shard_map.75.refs_1_ = bf16[512,512]{1,0:T(8,128)(2,1)S(1)} custom-call(f32[16,32]{1,0:T(8,128)S(1)} %bitcast.3, bf16[2,256,1024]{2,1,0:T(8,128)(2,1)S(1)} %copy-done, bf16[2,256,1024]{2,1,0:T(8,128)(2,1)S(1)} %copy-done.1, bf16[2,256,1024]{2,1,0:T(8,128)(2,1)S(1)} %copy-done.2, bf16[512,256]{1,0:T(8,128)(2,1)S(1)} %shard_map.74.refs_3_), custom_call_target="tpu_custom_call" | custom-call | flops 134217728 | bytes 1048576 | tf_op jit(solution)/shard_map/pallas_call | solution.py:111
  29.0 1.6 %collective-permute-done.5.refs_3_ = bf16[672,256]{1,0:T(8,128)(2,1)S(1)} collective-permute-done((bf16[672,256]{1,0:T(8,128)(2,1)S(1)}, bf16[672,256]{1,0:T(8,128)(2,1)S(1)}, u32[]{:S(2)}, u32[]{:S(2)}) %collective-permute-start.5) | collective-permute-done | bytes 344096 | tf_op jit(solution)/shard_map/ppermute | solution.py:286
  31.1 1.5 %collective-permute-start.9 = (bf16[704,256]{1,0:T(8,128)(2,1)S(1)}, bf16[704,256]{1,0:T(8,128)(2,1)S(1)}, u32[]{:S(2)}, u32[]{:S(2)}) collective-permute-start(bf16[704,256]{1,0:T(8,128)(2,1)S(1)} %pad_maximum_fusion.1), channel_id=1, source_target_pairs={{0,16},{1,17},{2,18},{3,19},{4,20},{5,21},{6,22},{7,23},{8,24},{9,... | collective-permute-start | bytes 1081352 | tf_op jit(solution)/shard_map/ppermute | solution.py:286
  32.6 1.4 %collective-permute-start.8 = (bf16[512,256]{1,0:T(8,128)(2,1)S(1)}, bf16[512,256]{1,0:T(8,128)(2,1)S(1)}, u32[]{:S(2)}, u32[]{:S(2)}) collective-permute-start(bf16[512,256]{1,0:T(8,128)(2,1)S(1)} %slice.35), channel_id=1, source_target_pairs={{0,2},{1,3},{4,0},{5,1},{8,4},{9,5},{12,8},{13,9},{14,12},{15,13},... | collective-permute-start | bytes 786440 | tf_op jit(solution)/shard_map/ppermute | solution.py:286
  34.1 0.6 %collective-permute-start.7 = (bf16[512,256]{1,0:T(8,128)(2,1)S(1)}, bf16[512,256]{1,0:T(8,128)(2,1)S(1)}, u32[]{:S(2)}, u32[]{:S(2)}) collective-permute-start(bf16[512,256]{1,0:T(8,128)(2,1)S(1)} %slice.34), channel_id=1, source_target_pairs={{0,4},{1,5},{4,8},{5,9},{8,12},{9,13},{12,14},{13,15},{14,10},{15,... | collective-permute-start | bytes 786440 | tf_op jit(solution)/shard_map/ppermute | solution.py:286
  34.7 1.0 %shard_map.79.refs_0_ = bf16[3,512,256]{2,1,0:T(8,128)(2,1)S(1)} custom-call(bf16[512,512]{1,0:T(8,128)(2,1)S(1)} %shard_map.73.refs_3_.refs_0_, bf16[512,512]{1,0:T(8,128)(2,1)S(1)} %shard_map.75.refs_1_, bf16[1024,256]{1,0:T(8,128)(2,1)S(1)} %copy-done.3, bf16[672,256]{1,0:T(8,128)(2,1)S(1)} %collective-permute-done.refs_3_, ...), custom_call_target="tpu_custom_call" | custom-call | flops 805306368 | bytes 2359296 | tf_op jit(solution)/shard_map/pallas_call | solution.py:191
  36.3 1.4 %shard_map.76 = (bf16[2,512,256]{2,1,0:T(8,128)(2,1)S(1)}, bf16[1,512,256]{2,1,0:T(8,128)(2,1)S(1)}) custom-call(bf16[512,512]{1,0:T(8,128)(2,1)S(1)} %shard_map.73.refs_3_.refs_0_, bf16[512,512]{1,0:T(8,128)(2,1)S(1)} %shard_map.75.refs_1_, bf16[672,256]{1,0:T(8,128)(2,1)S(1)} %collective-permute-done.1.refs_2_, ...), custom_call_target="tpu_custom_call" | custom-call | flops 536870912 | bytes 1572864 | tf_op jit(solution)/shard_map/pallas_call | solution.py:191
  37.7 1.3 %collective-permute-done.8.refs_6_ = bf16[512,256]{1,0:T(8,128)(2,1)S(1)} collective-permute-done((bf16[512,256]{1,0:T(8,128)(2,1)S(1)}, bf16[512,256]{1,0:T(8,128)(2,1)S(1)}, u32[]{:S(2)}, u32[]{:S(2)}) %collective-permute-start.8) | collective-permute-done | bytes 262176 | tf_op jit(solution)/shard_map/ppermute | solution.py:286
  39.1 1.4 %collective-permute-done.7.refs_5_ = bf16[512,256]{1,0:T(8,128)(2,1)S(1)} collective-permute-done((bf16[512,256]{1,0:T(8,128)(2,1)S(1)}, bf16[512,256]{1,0:T(8,128)(2,1)S(1)}, u32[]{:S(2)}, u32[]{:S(2)}) %collective-permute-start.7) | collective-permute-done | bytes 262176 | tf_op jit(solution)/shard_map/ppermute | solution.py:286
  40.4 0.7 %shard_map.78.refs_1_ = bf16[3,512,256]{2,1,0:T(8,128)(2,1)S(1)} custom-call(bf16[512,512]{1,0:T(8,128)(2,1)S(1)} %shard_map.73.refs_3_.refs_0_, bf16[512,512]{1,0:T(8,128)(2,1)S(1)} %shard_map.75.refs_1_, bf16[672,256]{1,0:T(8,128)(2,1)S(1)} %collective-permute-done.2.refs_2_, bf16[672,256]{1,0:T(8,128)(2,1)S(1)} %collective-permute-done.5.refs_3_, ...), custom_call_target="tpu_custom_call" | custom-call | flops 469762048 | bytes 1703936 | tf_op jit(solution)/shard_map/pallas_call | solution.py:191
  42.4 1.5 %shard_map.80.refs_4_ = bf16[2,256,1024]{2,1,0:T(8,128)(2,1)} custom-call(s32[1]{0:T(128)S(6)} %copy.10.counts_ref, s32[4]{0:T(128)S(1)} %copy-done.5, bf16[3,512,256]{2,1,0:T(8,128)(2,1)S(1)} %shard_map.79.refs_0_, bf16[3,512,256]{2,1,0:T(8,128)(2,1)S(1)} %collective-permute-done.13.refs_1_), custom_call_target="tpu_custom_call" | custom-call | flops 393216 | bytes 1179648 | tf_op jit(solution)/shard_map/pallas_call | solution.py:256
  43.9 1.4 %shard_map.81 = bf16[2,256,1024]{2,1,0:T(8,128)(2,1)} custom-call(s32[1]{0:T(128)S(6)} %copy.10.counts_ref, s32[4]{0:T(128)S(1)} %copy-done.5, bf16[2,512,256]{2,1,0:T(8,128)(2,1)S(1)} %get-tuple-element.33.refs_0_, bf16[3,512,256]{2,1,0:T(8,128)(2,1)S(1)} %shard_map.78.refs_1_, ...), custom_call_target="tpu_custom_call", output_to_operand_aliasing={{}: (6, {})} | custom-call | flops 655360 | bytes 1966080 | tf_op jit(solution)/shard_map/pallas_call | solution.py:256
  (37 shorter events, 3.0 us)
Async XLA Ops:
  0.0 4.3 %copy-start = (bf16[2,256,1024]{2,1,0:T(8,128)(2,1)S(1)}, bf16[2,256,1024]{2,1,0:T(8,128)(2,1)}, u32[]{:S(2)}) copy-start(bf16[2,256,1024]{2,1,0:T(8,128)(2,1)} %refs_0_.5) | copy-start | bytes 3145732
  0.0 4.3 %copy-start.4 = (f32[32,16]{0,1:T(8,128)S(1)}, f32[32,16]{0,1:T(8,128)}, u32[]{:S(2)}) copy-start(f32[32,16]{0,1:T(8,128)} %param.10) | copy-start | bytes 6148
  1.2 11.1 %collective-permute-start = (bf16[672,256]{1,0:T(8,128)(2,1)S(1)}, bf16[672,256]{1,0:T(8,128)(2,1)S(1)}, u32[]{:S(2)}, u32[]{:S(2)}) collective-permute-start(bf16[672,256]{1,0:T(8,128)(2,1)S(1)} %get-tuple-element.44), channel_id=1, source_target_pairs={{0,4},{1,5},{4,8},{5,9},{8,12},{9,13},{12,14},{13,15},{14,10},{15,... | collective-permute-start | bytes 1032200 | tf_op jit(solution)/shard_map/ppermute | solution.py:286
  4.3 9.8 %collective-permute-start.3 = (bf16[672,256]{1,0:T(8,128)(2,1)S(1)}, bf16[672,256]{1,0:T(8,128)(2,1)S(1)}, u32[]{:S(2)}, u32[]{:S(2)}) collective-permute-start(bf16[672,256]{1,0:T(8,128)(2,1)S(1)} %get-tuple-element.43), channel_id=1, source_target_pairs={{0,2},{1,3},{4,0},{5,1},{8,4},{9,5},{12,8},{13,9},{14,12},{15,13},... | collective-permute-start | bytes 1032200 | tf_op jit(solution)/shard_map/ppermute | solution.py:286
  4.3 1.2 %copy-start.1 = (bf16[2,256,1024]{2,1,0:T(8,128)(2,1)S(1)}, bf16[2,256,1024]{2,1,0:T(8,128)(2,1)}, u32[]{:S(2)}) copy-start(bf16[2,256,1024]{2,1,0:T(8,128)(2,1)} %refs_1_.5) | copy-start | bytes 3145732
  5.5 1.2 %copy-start.2 = (bf16[2,256,1024]{2,1,0:T(8,128)(2,1)S(1)}, bf16[2,256,1024]{2,1,0:T(8,128)(2,1)}, u32[]{:S(2)}) copy-start(bf16[2,256,1024]{2,1,0:T(8,128)(2,1)} %refs_2_.6) | copy-start | bytes 3145732
  12.3 9.2 %collective-permute-start.1 = (bf16[672,256]{1,0:T(8,128)(2,1)S(1)}, bf16[672,256]{1,0:T(8,128)(2,1)S(1)}, u32[]{:S(2)}, u32[]{:S(2)}) collective-permute-start(bf16[672,256]{1,0:T(8,128)(2,1)S(1)} %collective-permute-done.refs_3_), channel_id=1, source_target_pairs={{0,4},{1,5},{4,8},{5,9},{8,12},{9,13},{12,14},{13,15},{14,10},{15,... | collective-permute-start | bytes 1032200 | tf_op jit(solution)/shard_map/ppermute | solution.py:286
  14.1 8.7 %collective-permute-start.4 = (bf16[672,256]{1,0:T(8,128)(2,1)S(1)}, bf16[672,256]{1,0:T(8,128)(2,1)S(1)}, u32[]{:S(2)}, u32[]{:S(2)}) collective-permute-start(bf16[672,256]{1,0:T(8,128)(2,1)S(1)} %collective-permute-done.3.refs_4_), channel_id=1, source_target_pairs={{0,2},{1,3},{4,0},{5,1},{8,4},{9,5},{12,8},{13,9},{14,12},{15,13},... | collective-permute-start | bytes 1032200 | tf_op jit(solution)/shard_map/ppermute | solution.py:286
  14.4 14.6 %collective-permute-start.6 = (bf16[704,256]{1,0:T(8,128)(2,1)S(1)}, bf16[704,256]{1,0:T(8,128)(2,1)S(1)}, u32[]{:S(2)}, u32[]{:S(2)}) collective-permute-start(bf16[704,256]{1,0:T(8,128)(2,1)S(1)} %pad_maximum_fusion), channel_id=1, source_target_pairs={{0,16},{1,17},{2,18},{3,19},{4,20},{5,21},{6,22},{7,23},{8,24},{9,... | collective-permute-start | bytes 1081352 | tf_op jit(solution)/shard_map/ppermute | solution.py:286
  22.8 7.8 %collective-permute-start.5 = (bf16[672,256]{1,0:T(8,128)(2,1)S(1)}, bf16[672,256]{1,0:T(8,128)(2,1)S(1)}, u32[]{:S(2)}, u32[]{:S(2)}) collective-permute-start(bf16[672,256]{1,0:T(8,128)(2,1)S(1)} %collective-permute-done.4.refs_3_), channel_id=1, source_target_pairs={{0,2},{1,3},{4,0},{5,1},{8,4},{9,5},{12,8},{13,9},{14,12},{15,13},... | collective-permute-start | bytes 1032200 | tf_op jit(solution)/shard_map/ppermute | solution.py:286
  23.3 7.8 %collective-permute-start.2 = (bf16[672,256]{1,0:T(8,128)(2,1)S(1)}, bf16[672,256]{1,0:T(8,128)(2,1)S(1)}, u32[]{:S(2)}, u32[]{:S(2)}) collective-permute-start(bf16[672,256]{1,0:T(8,128)(2,1)S(1)} %collective-permute-done.1.refs_2_), channel_id=1, source_target_pairs={{0,4},{1,5},{4,8},{5,9},{8,12},{9,13},{12,14},{13,15},{14,10},{15,... | collective-permute-start | bytes 1032200 | tf_op jit(solution)/shard_map/ppermute | solution.py:286
  24.9 11.4 %collective-permute-start.10 = (bf16[704,256]{1,0:T(8,128)(2,1)S(1)}, bf16[704,256]{1,0:T(8,128)(2,1)S(1)}, u32[]{:S(2)}, u32[]{:S(2)}) collective-permute-start(bf16[704,256]{1,0:T(8,128)(2,1)S(1)} %pad_maximum_fusion.2), channel_id=1, source_target_pairs={{0,16},{1,17},{2,18},{3,19},{4,20},{5,21},{6,22},{7,23},{8,24},{9,... | collective-permute-start | bytes 1081352 | tf_op jit(solution)/shard_map/ppermute | solution.py:286
  31.1 3.6 %copy-start.3 = (bf16[1024,256]{1,0:T(8,128)(2,1)S(1)}, bf16[1024,256]{1,0:T(8,128)(2,1)}, u32[]{:S(2)}) copy-start(bf16[1024,256]{1,0:T(8,128)(2,1)} %refs_2_.7) | copy-start | bytes 1572868
  31.1 9.3 %collective-permute-start.9 = (bf16[704,256]{1,0:T(8,128)(2,1)S(1)}, bf16[704,256]{1,0:T(8,128)(2,1)S(1)}, u32[]{:S(2)}, u32[]{:S(2)}) collective-permute-start(bf16[704,256]{1,0:T(8,128)(2,1)S(1)} %pad_maximum_fusion.1), channel_id=1, source_target_pairs={{0,16},{1,17},{2,18},{3,19},{4,20},{5,21},{6,22},{7,23},{8,24},{9,... | collective-permute-start | bytes 1081352 | tf_op jit(solution)/shard_map/ppermute | solution.py:286
  32.6 6.4 %collective-permute-start.8 = (bf16[512,256]{1,0:T(8,128)(2,1)S(1)}, bf16[512,256]{1,0:T(8,128)(2,1)S(1)}, u32[]{:S(2)}, u32[]{:S(2)}) collective-permute-start(bf16[512,256]{1,0:T(8,128)(2,1)S(1)} %slice.35), channel_id=1, source_target_pairs={{0,2},{1,3},{4,0},{5,1},{8,4},{9,5},{12,8},{13,9},{14,12},{15,13},... | collective-permute-start | bytes 786440 | tf_op jit(solution)/shard_map/ppermute | solution.py:286
  34.1 6.4 %collective-permute-start.7 = (bf16[512,256]{1,0:T(8,128)(2,1)S(1)}, bf16[512,256]{1,0:T(8,128)(2,1)S(1)}, u32[]{:S(2)}, u32[]{:S(2)}) collective-permute-start(bf16[512,256]{1,0:T(8,128)(2,1)S(1)} %slice.34), channel_id=1, source_target_pairs={{0,4},{1,5},{4,8},{5,9},{8,12},{9,13},{12,14},{13,15},{14,10},{15,... | collective-permute-start | bytes 786440 | tf_op jit(solution)/shard_map/ppermute | solution.py:286
  35.7 6.7 %collective-permute-start.13 = (bf16[3,512,256]{2,1,0:T(8,128)(2,1)S(1)}, bf16[3,512,256]{2,1,0:T(8,128)(2,1)S(1)}, u32[]{:S(2)}, u32[]{:S(2)}) collective-permute-start(bf16[3,512,256]{2,1,0:T(8,128)(2,1)S(1)} %shard_map.79.refs_0_), channel_id=1, source_target_pairs={{0,1},{1,0},{2,3},{3,2},{4,5},{5,4},{6,7},{7,6},{8,9},{9,8},{10,11... | collective-permute-start | bytes 2359304 | tf_op jit(solution)/shard_map/ppermute | solution.py:286
  41.2 1.3 %copy-start.5 = (s32[4]{0:T(128)S(1)}, s32[4]{0:T(128)}, u32[]{:S(2)}) copy-start(s32[4]{0:T(128)} %donors_ref.3) | copy-start | bytes 52
  41.2 2.8 %collective-permute-start.12 = (bf16[3,512,256]{2,1,0:T(8,128)(2,1)S(1)}, bf16[3,512,256]{2,1,0:T(8,128)(2,1)S(1)}, u32[]{:S(2)}, u32[]{:S(2)}) collective-permute-start(bf16[3,512,256]{2,1,0:T(8,128)(2,1)S(1)} %shard_map.78.refs_1_), channel_id=1, source_target_pairs={{0,1},{1,0},{2,3},{3,2},{4,5},{5,4},{6,7},{7,6},{8,9},{9,8},{10,11... | collective-permute-start | bytes 2359304 | tf_op jit(solution)/shard_map/ppermute | solution.py:286
  41.2 2.7 %collective-permute-start.11 = (bf16[1,512,256]{2,1,0:T(8,128)(2,1)S(1)}, bf16[1,512,256]{2,1,0:T(8,128)(2,1)S(1)}, u32[]{:S(2)}, u32[]{:S(2)}) collective-permute-start(bf16[1,512,256]{2,1,0:T(8,128)(2,1)S(1)} %get-tuple-element.38), channel_id=1, source_target_pairs={{0,1},{1,0},{2,3},{3,2},{4,5},{5,4},{6,7},{7,6},{8,9},{9,8},{10,11... | collective-permute-start | bytes 786440 | tf_op jit(solution)/shard_map/ppermute | solution.py:286

commit v7 on v6

--- a/solution.py
+++ b/solution.py
@@ -10,6 +10,7 @@
 HEAD_DIM = 64
 PAIR = 2 * HEAD_DIM
 CHUNK = 256
+LIVE_ROWS = 16
 THRESHOLDS = (12, 16, 23, 32, 46, 64, 91)
 AXES = ("rep", "dp", "tensor")
 
@@ -205,62 +206,82 @@
     )(*context, *weights, *bases)
 
 
-def finish_kernel(distances, counts_ref, donors_ref, *refs):
+def live_kernel(counts_ref, donors_ref, after_ref, out_ref):
+    my_group = lax.axis_index("dp")
+    second = donors_ref[0] == my_group
+    for at in range(1, donors_ref.shape[0]):
+        second = jnp.logical_or(second, donors_ref[at] == my_group)
+    for slot, lives in enumerate((counts_ref[0] >= 1, second)):
+        rows = jnp.full((LIVE_ROWS, CHUNK), jnp.where(lives, 1.0, 0.0), jnp.float32)
+        out_ref[slot * LIVE_ROWS : (slot + 1) * LIVE_ROWS] = rows.astype(jnp.bfloat16)
+
+
+def live_slots(counts, donors, after):
+    smem = pl.BlockSpec(memory_space=pltpu.SMEM)
+    return pl.pallas_call(
+        live_kernel,
+        out_shape=jax.ShapeDtypeStruct((2 * LIVE_ROWS, CHUNK), jnp.bfloat16),
+        in_specs=[smem, smem, pl.BlockSpec(memory_space=pl.ANY)],
+        out_specs=pl.BlockSpec(memory_space=pltpu.VMEM),
+        compiler_params=pltpu.CompilerParams(vmem_limit_bytes=4 << 20),
+    )(counts, donors, after)
+
+
+def finish_kernel(distances, live_ref, *refs):
     n = len(distances)
     kept, other = refs[:n], refs[n : 2 * n]
     out_ref, buffer, sem = refs[-3:]
     slots, tokens = out_ref.shape[:2]
-    my_group, tensor = lax.axis_index("dp"), lax.axis_index("tensor")
-    second = donors_ref[0] == my_group
-    for at in range(1, donors_ref.shape[0]):
-        second = jnp.logical_or(second, donors_ref[at] == my_group)
-    live = [
-        jnp.where(lives, 1.0, 0.0).astype(jnp.bfloat16) for lives in (counts_ref[0] >= 1, second)
-    ]
-    at = 0
+    tensor = lax.axis_index("tensor")
     steps = []
     for array, group in enumerate(distances):
         several = other[array].shape[0] > 1
         for slot, distance in enumerate(group):
+            at = len(steps)
             block = block_of(distance)
             column = pl.multiple_of(block % 4 * CHUNK, CHUNK)
-            copy = pltpu.make_async_copy(
-                buffer.at[at], out_ref.at[:, :, pl.ds(column, CHUNK)], sem.at[at]
-            )
-            steps.append((block // 4 == tensor, copy))
+            copies = [
+                pltpu.make_async_copy(
+                    buffer.at[at, passage],
+                    out_ref.at[passage, :, pl.ds(column, CHUNK)],
+                    sem.at[at, passage],
+                )
+                for passage in range(slots)
+            ]
+            steps.append((block // 4 == tensor, copies))
 
             @pl.when(block // 4 == tensor)
             def _():
                 for passage in range(slots):
                     rows = slice(passage * tokens, (passage + 1) * tokens)
                     both = kept[array][slot, rows] + other[array][slot if several else 0, rows]
-                    buffer[at, passage] = both * live[passage]
-                copy.start()
-
-            at += 1
-    for mine, copy in steps:
+                    live = live_ref[passage * LIVE_ROWS : passage * LIVE_ROWS + 1]
+                    buffer[at, passage] = both * jnp.broadcast_to(live, both.shape)
+                    copies[passage].start()
+
+    for mine, copies in steps:
 
         @pl.when(mine)
         def _():
-            copy.wait()
-
-
-def finish(kept, other, distances, counts, donors, slots, held=()):
+            for copy in copies:
+                copy.wait()
+
+
+def finish(kept, other, distances, live, slots, held=()):
     rows = kept[0].shape[1]
     tokens = rows // slots
-    smem = pl.BlockSpec(memory_space=pltpu.SMEM)
     vmem = pl.BlockSpec(memory_space=pltpu.VMEM)
     away = pl.BlockSpec(memory_space=pl.ANY)
     blocks = sum(len(group) for group in distances)
-    n_in = 2 + 2 * len(kept)
+    n_in = 1 + 2 * len(kept)
     return pl.pallas_call(
         functools.partial(finish_kernel, distances),
         out_shape=jax.ShapeDtypeStruct((slots, tokens, 4 * CHUNK), jnp.bfloat16),
-        in_specs=[smem, smem] + [vmem] * (n_in - 2) + [away] * len(held),
+        in_specs=[vmem] * n_in + [away] * len(held),
         out_specs=away,
         scratch_shapes=[
             pltpu.VMEM((blocks, slots, tokens, CHUNK), jnp.bfloat16),
-            pltpu.SemaphoreType.DMA((blocks,)),
+            pltpu.SemaphoreType.DMA((blocks, slots)),
         ],
         input_output_aliases={n_in: 0} if held else {},
         compiler_params=pltpu.CompilerParams(vmem_limit_bytes=12 << 20),
@@ -269,7 +290,7 @@
             bytes_accessed=blocks * rows * CHUNK * 3,
             transcendentals=0,
         ),
-    )(counts, donors, *kept, *other, *held)
+    )(live, *kept, *other, *held)
 
 
 def with_ring(queries, key_rows, values, position_bias, out_weight, counts, donors, reps, dp_size):
@@ -298,7 +319,8 @@
 
     p2, q2, y1 = send(p1, ahead), send(q1, back), send(edge(p1, q1), across)
     c1 = attend(queries, key_rows, values, position_bias, 2, 1, (c0,))
-    p2, c1 = barrier((p2, c1))
+    live = live_slots(counts, donors, c0)
+    p2, c1, live = barrier((p2, c1, live))
 
     p3, q3, y2 = send(p2, ahead), send(q2, back), send(edge(p2, q2), across)
     c1 = attend(queries, key_rows, values, position_bias, 3, 1, (c1,), joined=True)
@@ -330,9 +352,9 @@
         context, (p3, q3, y3, p4, q4), [p_rest, q_rest, opposite], jnp.bfloat16, (started,)
     )
     x3 = send(e3, cores)
-    early = finish((e1,), (x1,), ((0, 1, -1),), counts, donors, slots)
+    early = finish((e1,), (x1,), ((0, 1, -1),), live, slots)
     x2, x3, early = barrier((x2, x3, early))
-    return finish((e2, e3), (x2, x3), ((2, -2), (3, -3, 4)), counts, donors, slots, (early,))
+    return finish((e2, e3), (x2, x3), ((2, -2), (3, -3, 4)), live, slots, (early,))
 
 
 def with_gather(queries, key_rows, values, position_bias, out_weight, counts, donors):

time: 45.5 us -> 44.9 us (0.987)
  Pallas kernels: 16.6 us -> 16.1 us
    pallas_call x2, Pallas kernels: 2.86 us -> 1.74 us  [finish(): pl.pallas_call(functools.partial(finish_kernel, distances), out_shape=jax...]
    pallas_call x0 -> x1, Pallas kernels: none -> 0.56 us  [live_slots(): pl.pallas_call(live_kernel, out_shape=jax.ShapeDtypeStruct((2 * LIVE_ROWS...]
  transfers between devices with their start and end apart: 14 -> 14, of which waited for: 7 -> 8; matrix products, arithmetic and copies ran while one was open for 0% -> 0% of each run, Pallas kernels for 34% -> 34%
where the time goes in v7:
time: 44.9 us; the launch traced here: 44.7 us
  Pallas kernels  16.1 us (36%)
  starting transfers between devices  14.6 us (33%)
  waiting for transfers between devices  9.25 us (21%)
  local copies, waits for them, and re-layouts  3.8 us (8%)
  between operations  0.87 us (2%)
    ppermute x14, starting transfers between devices, with_ring(): send = lambda value, pairs: lax.ppermute(value, AXES, pairs)  14.6 us
    pallas_call x3, Pallas kernels, attend(): pl.pallas_call(functools.partial(attention_kernel, first, joined), out_sh...  10.1 us
    ppermute x14, waiting for transfers between devices, with_ring(): send = lambda value, pairs: lax.ppermute(value, AXES, pairs)  9.25 us
    pallas_call x4, Pallas kernels, project(): pl.pallas_call(functools.partial(project_kernel, plan, len(context), len(...  3.62 us
    unnamed x12, local copies, waits for them, and re-layouts  2.46 us
    pallas_call x2, Pallas kernels, finish(): pl.pallas_call(functools.partial(finish_kernel, distances), out_shape=jax...  1.74 us
    slice x1, local copies, waits for them, and re-layouts, with_ring(): p1, q1 = (send(out_weight[:-cut], ahead), send(out_weight[cut:], back))  1.22 us
  transfers between devices with their start and end apart: 14, of which 8 were waited for; matrix products, arithmetic and copies ran while one was open for 0% of the time, Pallas kernels for 34%

profile of v7, /device:TPU:0, one launch (start us, length us, event | category | flops | bytes accessed | tf_op | source)
XLA Modules:
  0.0 44.7 jit_solution(3807708262069159327)
XLA Ops:
  0.0 1.2 %fusion = (bf16[672,256]{1,0:T(8,128)(2,1)S(1)}, bf16[672,256]{1,0:T(8,128)(2,1)S(1)}) fusion(bf16[1024,256]{1,0:T(8,128)(2,1)} %refs_2_.7), kind=kLoop, calls=%fused_computation.3 | loop fusion | bytes 1376256 | tf_op jit(solution)/shard_map/slice | solution.py:316
  1.2 3.1 %collective-permute-start = (bf16[672,256]{1,0:T(8,128)(2,1)S(1)}, bf16[672,256]{1,0:T(8,128)(2,1)S(1)}, u32[]{:S(2)}, u32[]{:S(2)}) collective-permute-start(bf16[672,256]{1,0:T(8,128)(2,1)S(1)} %get-tuple-element.46), channel_id=1, source_target_pairs={{0,4},{1,5},{4,8},{5,9},{8,12},{9,13},{12,14},{13,15},{14,10},{15,... | collective-permute-start | bytes 1032200 | tf_op jit(solution)/shard_map/ppermute | solution.py:307
  4.3 1.2 %copy-done.1 = bf16[2,256,1024]{2,1,0:T(8,128)(2,1)S(1)} copy-done((bf16[2,256,1024]{2,1,0:T(8,128)(2,1)S(1)}, bf16[2,256,1024]{2,1,0:T(8,128)(2,1)}, u32[]{:S(2)}) %copy-start.1) | copy-done | bytes 1048600
  5.5 1.2 %copy-done.2 = bf16[2,256,1024]{2,1,0:T(8,128)(2,1)S(1)} copy-done((bf16[2,256,1024]{2,1,0:T(8,128)(2,1)S(1)}, bf16[2,256,1024]{2,1,0:T(8,128)(2,1)}, u32[]{:S(2)}) %copy-start.2) | copy-done | bytes 1048600
  6.8 5.0 %shard_map.73.refs_3_.after_ref.refs_0_ = bf16[512,512]{1,0:T(8,128)(2,1)S(1)} custom-call(f32[16,32]{1,0:T(8,128)S(1)} %bitcast.1, bf16[2,256,1024]{2,1,0:T(8,128)(2,1)S(1)} %copy-done, bf16[2,256,1024]{2,1,0:T(8,128)(2,1)S(1)} %copy-done.1, bf16[2,256,1024]{2,1,0:T(8,128)(2,1)S(1)} %copy-done.2), custom_call_target="tpu_custom_call" | custom-call | flops 268435456 | bytes 2097152 | tf_op jit(solution)/shard_map/pallas_call | solution.py:112
  12.3 1.8 %collective-permute-start.1 = (bf16[672,256]{1,0:T(8,128)(2,1)S(1)}, bf16[672,256]{1,0:T(8,128)(2,1)S(1)}, u32[]{:S(2)}, u32[]{:S(2)}) collective-permute-start(bf16[672,256]{1,0:T(8,128)(2,1)S(1)} %collective-permute-done.refs_3_), channel_id=1, source_target_pairs={{0,4},{1,5},{4,8},{5,9},{8,12},{9,13},{12,14},{13,15},{14,10},{15,... | collective-permute-start | bytes 1032200 | tf_op jit(solution)/shard_map/ppermute | solution.py:307
  14.4 1.8 %collective-permute-start.6 = (bf16[704,256]{1,0:T(8,128)(2,1)S(1)}, bf16[704,256]{1,0:T(8,128)(2,1)S(1)}, u32[]{:S(2)}, u32[]{:S(2)}) collective-permute-start(bf16[704,256]{1,0:T(8,128)(2,1)S(1)} %pad_maximum_fusion), channel_id=1, source_target_pairs={{0,16},{1,17},{2,18},{3,19},{4,20},{5,21},{6,22},{7,23},{8,24},{9,... | collective-permute-start | bytes 1081352 | tf_op jit(solution)/shard_map/ppermute | solution.py:307
  17.4 2.6 %shard_map.74.refs_3_ = bf16[512,256]{1,0:T(8,128)(2,1)S(1)} custom-call(f32[16,32]{1,0:T(8,128)S(1)} %bitcast.2, bf16[2,256,1024]{2,1,0:T(8,128)(2,1)S(1)} %copy-done, bf16[2,256,1024]{2,1,0:T(8,128)(2,1)S(1)} %copy-done.1, bf16[2,256,1024]{2,1,0:T(8,128)(2,1)S(1)} %copy-done.2, bf16[512,512]{1,0:T(8,128)(2,1)S(1)} %shard_map.73.refs_3_.after_ref.refs_0_), custom_call_target="tpu_custom_call" | custom-call | flops 134217728 | bytes 1048576 | tf_op jit(solution)/shard_map/pallas_call | solution.py:112
  20.0 1.5 %collective-permute-done.1.refs_2_ = bf16[672,256]{1,0:T(8,128)(2,1)S(1)} collective-permute-done((bf16[672,256]{1,0:T(8,128)(2,1)S(1)}, bf16[672,256]{1,0:T(8,128)(2,1)S(1)}, u32[]{:S(2)}, u32[]{:S(2)}) %collective-permute-start.1) | collective-permute-done | bytes 344096 | tf_op jit(solution)/shard_map/ppermute | solution.py:307
  21.5 1.3 %collective-permute-done.4.refs_3_ = bf16[672,256]{1,0:T(8,128)(2,1)S(1)} collective-permute-done((bf16[672,256]{1,0:T(8,128)(2,1)S(1)}, bf16[672,256]{1,0:T(8,128)(2,1)S(1)}, u32[]{:S(2)}, u32[]{:S(2)}) %collective-permute-start.4) | collective-permute-done | bytes 344096 | tf_op jit(solution)/shard_map/ppermute | solution.py:307
  23.3 1.6 %collective-permute-start.2 = (bf16[672,256]{1,0:T(8,128)(2,1)S(1)}, bf16[672,256]{1,0:T(8,128)(2,1)S(1)}, u32[]{:S(2)}, u32[]{:S(2)}) collective-permute-start(bf16[672,256]{1,0:T(8,128)(2,1)S(1)} %collective-permute-done.1.refs_2_), channel_id=1, source_target_pairs={{0,4},{1,5},{4,8},{5,9},{8,12},{9,13},{12,14},{13,15},{14,10},{15,... | collective-permute-start | bytes 1032200 | tf_op jit(solution)/shard_map/ppermute | solution.py:307
  24.9 1.5 %collective-permute-start.10 = (bf16[704,256]{1,0:T(8,128)(2,1)S(1)}, bf16[704,256]{1,0:T(8,128)(2,1)S(1)}, u32[]{:S(2)}, u32[]{:S(2)}) collective-permute-start(bf16[704,256]{1,0:T(8,128)(2,1)S(1)} %pad_maximum_fusion.2), channel_id=1, source_target_pairs={{0,16},{1,17},{2,18},{3,19},{4,20},{5,21},{6,22},{7,23},{8,24},{9,... | collective-permute-start | bytes 1081352 | tf_op jit(solution)/shard_map/ppermute | solution.py:307
  26.4 2.6 %shard_map.76.refs_1_ = bf16[512,512]{1,0:T(8,128)(2,1)S(1)} custom-call(f32[16,32]{1,0:T(8,128)S(1)} %bitcast.3, bf16[2,256,1024]{2,1,0:T(8,128)(2,1)S(1)} %copy-done, bf16[2,256,1024]{2,1,0:T(8,128)(2,1)S(1)} %copy-done.1, bf16[2,256,1024]{2,1,0:T(8,128)(2,1)S(1)} %copy-done.2, bf16[512,256]{1,0:T(8,128)(2,1)S(1)} %shard_map.74.refs_3_), custom_call_target="tpu_custom_call" | custom-call | flops 134217728 | bytes 1048576 | tf_op jit(solution)/shard_map/pallas_call | solution.py:112
  29.0 1.6 %collective-permute-done.5.refs_3_ = bf16[672,256]{1,0:T(8,128)(2,1)S(1)} collective-permute-done((bf16[672,256]{1,0:T(8,128)(2,1)S(1)}, bf16[672,256]{1,0:T(8,128)(2,1)S(1)}, u32[]{:S(2)}, u32[]{:S(2)}) %collective-permute-start.5) | collective-permute-done | bytes 344096 | tf_op jit(solution)/shard_map/ppermute | solution.py:307
  31.1 1.5 %collective-permute-start.9 = (bf16[704,256]{1,0:T(8,128)(2,1)S(1)}, bf16[704,256]{1,0:T(8,128)(2,1)S(1)}, u32[]{:S(2)}, u32[]{:S(2)}) collective-permute-start(bf16[704,256]{1,0:T(8,128)(2,1)S(1)} %pad_maximum_fusion.1), channel_id=1, source_target_pairs={{0,16},{1,17},{2,18},{3,19},{4,20},{5,21},{6,22},{7,23},{8,24},{9,... | collective-permute-start | bytes 1081352 | tf_op jit(solution)/shard_map/ppermute | solution.py:307
  32.6 1.4 %collective-permute-start.8 = (bf16[512,256]{1,0:T(8,128)(2,1)S(1)}, bf16[512,256]{1,0:T(8,128)(2,1)S(1)}, u32[]{:S(2)}, u32[]{:S(2)}) collective-permute-start(bf16[512,256]{1,0:T(8,128)(2,1)S(1)} %slice.35), channel_id=1, source_target_pairs={{0,2},{1,3},{4,0},{5,1},{8,4},{9,5},{12,8},{13,9},{14,12},{15,13},... | collective-permute-start | bytes 786440 | tf_op jit(solution)/shard_map/ppermute | solution.py:307
  34.7 1.0 %shard_map.80.refs_0_ = bf16[3,512,256]{2,1,0:T(8,128)(2,1)S(1)} custom-call(bf16[512,512]{1,0:T(8,128)(2,1)S(1)} %shard_map.73.refs_3_.after_ref.refs_0_, bf16[512,512]{1,0:T(8,128)(2,1)S(1)} %shard_map.76.refs_1_, bf16[1024,256]{1,0:T(8,128)(2,1)S(1)} %copy-done.3, bf16[672,256]{1,0:T(8,128)(2,1)S(1)} %collective-permute-done.refs_3_, ...), custom_call_target="tpu_custom_call" | custom-call | flops 805306368 | bytes 2359296 | tf_op jit(solution)/shard_map/pallas_call | solution.py:192
  36.3 1.4 %shard_map.77 = (bf16[2,512,256]{2,1,0:T(8,128)(2,1)S(1)}, bf16[1,512,256]{2,1,0:T(8,128)(2,1)S(1)}) custom-call(bf16[512,512]{1,0:T(8,128)(2,1)S(1)} %shard_map.73.refs_3_.after_ref.refs_0_, bf16[512,512]{1,0:T(8,128)(2,1)S(1)} %shard_map.76.refs_1_, bf16[672,256]{1,0:T(8,128)(2,1)S(1)} %collective-permute-done.1.refs_2_, ...), custom_call_target="tpu_custom_call" | custom-call | flops 536870912 | bytes 1572864 | tf_op jit(solution)/shard_map/pallas_call | solution.py:192
  37.7 1.3 %collective-permute-done.8.refs_6_ = bf16[512,256]{1,0:T(8,128)(2,1)S(1)} collective-permute-done((bf16[512,256]{1,0:T(8,128)(2,1)S(1)}, bf16[512,256]{1,0:T(8,128)(2,1)S(1)}, u32[]{:S(2)}, u32[]{:S(2)}) %collective-permute-start.8) | collective-permute-done | bytes 262176 | tf_op jit(solution)/shard_map/ppermute | solution.py:307
  39.1 1.4 %collective-permute-done.7.refs_5_ = bf16[512,256]{1,0:T(8,128)(2,1)S(1)} collective-permute-done((bf16[512,256]{1,0:T(8,128)(2,1)S(1)}, bf16[512,256]{1,0:T(8,128)(2,1)S(1)}, u32[]{:S(2)}, u32[]{:S(2)}) %collective-permute-start.7) | collective-permute-done | bytes 262176 | tf_op jit(solution)/shard_map/ppermute | solution.py:307
  40.4 0.7 %shard_map.79.refs_1_ = bf16[3,512,256]{2,1,0:T(8,128)(2,1)S(1)} custom-call(bf16[512,512]{1,0:T(8,128)(2,1)S(1)} %shard_map.73.refs_3_.after_ref.refs_0_, bf16[512,512]{1,0:T(8,128)(2,1)S(1)} %shard_map.76.refs_1_, bf16[672,256]{1,0:T(8,128)(2,1)S(1)} %collective-permute-done.2.refs_2_, bf16[672,256]{1,0:T(8,128)(2,1)S(1)} %collective-permute-done.5.refs_3_, ...), custom_call_target="tpu_custom_call" | custom-call | flops 469762048 | bytes 1703936 | tf_op jit(solution)/shard_map/pallas_call | solution.py:192
  41.7 0.9 %shard_map.81.refs_4_ = bf16[2,256,1024]{2,1,0:T(8,128)(2,1)} custom-call(bf16[32,256]{1,0:T(8,128)(2,1)S(1)} %shard_map.75.live_ref, bf16[3,512,256]{2,1,0:T(8,128)(2,1)S(1)} %shard_map.80.refs_0_, bf16[3,512,256]{2,1,0:T(8,128)(2,1)S(1)} %collective-permute-done.13.refs_1_), custom_call_target="tpu_custom_call" | custom-call | flops 393216 | bytes 1179648 | tf_op jit(solution)/shard_map/pallas_call | solution.py:277
  42.7 1.2 %collective-permute-done.11.refs_2_ = bf16[1,512,256]{2,1,0:T(8,128)(2,1)S(1)} collective-permute-done((bf16[1,512,256]{2,1,0:T(8,128)(2,1)S(1)}, bf16[1,512,256]{2,1,0:T(8,128)(2,1)S(1)}, u32[]{:S(2)}, u32[]{:S(2)}) %collective-permute-start.11) | collective-permute-done | bytes 262176 | tf_op jit(solution)/shard_map/ppermute | solution.py:307
  43.9 0.8 %shard_map.82 = bf16[2,256,1024]{2,1,0:T(8,128)(2,1)} custom-call(bf16[32,256]{1,0:T(8,128)(2,1)S(1)} %shard_map.75.live_ref, bf16[2,512,256]{2,1,0:T(8,128)(2,1)S(1)} %get-tuple-element.35.refs_0_, bf16[3,512,256]{2,1,0:T(8,128)(2,1)S(1)} %shard_map.79.refs_1_, ...), custom_call_target="tpu_custom_call", output_to_operand_aliasing={{}: (5, {})} | custom-call | flops 655360 | bytes 1966080 | tf_op jit(solution)/shard_map/pallas_call | solution.py:277
  (38 shorter events, 4.2 us)
Async XLA Ops:
  0.0 4.3 %copy-start = (bf16[2,256,1024]{2,1,0:T(8,128)(2,1)S(1)}, bf16[2,256,1024]{2,1,0:T(8,128)(2,1)}, u32[]{:S(2)}) copy-start(bf16[2,256,1024]{2,1,0:T(8,128)(2,1)} %refs_0_.5) | copy-start | bytes 3145732
  0.0 4.3 %copy-start.4 = (f32[32,16]{0,1:T(8,128)S(1)}, f32[32,16]{0,1:T(8,128)}, u32[]{:S(2)}) copy-start(f32[32,16]{0,1:T(8,128)} %param.10) | copy-start | bytes 6148
  1.2 11.1 %collective-permute-start = (bf16[672,256]{1,0:T(8,128)(2,1)S(1)}, bf16[672,256]{1,0:T(8,128)(2,1)S(1)}, u32[]{:S(2)}, u32[]{:S(2)}) collective-permute-start(bf16[672,256]{1,0:T(8,128)(2,1)S(1)} %get-tuple-element.46), channel_id=1, source_target_pairs={{0,4},{1,5},{4,8},{5,9},{8,12},{9,13},{12,14},{13,15},{14,10},{15,... | collective-permute-start | bytes 1032200 | tf_op jit(solution)/shard_map/ppermute | solution.py:307
  4.3 9.8 %collective-permute-start.3 = (bf16[672,256]{1,0:T(8,128)(2,1)S(1)}, bf16[672,256]{1,0:T(8,128)(2,1)S(1)}, u32[]{:S(2)}, u32[]{:S(2)}) collective-permute-start(bf16[672,256]{1,0:T(8,128)(2,1)S(1)} %get-tuple-element.45), channel_id=1, source_target_pairs={{0,2},{1,3},{4,0},{5,1},{8,4},{9,5},{12,8},{13,9},{14,12},{15,13},... | collective-permute-start | bytes 1032200 | tf_op jit(solution)/shard_map/ppermute | solution.py:307
  4.3 1.2 %copy-start.1 = (bf16[2,256,1024]{2,1,0:T(8,128)(2,1)S(1)}, bf16[2,256,1024]{2,1,0:T(8,128)(2,1)}, u32[]{:S(2)}) copy-start(bf16[2,256,1024]{2,1,0:T(8,128)(2,1)} %refs_1_.5) | copy-start | bytes 3145732
  5.5 1.2 %copy-start.2 = (bf16[2,256,1024]{2,1,0:T(8,128)(2,1)S(1)}, bf16[2,256,1024]{2,1,0:T(8,128)(2,1)}, u32[]{:S(2)}) copy-start(bf16[2,256,1024]{2,1,0:T(8,128)(2,1)} %refs_2_.6) | copy-start | bytes 3145732
  12.3 9.2 %collective-permute-start.1 = (bf16[672,256]{1,0:T(8,128)(2,1)S(1)}, bf16[672,256]{1,0:T(8,128)(2,1)S(1)}, u32[]{:S(2)}, u32[]{:S(2)}) collective-permute-start(bf16[672,256]{1,0:T(8,128)(2,1)S(1)} %collective-permute-done.refs_3_), channel_id=1, source_target_pairs={{0,4},{1,5},{4,8},{5,9},{8,12},{9,13},{12,14},{13,15},{14,10},{15,... | collective-permute-start | bytes 1032200 | tf_op jit(solution)/shard_map/ppermute | solution.py:307
  14.1 8.7 %collective-permute-start.4 = (bf16[672,256]{1,0:T(8,128)(2,1)S(1)}, bf16[672,256]{1,0:T(8,128)(2,1)S(1)}, u32[]{:S(2)}, u32[]{:S(2)}) collective-permute-start(bf16[672,256]{1,0:T(8,128)(2,1)S(1)} %collective-permute-done.3.refs_4_), channel_id=1, source_target_pairs={{0,2},{1,3},{4,0},{5,1},{8,4},{9,5},{12,8},{13,9},{14,12},{15,13},... | collective-permute-start | bytes 1032200 | tf_op jit(solution)/shard_map/ppermute | solution.py:307
  14.4 2.5 %copy-start.5 = (s32[4]{0:T(128)S(1)}, s32[4]{0:T(128)}, u32[]{:S(2)}) copy-start(s32[4]{0:T(128)} %donors_ref.1) | copy-start | bytes 52
  14.4 14.6 %collective-permute-start.6 = (bf16[704,256]{1,0:T(8,128)(2,1)S(1)}, bf16[704,256]{1,0:T(8,128)(2,1)S(1)}, u32[]{:S(2)}, u32[]{:S(2)}) collective-permute-start(bf16[704,256]{1,0:T(8,128)(2,1)S(1)} %pad_maximum_fusion), channel_id=1, source_target_pairs={{0,16},{1,17},{2,18},{3,19},{4,20},{5,21},{6,22},{7,23},{8,24},{9,... | collective-permute-start | bytes 1081352 | tf_op jit(solution)/shard_map/ppermute | solution.py:307
  22.8 7.8 %collective-permute-start.5 = (bf16[672,256]{1,0:T(8,128)(2,1)S(1)}, bf16[672,256]{1,0:T(8,128)(2,1)S(1)}, u32[]{:S(2)}, u32[]{:S(2)}) collective-permute-start(bf16[672,256]{1,0:T(8,128)(2,1)S(1)} %collective-permute-done.4.refs_3_), channel_id=1, source_target_pairs={{0,2},{1,3},{4,0},{5,1},{8,4},{9,5},{12,8},{13,9},{14,12},{15,13},... | collective-permute-start | bytes 1032200 | tf_op jit(solution)/shard_map/ppermute | solution.py:307
  23.3 7.8 %collective-permute-start.2 = (bf16[672,256]{1,0:T(8,128)(2,1)S(1)}, bf16[672,256]{1,0:T(8,128)(2,1)S(1)}, u32[]{:S(2)}, u32[]{:S(2)}) collective-permute-start(bf16[672,256]{1,0:T(8,128)(2,1)S(1)} %collective-permute-done.1.refs_2_), channel_id=1, source_target_pairs={{0,4},{1,5},{4,8},{5,9},{8,12},{9,13},{12,14},{13,15},{14,10},{15,... | collective-permute-start | bytes 1032200 | tf_op jit(solution)/shard_map/ppermute | solution.py:307
  24.9 11.4 %collective-permute-start.10 = (bf16[704,256]{1,0:T(8,128)(2,1)S(1)}, bf16[704,256]{1,0:T(8,128)(2,1)S(1)}, u32[]{:S(2)}, u32[]{:S(2)}) collective-permute-start(bf16[704,256]{1,0:T(8,128)(2,1)S(1)} %pad_maximum_fusion.2), channel_id=1, source_target_pairs={{0,16},{1,17},{2,18},{3,19},{4,20},{5,21},{6,22},{7,23},{8,24},{9,... | collective-permute-start | bytes 1081352 | tf_op jit(solution)/shard_map/ppermute | solution.py:307
  31.1 3.6 %copy-start.3 = (bf16[1024,256]{1,0:T(8,128)(2,1)S(1)}, bf16[1024,256]{1,0:T(8,128)(2,1)}, u32[]{:S(2)}) copy-start(bf16[1024,256]{1,0:T(8,128)(2,1)} %refs_2_.7) | copy-start | bytes 1572868
  31.1 9.3 %collective-permute-start.9 = (bf16[704,256]{1,0:T(8,128)(2,1)S(1)}, bf16[704,256]{1,0:T(8,128)(2,1)S(1)}, u32[]{:S(2)}, u32[]{:S(2)}) collective-permute-start(bf16[704,256]{1,0:T(8,128)(2,1)S(1)} %pad_maximum_fusion.1), channel_id=1, source_target_pairs={{0,16},{1,17},{2,18},{3,19},{4,20},{5,21},{6,22},{7,23},{8,24},{9,... | collective-permute-start | bytes 1081352 | tf_op jit(solution)/shard_map/ppermute | solution.py:307
  32.6 6.4 %collective-permute-start.8 = (bf16[512,256]{1,0:T(8,128)(2,1)S(1)}, bf16[512,256]{1,0:T(8,128)(2,1)S(1)}, u32[]{:S(2)}, u32[]{:S(2)}) collective-permute-start(bf16[512,256]{1,0:T(8,128)(2,1)S(1)} %slice.35), channel_id=1, source_target_pairs={{0,2},{1,3},{4,0},{5,1},{8,4},{9,5},{12,8},{13,9},{14,12},{15,13},... | collective-permute-start | bytes 786440 | tf_op jit(solution)/shard_map/ppermute | solution.py:307
  34.1 6.4 %collective-permute-start.7 = (bf16[512,256]{1,0:T(8,128)(2,1)S(1)}, bf16[512,256]{1,0:T(8,128)(2,1)S(1)}, u32[]{:S(2)}, u32[]{:S(2)}) collective-permute-start(bf16[512,256]{1,0:T(8,128)(2,1)S(1)} %slice.34), channel_id=1, source_target_pairs={{0,4},{1,5},{4,8},{5,9},{8,12},{9,13},{12,14},{13,15},{14,10},{15,... | collective-permute-start | bytes 786440 | tf_op jit(solution)/shard_map/ppermute | solution.py:307
  35.7 6.0 %collective-permute-start.13 = (bf16[3,512,256]{2,1,0:T(8,128)(2,1)S(1)}, bf16[3,512,256]{2,1,0:T(8,128)(2,1)S(1)}, u32[]{:S(2)}, u32[]{:S(2)}) collective-permute-start(bf16[3,512,256]{2,1,0:T(8,128)(2,1)S(1)} %shard_map.80.refs_0_), channel_id=1, source_target_pairs={{0,1},{1,0},{2,3},{3,2},{4,5},{5,4},{6,7},{7,6},{8,9},{9,8},{10,11... | collective-permute-start | bytes 2359304 | tf_op jit(solution)/shard_map/ppermute | solution.py:307
  41.2 2.7 %collective-permute-start.12 = (bf16[3,512,256]{2,1,0:T(8,128)(2,1)S(1)}, bf16[3,512,256]{2,1,0:T(8,128)(2,1)S(1)}, u32[]{:S(2)}, u32[]{:S(2)}) collective-permute-start(bf16[3,512,256]{2,1,0:T(8,128)(2,1)S(1)} %shard_map.79.refs_1_), channel_id=1, source_target_pairs={{0,1},{1,0},{2,3},{3,2},{4,5},{5,4},{6,7},{7,6},{8,9},{9,8},{10,11... | collective-permute-start | bytes 2359304 | tf_op jit(solution)/shard_map/ppermute | solution.py:307
  41.2 2.6 %collective-permute-start.11 = (bf16[1,512,256]{2,1,0:T(8,128)(2,1)S(1)}, bf16[1,512,256]{2,1,0:T(8,128)(2,1)S(1)}, u32[]{:S(2)}, u32[]{:S(2)}) collective-permute-start(bf16[1,512,256]{2,1,0:T(8,128)(2,1)S(1)} %get-tuple-element.40), channel_id=1, source_target_pairs={{0,1},{1,0},{2,3},{3,2},{4,5},{5,4},{6,7},{7,6},{8,9},{9,8},{10,11... | collective-permute-start | bytes 786440 | tf_op jit(solution)/shard_map/ppermute | solution.py:307

commit v8 on v7

--- a/solution.py
+++ b/solution.py
@@ -320,7 +320,8 @@
     p2, q2, y1 = send(p1, ahead), send(q1, back), send(edge(p1, q1), across)
     c1 = attend(queries, key_rows, values, position_bias, 2, 1, (c0,))
     live = live_slots(counts, donors, c0)
-    p2, c1, live = barrier((p2, c1, live))
+    p2, c1 = barrier((p2, c1))
+    q2, live = barrier((q2, live))
 
     p3, q3, y2 = send(p2, ahead), send(q2, back), send(edge(p2, q2), across)
     c1 = attend(queries, key_rows, values, position_bias, 3, 1, (c1,), joined=True)

time: 44.9 us -> 45.2 us (level)
  transfers between devices with their start and end apart: 14 -> 14, of which waited for: 8 -> 7; matrix products, arithmetic and copies ran while one was open for 0% -> 0% of each run, Pallas kernels for 34% -> 34%
where the time goes in v8:
time: 45.2 us; the launch traced here: 44.9 us
  Pallas kernels  16.1 us (36%)
  starting transfers between devices  14.8 us (33%)
  waiting for transfers between devices  9.38 us (21%)
  local copies, waits for them, and re-layouts  3.8 us (8%)
  between operations  0.87 us (2%)
    ppermute x14, starting transfers between devices, with_ring(): send = lambda value, pairs: lax.ppermute(value, AXES, pairs)  14.8 us
    pallas_call x3, Pallas kernels, attend(): pl.pallas_call(functools.partial(attention_kernel, first, joined), out_sh...  10.1 us
    ppermute x14, waiting for transfers between devices, with_ring(): send = lambda value, pairs: lax.ppermute(value, AXES, pairs)  9.38 us
    pallas_call x4, Pallas kernels, project(): pl.pallas_call(functools.partial(project_kernel, plan, len(context), len(...  3.62 us
    unnamed x12, local copies, waits for them, and re-layouts  2.46 us
    pallas_call x2, Pallas kernels, finish(): pl.pallas_call(functools.partial(finish_kernel, distances), out_shape=jax...  1.74 us
    slice x1, local copies, waits for them, and re-layouts, with_ring(): p1, q1 = (send(out_weight[:-cut], ahead), send(out_weight[cut:], back))  1.22 us
  transfers between devices with their start and end apart: 14, of which 7 were waited for; matrix products, arithmetic and copies ran while one was open for 0% of the time, Pallas kernels for 34%

profile of v8, /device:TPU:0, one launch (start us, length us, event | category | flops | bytes accessed | tf_op | source)
XLA Modules:
  0.0 44.9 jit_solution(11832129947665538192)
XLA Ops:
  0.0 1.2 %fusion = (bf16[672,256]{1,0:T(8,128)(2,1)S(1)}, bf16[672,256]{1,0:T(8,128)(2,1)S(1)}) fusion(bf16[1024,256]{1,0:T(8,128)(2,1)} %refs_2_.7), kind=kLoop, calls=%fused_computation.3 | loop fusion | bytes 1376256 | tf_op jit(solution)/shard_map/slice | solution.py:316
  1.2 3.1 %collective-permute-start.2 = (bf16[672,256]{1,0:T(8,128)(2,1)S(1)}, bf16[672,256]{1,0:T(8,128)(2,1)S(1)}, u32[]{:S(2)}, u32[]{:S(2)}) collective-permute-start(bf16[672,256]{1,0:T(8,128)(2,1)S(1)} %get-tuple-element.47), channel_id=1, source_target_pairs={{0,4},{1,5},{4,8},{5,9},{8,12},{9,13},{12,14},{13,15},{14,10},{15,... | collective-permute-start | bytes 1032200 | tf_op jit(solution)/shard_map/ppermute | solution.py:307
  4.3 1.2 %copy-done.1 = bf16[2,256,1024]{2,1,0:T(8,128)(2,1)S(1)} copy-done((bf16[2,256,1024]{2,1,0:T(8,128)(2,1)S(1)}, bf16[2,256,1024]{2,1,0:T(8,128)(2,1)}, u32[]{:S(2)}) %copy-start.1) | copy-done | bytes 1048600
  5.5 1.2 %copy-done.2 = bf16[2,256,1024]{2,1,0:T(8,128)(2,1)S(1)} copy-done((bf16[2,256,1024]{2,1,0:T(8,128)(2,1)S(1)}, bf16[2,256,1024]{2,1,0:T(8,128)(2,1)}, u32[]{:S(2)}) %copy-start.2) | copy-done | bytes 1048600
  6.8 5.0 %shard_map.73.after_ref.refs_3_.refs_0_ = bf16[512,512]{1,0:T(8,128)(2,1)S(1)} custom-call(f32[16,32]{1,0:T(8,128)S(1)} %bitcast.1, bf16[2,256,1024]{2,1,0:T(8,128)(2,1)S(1)} %copy-done, bf16[2,256,1024]{2,1,0:T(8,128)(2,1)S(1)} %copy-done.1, bf16[2,256,1024]{2,1,0:T(8,128)(2,1)S(1)} %copy-done.2), custom_call_target="tpu_custom_call" | custom-call | flops 268435456 | bytes 2097152 | tf_op jit(solution)/shard_map/pallas_call | solution.py:112
  12.3 1.8 %collective-permute-start.3 = (bf16[672,256]{1,0:T(8,128)(2,1)S(1)}, bf16[672,256]{1,0:T(8,128)(2,1)S(1)}, u32[]{:S(2)}, u32[]{:S(2)}) collective-permute-start(bf16[672,256]{1,0:T(8,128)(2,1)S(1)} %collective-permute-done.2.refs_3_), channel_id=1, source_target_pairs={{0,4},{1,5},{4,8},{5,9},{8,12},{9,13},{12,14},{13,15},{14,10},{15,... | collective-permute-start | bytes 1032200 | tf_op jit(solution)/shard_map/ppermute | solution.py:307
  14.4 1.8 %collective-permute-start.6 = (bf16[704,256]{1,0:T(8,128)(2,1)S(1)}, bf16[704,256]{1,0:T(8,128)(2,1)S(1)}, u32[]{:S(2)}, u32[]{:S(2)}) collective-permute-start(bf16[704,256]{1,0:T(8,128)(2,1)S(1)} %pad_maximum_fusion), channel_id=1, source_target_pairs={{0,16},{1,17},{2,18},{3,19},{4,20},{5,21},{6,22},{7,23},{8,24},{9,... | collective-permute-start | bytes 1081352 | tf_op jit(solution)/shard_map/ppermute | solution.py:307
  17.4 2.6 %shard_map.75.refs_3_ = bf16[512,256]{1,0:T(8,128)(2,1)S(1)} custom-call(f32[16,32]{1,0:T(8,128)S(1)} %bitcast.2, bf16[2,256,1024]{2,1,0:T(8,128)(2,1)S(1)} %copy-done, bf16[2,256,1024]{2,1,0:T(8,128)(2,1)S(1)} %copy-done.1, bf16[2,256,1024]{2,1,0:T(8,128)(2,1)S(1)} %copy-done.2, bf16[512,512]{1,0:T(8,128)(2,1)S(1)} %shard_map.73.after_ref.refs_3_.refs_0_), custom_call_target="tpu_custom_call" | custom-call | flops 134217728 | bytes 1048576 | tf_op jit(solution)/shard_map/pallas_call | solution.py:112
  20.0 1.5 %collective-permute-done.3.refs_2_ = bf16[672,256]{1,0:T(8,128)(2,1)S(1)} collective-permute-done((bf16[672,256]{1,0:T(8,128)(2,1)S(1)}, bf16[672,256]{1,0:T(8,128)(2,1)S(1)}, u32[]{:S(2)}, u32[]{:S(2)}) %collective-permute-start.3) | collective-permute-done | bytes 344096 | tf_op jit(solution)/shard_map/ppermute | solution.py:307
  21.5 1.6 %collective-permute-start.4 = (bf16[672,256]{1,0:T(8,128)(2,1)S(1)}, bf16[672,256]{1,0:T(8,128)(2,1)S(1)}, u32[]{:S(2)}, u32[]{:S(2)}) collective-permute-start(bf16[672,256]{1,0:T(8,128)(2,1)S(1)} %collective-permute-done.3.refs_2_), channel_id=1, source_target_pairs={{0,4},{1,5},{4,8},{5,9},{8,12},{9,13},{12,14},{13,15},{14,10},{15,... | collective-permute-start | bytes 1032200 | tf_op jit(solution)/shard_map/ppermute | solution.py:307
  23.6 1.6 %collective-permute-start.10 = (bf16[704,256]{1,0:T(8,128)(2,1)S(1)}, bf16[704,256]{1,0:T(8,128)(2,1)S(1)}, u32[]{:S(2)}, u32[]{:S(2)}) collective-permute-start(bf16[704,256]{1,0:T(8,128)(2,1)S(1)} %pad_maximum_fusion.2), channel_id=1, source_target_pairs={{0,16},{1,17},{2,18},{3,19},{4,20},{5,21},{6,22},{7,23},{8,24},{9,... | collective-permute-start | bytes 1081352 | tf_op jit(solution)/shard_map/ppermute | solution.py:307
  25.2 2.6 %shard_map.76.refs_1_ = bf16[512,512]{1,0:T(8,128)(2,1)S(1)} custom-call(f32[16,32]{1,0:T(8,128)S(1)} %bitcast.3, bf16[2,256,1024]{2,1,0:T(8,128)(2,1)S(1)} %copy-done, bf16[2,256,1024]{2,1,0:T(8,128)(2,1)S(1)} %copy-done.1, bf16[2,256,1024]{2,1,0:T(8,128)(2,1)S(1)} %copy-done.2, bf16[512,256]{1,0:T(8,128)(2,1)S(1)} %shard_map.75.refs_3_), custom_call_target="tpu_custom_call" | custom-call | flops 134217728 | bytes 1048576 | tf_op jit(solution)/shard_map/pallas_call | solution.py:112
  27.8 2.1 %collective-permute-done.4.refs_2_ = bf16[672,256]{1,0:T(8,128)(2,1)S(1)} collective-permute-done((bf16[672,256]{1,0:T(8,128)(2,1)S(1)}, bf16[672,256]{1,0:T(8,128)(2,1)S(1)}, u32[]{:S(2)}, u32[]{:S(2)}) %collective-permute-start.4) | collective-permute-done | bytes 344096 | tf_op jit(solution)/shard_map/ppermute | solution.py:307
  29.9 1.1 %collective-permute-done.5.refs_3_ = bf16[672,256]{1,0:T(8,128)(2,1)S(1)} collective-permute-done((bf16[672,256]{1,0:T(8,128)(2,1)S(1)}, bf16[672,256]{1,0:T(8,128)(2,1)S(1)}, u32[]{:S(2)}, u32[]{:S(2)}) %collective-permute-start.5) | collective-permute-done | bytes 344096 | tf_op jit(solution)/shard_map/ppermute | solution.py:307
  31.0 1.5 %collective-permute-start.9 = (bf16[704,256]{1,0:T(8,128)(2,1)S(1)}, bf16[704,256]{1,0:T(8,128)(2,1)S(1)}, u32[]{:S(2)}, u32[]{:S(2)}) collective-permute-start(bf16[704,256]{1,0:T(8,128)(2,1)S(1)} %pad_maximum_fusion.1), channel_id=1, source_target_pairs={{0,16},{1,17},{2,18},{3,19},{4,20},{5,21},{6,22},{7,23},{8,24},{9,... | collective-permute-start | bytes 1081352 | tf_op jit(solution)/shard_map/ppermute | solution.py:307
  32.6 1.8 %collective-permute-start.8 = (bf16[512,256]{1,0:T(8,128)(2,1)S(1)}, bf16[512,256]{1,0:T(8,128)(2,1)S(1)}, u32[]{:S(2)}, u32[]{:S(2)}) collective-permute-start(bf16[512,256]{1,0:T(8,128)(2,1)S(1)} %slice.35), channel_id=1, source_target_pairs={{0,2},{1,3},{4,0},{5,1},{8,4},{9,5},{12,8},{13,9},{14,12},{15,13},... | collective-permute-start | bytes 786440 | tf_op jit(solution)/shard_map/ppermute | solution.py:307
  34.6 1.0 %shard_map.80.refs_0_ = bf16[3,512,256]{2,1,0:T(8,128)(2,1)S(1)} custom-call(bf16[512,512]{1,0:T(8,128)(2,1)S(1)} %shard_map.73.after_ref.refs_3_.refs_0_, bf16[512,512]{1,0:T(8,128)(2,1)S(1)} %shard_map.76.refs_1_, bf16[1024,256]{1,0:T(8,128)(2,1)S(1)} %copy-done.3, bf16[672,256]{1,0:T(8,128)(2,1)S(1)} %collective-permute-done.2.refs_3_, ...), custom_call_target="tpu_custom_call" | custom-call | flops 805306368 | bytes 2359296 | tf_op jit(solution)/shard_map/pallas_call | solution.py:192
  36.3 1.4 %shard_map.77 = (bf16[2,512,256]{2,1,0:T(8,128)(2,1)S(1)}, bf16[1,512,256]{2,1,0:T(8,128)(2,1)S(1)}) custom-call(bf16[512,512]{1,0:T(8,128)(2,1)S(1)} %shard_map.73.after_ref.refs_3_.refs_0_, bf16[512,512]{1,0:T(8,128)(2,1)S(1)} %shard_map.76.refs_1_, bf16[672,256]{1,0:T(8,128)(2,1)S(1)} %collective-permute-done.3.refs_2_, ...), custom_call_target="tpu_custom_call" | custom-call | flops 536870912 | bytes 1572864 | tf_op jit(solution)/shard_map/pallas_call | solution.py:192
  37.7 1.3 %collective-permute-done.8.refs_6_ = bf16[512,256]{1,0:T(8,128)(2,1)S(1)} collective-permute-done((bf16[512,256]{1,0:T(8,128)(2,1)S(1)}, bf16[512,256]{1,0:T(8,128)(2,1)S(1)}, u32[]{:S(2)}, u32[]{:S(2)}) %collective-permute-start.8) | collective-permute-done | bytes 262176 | tf_op jit(solution)/shard_map/ppermute | solution.py:307
  39.0 1.7 %collective-permute-done.7.refs_5_ = bf16[512,256]{1,0:T(8,128)(2,1)S(1)} collective-permute-done((bf16[512,256]{1,0:T(8,128)(2,1)S(1)}, bf16[512,256]{1,0:T(8,128)(2,1)S(1)}, u32[]{:S(2)}, u32[]{:S(2)}) %collective-permute-start.7) | collective-permute-done | bytes 262176 | tf_op jit(solution)/shard_map/ppermute | solution.py:307
  40.7 0.7 %shard_map.79.refs_1_ = bf16[3,512,256]{2,1,0:T(8,128)(2,1)S(1)} custom-call(bf16[512,512]{1,0:T(8,128)(2,1)S(1)} %shard_map.73.after_ref.refs_3_.refs_0_, bf16[512,512]{1,0:T(8,128)(2,1)S(1)} %shard_map.76.refs_1_, bf16[672,256]{1,0:T(8,128)(2,1)S(1)} %collective-permute-done.4.refs_2_, bf16[672,256]{1,0:T(8,128)(2,1)S(1)} %collective-permute-done.5.refs_3_, ...), custom_call_target="tpu_custom_call" | custom-call | flops 469762048 | bytes 1703936 | tf_op jit(solution)/shard_map/pallas_call | solution.py:192
  42.0 0.9 %shard_map.81.refs_4_ = bf16[2,256,1024]{2,1,0:T(8,128)(2,1)} custom-call(bf16[32,256]{1,0:T(8,128)(2,1)S(1)} %shard_map.74.live_ref, bf16[3,512,256]{2,1,0:T(8,128)(2,1)S(1)} %shard_map.80.refs_0_, bf16[3,512,256]{2,1,0:T(8,128)(2,1)S(1)} %collective-permute-done.13.refs_1_), custom_call_target="tpu_custom_call" | custom-call | flops 393216 | bytes 1179648 | tf_op jit(solution)/shard_map/pallas_call | solution.py:277
  42.9 1.2 %collective-permute-done.11.refs_2_ = bf16[1,512,256]{2,1,0:T(8,128)(2,1)S(1)} collective-permute-done((bf16[1,512,256]{2,1,0:T(8,128)(2,1)S(1)}, bf16[1,512,256]{2,1,0:T(8,128)(2,1)S(1)}, u32[]{:S(2)}, u32[]{:S(2)}) %collective-permute-start.11) | collective-permute-done | bytes 262176 | tf_op jit(solution)/shard_map/ppermute | solution.py:307
  44.1 0.8 %shard_map.82 = bf16[2,256,1024]{2,1,0:T(8,128)(2,1)} custom-call(bf16[32,256]{1,0:T(8,128)(2,1)S(1)} %shard_map.74.live_ref, bf16[2,512,256]{2,1,0:T(8,128)(2,1)S(1)} %get-tuple-element.37.refs_0_, bf16[3,512,256]{2,1,0:T(8,128)(2,1)S(1)} %shard_map.79.refs_1_, ...), custom_call_target="tpu_custom_call", output_to_operand_aliasing={{}: (5, {})} | custom-call | flops 655360 | bytes 1966080 | tf_op jit(solution)/shard_map/pallas_call | solution.py:277
  (38 shorter events, 3.4 us)
Async XLA Ops:
  0.0 4.3 %copy-start = (bf16[2,256,1024]{2,1,0:T(8,128)(2,1)S(1)}, bf16[2,256,1024]{2,1,0:T(8,128)(2,1)}, u32[]{:S(2)}) copy-start(bf16[2,256,1024]{2,1,0:T(8,128)(2,1)} %refs_0_.5) | copy-start | bytes 3145732
  0.0 4.3 %copy-start.4 = (f32[32,16]{0,1:T(8,128)S(1)}, f32[32,16]{0,1:T(8,128)}, u32[]{:S(2)}) copy-start(f32[32,16]{0,1:T(8,128)} %param.10) | copy-start | bytes 6148
  1.2 11.1 %collective-permute-start.2 = (bf16[672,256]{1,0:T(8,128)(2,1)S(1)}, bf16[672,256]{1,0:T(8,128)(2,1)S(1)}, u32[]{:S(2)}, u32[]{:S(2)}) collective-permute-start(bf16[672,256]{1,0:T(8,128)(2,1)S(1)} %get-tuple-element.47), channel_id=1, source_target_pairs={{0,4},{1,5},{4,8},{5,9},{8,12},{9,13},{12,14},{13,15},{14,10},{15,... | collective-permute-start | bytes 1032200 | tf_op jit(solution)/shard_map/ppermute | solution.py:307
  4.3 9.8 %collective-permute-start = (bf16[672,256]{1,0:T(8,128)(2,1)S(1)}, bf16[672,256]{1,0:T(8,128)(2,1)S(1)}, u32[]{:S(2)}, u32[]{:S(2)}) collective-permute-start(bf16[672,256]{1,0:T(8,128)(2,1)S(1)} %get-tuple-element.48), channel_id=1, source_target_pairs={{0,2},{1,3},{4,0},{5,1},{8,4},{9,5},{12,8},{13,9},{14,12},{15,13},... | collective-permute-start | bytes 1032200 | tf_op jit(solution)/shard_map/ppermute | solution.py:307
  4.3 1.2 %copy-start.1 = (bf16[2,256,1024]{2,1,0:T(8,128)(2,1)S(1)}, bf16[2,256,1024]{2,1,0:T(8,128)(2,1)}, u32[]{:S(2)}) copy-start(bf16[2,256,1024]{2,1,0:T(8,128)(2,1)} %refs_1_.5) | copy-start | bytes 3145732
  5.5 1.2 %copy-start.2 = (bf16[2,256,1024]{2,1,0:T(8,128)(2,1)S(1)}, bf16[2,256,1024]{2,1,0:T(8,128)(2,1)}, u32[]{:S(2)}) copy-start(bf16[2,256,1024]{2,1,0:T(8,128)(2,1)} %refs_2_.6) | copy-start | bytes 3145732
  12.3 9.2 %collective-permute-start.3 = (bf16[672,256]{1,0:T(8,128)(2,1)S(1)}, bf16[672,256]{1,0:T(8,128)(2,1)S(1)}, u32[]{:S(2)}, u32[]{:S(2)}) collective-permute-start(bf16[672,256]{1,0:T(8,128)(2,1)S(1)} %collective-permute-done.2.refs_3_), channel_id=1, source_target_pairs={{0,4},{1,5},{4,8},{5,9},{8,12},{9,13},{12,14},{13,15},{14,10},{15,... | collective-permute-start | bytes 1032200 | tf_op jit(solution)/shard_map/ppermute | solution.py:307
  14.1 9.0 %collective-permute-start.1 = (bf16[672,256]{1,0:T(8,128)(2,1)S(1)}, bf16[672,256]{1,0:T(8,128)(2,1)S(1)}, u32[]{:S(2)}, u32[]{:S(2)}) collective-permute-start(bf16[672,256]{1,0:T(8,128)(2,1)S(1)} %collective-permute-done.refs_4_), channel_id=1, source_target_pairs={{0,2},{1,3},{4,0},{5,1},{8,4},{9,5},{12,8},{13,9},{14,12},{15,13},... | collective-permute-start | bytes 1032200 | tf_op jit(solution)/shard_map/ppermute | solution.py:307
  14.4 2.5 %copy-start.5 = (s32[4]{0:T(128)S(1)}, s32[4]{0:T(128)}, u32[]{:S(2)}) copy-start(s32[4]{0:T(128)} %donors_ref.1) | copy-start | bytes 52
  14.4 13.4 %collective-permute-start.6 = (bf16[704,256]{1,0:T(8,128)(2,1)S(1)}, bf16[704,256]{1,0:T(8,128)(2,1)S(1)}, u32[]{:S(2)}, u32[]{:S(2)}) collective-permute-start(bf16[704,256]{1,0:T(8,128)(2,1)S(1)} %pad_maximum_fusion), channel_id=1, source_target_pairs={{0,16},{1,17},{2,18},{3,19},{4,20},{5,21},{6,22},{7,23},{8,24},{9,... | collective-permute-start | bytes 1081352 | tf_op jit(solution)/shard_map/ppermute | solution.py:307
  21.5 8.3 %collective-permute-start.4 = (bf16[672,256]{1,0:T(8,128)(2,1)S(1)}, bf16[672,256]{1,0:T(8,128)(2,1)S(1)}, u32[]{:S(2)}, u32[]{:S(2)}) collective-permute-start(bf16[672,256]{1,0:T(8,128)(2,1)S(1)} %collective-permute-done.3.refs_2_), channel_id=1, source_target_pairs={{0,4},{1,5},{4,8},{5,9},{8,12},{9,13},{12,14},{13,15},{14,10},{15,... | collective-permute-start | bytes 1032200 | tf_op jit(solution)/shard_map/ppermute | solution.py:307
  23.1 7.8 %collective-permute-start.5 = (bf16[672,256]{1,0:T(8,128)(2,1)S(1)}, bf16[672,256]{1,0:T(8,128)(2,1)S(1)}, u32[]{:S(2)}, u32[]{:S(2)}) collective-permute-start(bf16[672,256]{1,0:T(8,128)(2,1)S(1)} %collective-permute-done.1.refs_3_), channel_id=1, source_target_pairs={{0,2},{1,3},{4,0},{5,1},{8,4},{9,5},{12,8},{13,9},{14,12},{15,13},... | collective-permute-start | bytes 1032200 | tf_op jit(solution)/shard_map/ppermute | solution.py:307
  23.6 12.6 %collective-permute-start.10 = (bf16[704,256]{1,0:T(8,128)(2,1)S(1)}, bf16[704,256]{1,0:T(8,128)(2,1)S(1)}, u32[]{:S(2)}, u32[]{:S(2)}) collective-permute-start(bf16[704,256]{1,0:T(8,128)(2,1)S(1)} %pad_maximum_fusion.2), channel_id=1, source_target_pairs={{0,16},{1,17},{2,18},{3,19},{4,20},{5,21},{6,22},{7,23},{8,24},{9,... | collective-permute-start | bytes 1081352 | tf_op jit(solution)/shard_map/ppermute | solution.py:307
  31.0 3.6 %copy-start.3 = (bf16[1024,256]{1,0:T(8,128)(2,1)S(1)}, bf16[1024,256]{1,0:T(8,128)(2,1)}, u32[]{:S(2)}) copy-start(bf16[1024,256]{1,0:T(8,128)(2,1)} %refs_2_.7) | copy-start | bytes 1572868
  31.0 9.7 %collective-permute-start.9 = (bf16[704,256]{1,0:T(8,128)(2,1)S(1)}, bf16[704,256]{1,0:T(8,128)(2,1)S(1)}, u32[]{:S(2)}, u32[]{:S(2)}) collective-permute-start(bf16[704,256]{1,0:T(8,128)(2,1)S(1)} %pad_maximum_fusion.1), channel_id=1, source_target_pairs={{0,16},{1,17},{2,18},{3,19},{4,20},{5,21},{6,22},{7,23},{8,24},{9,... | collective-permute-start | bytes 1081352 | tf_op jit(solution)/shard_map/ppermute | solution.py:307
  32.6 6.4 %collective-permute-start.8 = (bf16[512,256]{1,0:T(8,128)(2,1)S(1)}, bf16[512,256]{1,0:T(8,128)(2,1)S(1)}, u32[]{:S(2)}, u32[]{:S(2)}) collective-permute-start(bf16[512,256]{1,0:T(8,128)(2,1)S(1)} %slice.35), channel_id=1, source_target_pairs={{0,2},{1,3},{4,0},{5,1},{8,4},{9,5},{12,8},{13,9},{14,12},{15,13},... | collective-permute-start | bytes 786440 | tf_op jit(solution)/shard_map/ppermute | solution.py:307
  34.3 6.4 %collective-permute-start.7 = (bf16[512,256]{1,0:T(8,128)(2,1)S(1)}, bf16[512,256]{1,0:T(8,128)(2,1)S(1)}, u32[]{:S(2)}, u32[]{:S(2)}) collective-permute-start(bf16[512,256]{1,0:T(8,128)(2,1)S(1)} %slice.34), channel_id=1, source_target_pairs={{0,4},{1,5},{4,8},{5,9},{8,12},{9,13},{12,14},{13,15},{14,10},{15,... | collective-permute-start | bytes 786440 | tf_op jit(solution)/shard_map/ppermute | solution.py:307
  35.6 6.4 %collective-permute-start.13 = (bf16[3,512,256]{2,1,0:T(8,128)(2,1)S(1)}, bf16[3,512,256]{2,1,0:T(8,128)(2,1)S(1)}, u32[]{:S(2)}, u32[]{:S(2)}) collective-permute-start(bf16[3,512,256]{2,1,0:T(8,128)(2,1)S(1)} %shard_map.80.refs_0_), channel_id=1, source_target_pairs={{0,1},{1,0},{2,3},{3,2},{4,5},{5,4},{6,7},{7,6},{8,9},{9,8},{10,11... | collective-permute-start | bytes 2359304 | tf_op jit(solution)/shard_map/ppermute | solution.py:307
  41.4 2.7 %collective-permute-start.12 = (bf16[3,512,256]{2,1,0:T(8,128)(2,1)S(1)}, bf16[3,512,256]{2,1,0:T(8,128)(2,1)S(1)}, u32[]{:S(2)}, u32[]{:S(2)}) collective-permute-start(bf16[3,512,256]{2,1,0:T(8,128)(2,1)S(1)} %shard_map.79.refs_1_), channel_id=1, source_target_pairs={{0,1},{1,0},{2,3},{3,2},{4,5},{5,4},{6,7},{7,6},{8,9},{9,8},{10,11... | collective-permute-start | bytes 2359304 | tf_op jit(solution)/shard_map/ppermute | solution.py:307
  41.5 2.6 %collective-permute-start.11 = (bf16[1,512,256]{2,1,0:T(8,128)(2,1)S(1)}, bf16[1,512,256]{2,1,0:T(8,128)(2,1)S(1)}, u32[]{:S(2)}, u32[]{:S(2)}) collective-permute-start(bf16[1,512,256]{2,1,0:T(8,128)(2,1)S(1)} %get-tuple-element.42), channel_id=1, source_target_pairs={{0,1},{1,0},{2,3},{3,2},{4,5},{5,4},{6,7},{7,6},{8,9},{9,8},{10,11... | collective-permute-start | bytes 786440 | tf_op jit(solution)/shard_map/ppermute | solution.py:307

commit v9 on v7

--- a/solution.py
+++ b/solution.py
@@ -334,7 +334,7 @@
     q_part = [(0, half - lead, [(1, spill, lead)]), (1, 0, [(1, over, half)])]
     p_rest = [(1, lead, [(0, half + lead, spill), (2, cut, cut)])]
     q_rest = [(0, 0, [(2, 0, cut), (1, 0, spill)])]
-    opposite = [(0, 0, [(3, 0, half)]), (1, 0, [(4, 0, half)])]
+    opposite = [(0, 0, [(0, 0, half)]), (1, 0, [(1, 0, half)])]
 
     p4, q4 = send(p3[:half], ahead), send(q3[-half:], back)
     y3 = send(edge(p3, q3), across)
@@ -345,16 +345,18 @@
         context, (p2, q2, y2), [p_block(0, 2), q_block(1, 2)], jnp.bfloat16, choice=(2, -2)
     )
     (started,) = project(context, (p3, q3), [p_part, q_part], jnp.float32)
-    p4, q4, y3, e2, s2, started = barrier((p4, q4, y3, e2, s2, started))
-
-    x1, x2 = send(e1, cores), send(s2, cores)
-    (e3,) = project(
-        context, (p3, q3, y3, p4, q4), [p_rest, q_rest, opposite], jnp.bfloat16, (started,)
-    )
+    p4, q4, e2, s2, started = barrier((p4, q4, e2, s2, started))
+
+    (e4,) = project(context, (p4, q4), [opposite], jnp.bfloat16)
+    x1, x2, x4 = send(e1, cores), send(s2, cores), send(e4, cores)
+    y3, e4 = barrier((y3, e4))
+    (e3,) = project(context, (p3, q3, y3), [p_rest, q_rest], jnp.bfloat16, (started,))
     x3 = send(e3, cores)
     early = finish((e1,), (x1,), ((0, 1, -1),), live, slots)
-    x2, x3, early = barrier((x2, x3, early))
-    return finish((e2, e3), (x2, x3), ((2, -2), (3, -3, 4)), live, slots, (early,))
+    x2, x3, x4, early = barrier((x2, x3, x4, early))
+    return finish(
+        (e2, e4, e3), (x2, x4, x3), ((2, -2), (4,), (3, -3)), live, slots, (early,)
+    )
 
 
 def with_gather(queries, key_rows, values, position_bias, out_weight, counts, donors):

time: 44.9 us -> 44.2 us (0.984)
  waiting for transfers between devices: 9.25 us -> 8.1 us
    ppermute x14 -> x15, waiting for transfers between devices: 9.25 us -> 8.1 us  [with_ring(): send = lambda value, pairs: lax.ppermute(value, AXES, pairs)]
    ppermute x14 -> x15, starting transfers between devices: 14.6 us -> 14.9 us  [with_ring(): send = lambda value, pairs: lax.ppermute(value, AXES, pairs)]
    pallas_call x4 -> x5, Pallas kernels: 3.62 us -> 3.79 us  [project(): pl.pallas_call(functools.partial(project_kernel, plan, len(context), len(...]
  transfers between devices with their start and end apart: 14 -> 15, of which waited for: 8 -> 8; matrix products, arithmetic and copies ran while one was open for 0% -> 0% of each run, Pallas kernels for 34% -> 35%
where the time goes in v9:
time: 44.2 us; the launch traced here: 43.9 us
  Pallas kernels  16.2 us (37%)
  starting transfers between devices  14.9 us (34%)
  waiting for transfers between devices  8.1 us (18%)
  local copies, waits for them, and re-layouts  3.8 us (9%)
  between operations  0.89 us (2%)
    ppermute x15, starting transfers between devices, with_ring(): send = lambda value, pairs: lax.ppermute(value, AXES, pairs)  14.9 us
    pallas_call x3, Pallas kernels, attend(): pl.pallas_call(functools.partial(attention_kernel, first, joined), out_sh...  10.1 us
    ppermute x15, waiting for transfers between devices, with_ring(): send = lambda value, pairs: lax.ppermute(value, AXES, pairs)  8.1 us
    pallas_call x5, Pallas kernels, project(): pl.pallas_call(functools.partial(project_kernel, plan, len(context), len(...  3.79 us
    unnamed x12, local copies, waits for them, and re-layouts  2.46 us
    pallas_call x2, Pallas kernels, finish(): pl.pallas_call(functools.partial(finish_kernel, distances), out_shape=jax...  1.75 us
    slice x1, local copies, waits for them, and re-layouts, with_ring(): p1, q1 = (send(out_weight[:-cut], ahead), send(out_weight[cut:], back))  1.22 us
  transfers between devices with their start and end apart: 15, of which 8 were waited for; matrix products, arithmetic and copies ran while one was open for 0% of the time, Pallas kernels for 35%

profile of v9, /device:TPU:0, one launch (start us, length us, event | category | flops | bytes accessed | tf_op | source)
XLA Modules:
  0.0 43.9 jit_solution(1853612164732361698)
XLA Ops:
  0.0 1.2 %fusion = (bf16[672,256]{1,0:T(8,128)(2,1)S(1)}, bf16[672,256]{1,0:T(8,128)(2,1)S(1)}) fusion(bf16[1024,256]{1,0:T(8,128)(2,1)} %refs_2_.7), kind=kLoop, calls=%fused_computation.3 | loop fusion | bytes 1376256 | tf_op jit(solution)/shard_map/slice | solution.py:316
  1.2 3.1 %collective-permute-start = (bf16[672,256]{1,0:T(8,128)(2,1)S(1)}, bf16[672,256]{1,0:T(8,128)(2,1)S(1)}, u32[]{:S(2)}, u32[]{:S(2)}) collective-permute-start(bf16[672,256]{1,0:T(8,128)(2,1)S(1)} %get-tuple-element.50), channel_id=1, source_target_pairs={{0,4},{1,5},{4,8},{5,9},{8,12},{9,13},{12,14},{13,15},{14,10},{15,... | collective-permute-start | bytes 1032200 | tf_op jit(solution)/shard_map/ppermute | solution.py:307
  4.3 1.2 %copy-done.1 = bf16[2,256,1024]{2,1,0:T(8,128)(2,1)S(1)} copy-done((bf16[2,256,1024]{2,1,0:T(8,128)(2,1)S(1)}, bf16[2,256,1024]{2,1,0:T(8,128)(2,1)}, u32[]{:S(2)}) %copy-start.1) | copy-done | bytes 1048600
  5.5 1.2 %copy-done.2 = bf16[2,256,1024]{2,1,0:T(8,128)(2,1)S(1)} copy-done((bf16[2,256,1024]{2,1,0:T(8,128)(2,1)S(1)}, bf16[2,256,1024]{2,1,0:T(8,128)(2,1)}, u32[]{:S(2)}) %copy-start.2) | copy-done | bytes 1048600
  6.8 5.0 %shard_map.73.refs_3_.after_ref.refs_0_ = bf16[512,512]{1,0:T(8,128)(2,1)S(1)} custom-call(f32[16,32]{1,0:T(8,128)S(1)} %bitcast.1, bf16[2,256,1024]{2,1,0:T(8,128)(2,1)S(1)} %copy-done, bf16[2,256,1024]{2,1,0:T(8,128)(2,1)S(1)} %copy-done.1, bf16[2,256,1024]{2,1,0:T(8,128)(2,1)S(1)} %copy-done.2), custom_call_target="tpu_custom_call" | custom-call | flops 268435456 | bytes 2097152 | tf_op jit(solution)/shard_map/pallas_call | solution.py:112
  12.3 1.8 %collective-permute-start.1 = (bf16[672,256]{1,0:T(8,128)(2,1)S(1)}, bf16[672,256]{1,0:T(8,128)(2,1)S(1)}, u32[]{:S(2)}, u32[]{:S(2)}) collective-permute-start(bf16[672,256]{1,0:T(8,128)(2,1)S(1)} %collective-permute-done.refs_3_), channel_id=1, source_target_pairs={{0,4},{1,5},{4,8},{5,9},{8,12},{9,13},{12,14},{13,15},{14,10},{15,... | collective-permute-start | bytes 1032200 | tf_op jit(solution)/shard_map/ppermute | solution.py:307
  14.4 1.8 %collective-permute-start.6 = (bf16[704,256]{1,0:T(8,128)(2,1)S(1)}, bf16[704,256]{1,0:T(8,128)(2,1)S(1)}, u32[]{:S(2)}, u32[]{:S(2)}) collective-permute-start(bf16[704,256]{1,0:T(8,128)(2,1)S(1)} %pad_maximum_fusion), channel_id=1, source_target_pairs={{0,16},{1,17},{2,18},{3,19},{4,20},{5,21},{6,22},{7,23},{8,24},{9,... | collective-permute-start | bytes 1081352 | tf_op jit(solution)/shard_map/ppermute | solution.py:307
  17.4 2.6 %shard_map.74.refs_3_ = bf16[512,256]{1,0:T(8,128)(2,1)S(1)} custom-call(f32[16,32]{1,0:T(8,128)S(1)} %bitcast.2, bf16[2,256,1024]{2,1,0:T(8,128)(2,1)S(1)} %copy-done, bf16[2,256,1024]{2,1,0:T(8,128)(2,1)S(1)} %copy-done.1, bf16[2,256,1024]{2,1,0:T(8,128)(2,1)S(1)} %copy-done.2, bf16[512,512]{1,0:T(8,128)(2,1)S(1)} %shard_map.73.refs_3_.after_ref.refs_0_), custom_call_target="tpu_custom_call" | custom-call | flops 134217728 | bytes 1048576 | tf_op jit(solution)/shard_map/pallas_call | solution.py:112
  20.0 1.5 %collective-permute-done.1.refs_2_ = bf16[672,256]{1,0:T(8,128)(2,1)S(1)} collective-permute-done((bf16[672,256]{1,0:T(8,128)(2,1)S(1)}, bf16[672,256]{1,0:T(8,128)(2,1)S(1)}, u32[]{:S(2)}, u32[]{:S(2)}) %collective-permute-start.1) | collective-permute-done | bytes 344096 | tf_op jit(solution)/shard_map/ppermute | solution.py:307
  21.5 1.6 %collective-permute-start.2 = (bf16[672,256]{1,0:T(8,128)(2,1)S(1)}, bf16[672,256]{1,0:T(8,128)(2,1)S(1)}, u32[]{:S(2)}, u32[]{:S(2)}) collective-permute-start(bf16[672,256]{1,0:T(8,128)(2,1)S(1)} %collective-permute-done.1.refs_2_), channel_id=1, source_target_pairs={{0,4},{1,5},{4,8},{5,9},{8,12},{9,13},{12,14},{13,15},{14,10},{15,... | collective-permute-start | bytes 1032200 | tf_op jit(solution)/shard_map/ppermute | solution.py:307
  23.6 1.6 %collective-permute-start.9 = (bf16[704,256]{1,0:T(8,128)(2,1)S(1)}, bf16[704,256]{1,0:T(8,128)(2,1)S(1)}, u32[]{:S(2)}, u32[]{:S(2)}) collective-permute-start(bf16[704,256]{1,0:T(8,128)(2,1)S(1)} %pad_maximum_fusion.1), channel_id=1, source_target_pairs={{0,16},{1,17},{2,18},{3,19},{4,20},{5,21},{6,22},{7,23},{8,24},{9,... | collective-permute-start | bytes 1081352 | tf_op jit(solution)/shard_map/ppermute | solution.py:307
  25.2 2.6 %shard_map.76.refs_1_ = bf16[512,512]{1,0:T(8,128)(2,1)S(1)} custom-call(f32[16,32]{1,0:T(8,128)S(1)} %bitcast.3, bf16[2,256,1024]{2,1,0:T(8,128)(2,1)S(1)} %copy-done, bf16[2,256,1024]{2,1,0:T(8,128)(2,1)S(1)} %copy-done.1, bf16[2,256,1024]{2,1,0:T(8,128)(2,1)S(1)} %copy-done.2, bf16[512,256]{1,0:T(8,128)(2,1)S(1)} %shard_map.74.refs_3_), custom_call_target="tpu_custom_call" | custom-call | flops 134217728 | bytes 1048576 | tf_op jit(solution)/shard_map/pallas_call | solution.py:112
  27.8 2.0 %collective-permute-done.2.refs_2_ = bf16[672,256]{1,0:T(8,128)(2,1)S(1)} collective-permute-done((bf16[672,256]{1,0:T(8,128)(2,1)S(1)}, bf16[672,256]{1,0:T(8,128)(2,1)S(1)}, u32[]{:S(2)}, u32[]{:S(2)}) %collective-permute-start.2) | collective-permute-done | bytes 344096 | tf_op jit(solution)/shard_map/ppermute | solution.py:307
  29.9 1.1 %collective-permute-done.5.refs_3_ = bf16[672,256]{1,0:T(8,128)(2,1)S(1)} collective-permute-done((bf16[672,256]{1,0:T(8,128)(2,1)S(1)}, bf16[672,256]{1,0:T(8,128)(2,1)S(1)}, u32[]{:S(2)}, u32[]{:S(2)}) %collective-permute-start.5) | collective-permute-done | bytes 344096 | tf_op jit(solution)/shard_map/ppermute | solution.py:307
  31.0 1.5 %collective-permute-start.10 = (bf16[704,256]{1,0:T(8,128)(2,1)S(1)}, bf16[704,256]{1,0:T(8,128)(2,1)S(1)}, u32[]{:S(2)}, u32[]{:S(2)}) collective-permute-start(bf16[704,256]{1,0:T(8,128)(2,1)S(1)} %pad_maximum_fusion.2), channel_id=1, source_target_pairs={{0,16},{1,17},{2,18},{3,19},{4,20},{5,21},{6,22},{7,23},{8,24},{9,... | collective-permute-start | bytes 1081352 | tf_op jit(solution)/shard_map/ppermute | solution.py:307
  32.6 0.6 %collective-permute-start.7 = (bf16[512,256]{1,0:T(8,128)(2,1)S(1)}, bf16[512,256]{1,0:T(8,128)(2,1)S(1)}, u32[]{:S(2)}, u32[]{:S(2)}) collective-permute-start(bf16[512,256]{1,0:T(8,128)(2,1)S(1)} %slice.34), channel_id=1, source_target_pairs={{0,4},{1,5},{4,8},{5,9},{8,12},{9,13},{12,14},{13,15},{14,10},{15,... | collective-permute-start | bytes 786440 | tf_op jit(solution)/shard_map/ppermute | solution.py:307
  33.1 1.5 %collective-permute-start.8 = (bf16[512,256]{1,0:T(8,128)(2,1)S(1)}, bf16[512,256]{1,0:T(8,128)(2,1)S(1)}, u32[]{:S(2)}, u32[]{:S(2)}) collective-permute-start(bf16[512,256]{1,0:T(8,128)(2,1)S(1)} %slice.35), channel_id=1, source_target_pairs={{0,2},{1,3},{4,0},{5,1},{8,4},{9,5},{12,8},{13,9},{14,12},{15,13},... | collective-permute-start | bytes 786440 | tf_op jit(solution)/shard_map/ppermute | solution.py:307
  34.6 1.0 %shard_map.81.refs_0_ = bf16[3,512,256]{2,1,0:T(8,128)(2,1)S(1)} custom-call(bf16[512,512]{1,0:T(8,128)(2,1)S(1)} %shard_map.73.refs_3_.after_ref.refs_0_, bf16[512,512]{1,0:T(8,128)(2,1)S(1)} %shard_map.76.refs_1_, bf16[1024,256]{1,0:T(8,128)(2,1)S(1)} %copy-done.3, bf16[672,256]{1,0:T(8,128)(2,1)S(1)} %collective-permute-done.refs_3_, ...), custom_call_target="tpu_custom_call" | custom-call | flops 805306368 | bytes 2359296 | tf_op jit(solution)/shard_map/pallas_call | solution.py:192
  35.7 0.6 %shard_map.78.refs_5_ = f32[2,512,256]{2,1,0:T(8,128)S(1)} custom-call(bf16[512,512]{1,0:T(8,128)(2,1)S(1)} %shard_map.73.refs_3_.after_ref.refs_0_, bf16[512,512]{1,0:T(8,128)(2,1)S(1)} %shard_map.76.refs_1_, bf16[672,256]{1,0:T(8,128)(2,1)S(1)} %collective-permute-done.2.refs_2_, bf16[672,256]{1,0:T(8,128)(2,1)S(1)} %collective-permute-done.5.refs_3_), custom_call_target="tpu_custom_call" | custom-call | flops 335544320 | bytes 1179648 | tf_op jit(solution)/shard_map/pallas_call | solution.py:192
  36.3 1.4 %shard_map.77 = (bf16[2,512,256]{2,1,0:T(8,128)(2,1)S(1)}, bf16[1,512,256]{2,1,0:T(8,128)(2,1)S(1)}) custom-call(bf16[512,512]{1,0:T(8,128)(2,1)S(1)} %shard_map.73.refs_3_.after_ref.refs_0_, bf16[512,512]{1,0:T(8,128)(2,1)S(1)} %shard_map.76.refs_1_, bf16[672,256]{1,0:T(8,128)(2,1)S(1)} %collective-permute-done.1.refs_2_, ...), custom_call_target="tpu_custom_call" | custom-call | flops 536870912 | bytes 1572864 | tf_op jit(solution)/shard_map/pallas_call | solution.py:192
  37.7 1.3 %collective-permute-done.7.refs_2_ = bf16[512,256]{1,0:T(8,128)(2,1)S(1)} collective-permute-done((bf16[512,256]{1,0:T(8,128)(2,1)S(1)}, bf16[512,256]{1,0:T(8,128)(2,1)S(1)}, u32[]{:S(2)}, u32[]{:S(2)}) %collective-permute-start.7) | collective-permute-done | bytes 262176 | tf_op jit(solution)/shard_map/ppermute | solution.py:307
  41.1 0.9 %shard_map.82.refs_6_ = bf16[2,256,1024]{2,1,0:T(8,128)(2,1)} custom-call(bf16[32,256]{1,0:T(8,128)(2,1)S(1)} %shard_map.75.live_ref, bf16[3,512,256]{2,1,0:T(8,128)(2,1)S(1)} %shard_map.81.refs_0_, bf16[3,512,256]{2,1,0:T(8,128)(2,1)S(1)} %collective-permute-done.14.refs_1_), custom_call_target="tpu_custom_call" | custom-call | flops 393216 | bytes 1179648 | tf_op jit(solution)/shard_map/pallas_call | solution.py:277
  42.0 0.7 %collective-permute-done.13.refs_4_ = bf16[1,512,256]{2,1,0:T(8,128)(2,1)S(1)} collective-permute-done((bf16[1,512,256]{2,1,0:T(8,128)(2,1)S(1)}, bf16[1,512,256]{2,1,0:T(8,128)(2,1)S(1)}, u32[]{:S(2)}, u32[]{:S(2)}) %collective-permute-start.13) | collective-permute-done | bytes 262176 | tf_op jit(solution)/shard_map/ppermute | solution.py:307
  43.1 0.8 %shard_map.83 = bf16[2,256,1024]{2,1,0:T(8,128)(2,1)} custom-call(bf16[32,256]{1,0:T(8,128)(2,1)S(1)} %shard_map.75.live_ref, bf16[2,512,256]{2,1,0:T(8,128)(2,1)S(1)} %get-tuple-element.37.refs_0_, bf16[1,512,256]{2,1,0:T(8,128)(2,1)S(1)} %shard_map.79.refs_1_, bf16[2,512,256]{2,1,0:T(8,128)(2,1)S(1)} %shard_map.80.refs_2_, ...), custom_call_target="tpu_custom_call", output_to_operand_aliasing={{}: (7, {})} | custom-call | flops 655360 | bytes 1966080 | tf_op jit(solution)/shard_map/pallas_call | solution.py:277
  (41 shorter events, 4.4 us)
Async XLA Ops:
  0.0 4.3 %copy-start = (bf16[2,256,1024]{2,1,0:T(8,128)(2,1)S(1)}, bf16[2,256,1024]{2,1,0:T(8,128)(2,1)}, u32[]{:S(2)}) copy-start(bf16[2,256,1024]{2,1,0:T(8,128)(2,1)} %refs_0_.5) | copy-start | bytes 3145732
  0.0 4.3 %copy-start.4 = (f32[32,16]{0,1:T(8,128)S(1)}, f32[32,16]{0,1:T(8,128)}, u32[]{:S(2)}) copy-start(f32[32,16]{0,1:T(8,128)} %param.10) | copy-start | bytes 6148
  1.2 11.1 %collective-permute-start = (bf16[672,256]{1,0:T(8,128)(2,1)S(1)}, bf16[672,256]{1,0:T(8,128)(2,1)S(1)}, u32[]{:S(2)}, u32[]{:S(2)}) collective-permute-start(bf16[672,256]{1,0:T(8,128)(2,1)S(1)} %get-tuple-element.50), channel_id=1, source_target_pairs={{0,4},{1,5},{4,8},{5,9},{8,12},{9,13},{12,14},{13,15},{14,10},{15,... | collective-permute-start | bytes 1032200 | tf_op jit(solution)/shard_map/ppermute | solution.py:307
  4.3 9.8 %collective-permute-start.3 = (bf16[672,256]{1,0:T(8,128)(2,1)S(1)}, bf16[672,256]{1,0:T(8,128)(2,1)S(1)}, u32[]{:S(2)}, u32[]{:S(2)}) collective-permute-start(bf16[672,256]{1,0:T(8,128)(2,1)S(1)} %get-tuple-element.49), channel_id=1, source_target_pairs={{0,2},{1,3},{4,0},{5,1},{8,4},{9,5},{12,8},{13,9},{14,12},{15,13},... | collective-permute-start | bytes 1032200 | tf_op jit(solution)/shard_map/ppermute | solution.py:307
  4.3 1.2 %copy-start.1 = (bf16[2,256,1024]{2,1,0:T(8,128)(2,1)S(1)}, bf16[2,256,1024]{2,1,0:T(8,128)(2,1)}, u32[]{:S(2)}) copy-start(bf16[2,256,1024]{2,1,0:T(8,128)(2,1)} %refs_1_.5) | copy-start | bytes 3145732
  5.5 1.2 %copy-start.2 = (bf16[2,256,1024]{2,1,0:T(8,128)(2,1)S(1)}, bf16[2,256,1024]{2,1,0:T(8,128)(2,1)}, u32[]{:S(2)}) copy-start(bf16[2,256,1024]{2,1,0:T(8,128)(2,1)} %refs_2_.6) | copy-start | bytes 3145732
  12.3 9.2 %collective-permute-start.1 = (bf16[672,256]{1,0:T(8,128)(2,1)S(1)}, bf16[672,256]{1,0:T(8,128)(2,1)S(1)}, u32[]{:S(2)}, u32[]{:S(2)}) collective-permute-start(bf16[672,256]{1,0:T(8,128)(2,1)S(1)} %collective-permute-done.refs_3_), channel_id=1, source_target_pairs={{0,4},{1,5},{4,8},{5,9},{8,12},{9,13},{12,14},{13,15},{14,10},{15,... | collective-permute-start | bytes 1032200 | tf_op jit(solution)/shard_map/ppermute | solution.py:307
  14.1 9.0 %collective-permute-start.4 = (bf16[672,256]{1,0:T(8,128)(2,1)S(1)}, bf16[672,256]{1,0:T(8,128)(2,1)S(1)}, u32[]{:S(2)}, u32[]{:S(2)}) collective-permute-start(bf16[672,256]{1,0:T(8,128)(2,1)S(1)} %collective-permute-done.3.refs_4_), channel_id=1, source_target_pairs={{0,2},{1,3},{4,0},{5,1},{8,4},{9,5},{12,8},{13,9},{14,12},{15,13},... | collective-permute-start | bytes 1032200 | tf_op jit(solution)/shard_map/ppermute | solution.py:307
  14.4 2.5 %copy-start.5 = (s32[4]{0:T(128)S(1)}, s32[4]{0:T(128)}, u32[]{:S(2)}) copy-start(s32[4]{0:T(128)} %donors_ref.1) | copy-start | bytes 52
  14.4 13.4 %collective-permute-start.6 = (bf16[704,256]{1,0:T(8,128)(2,1)S(1)}, bf16[704,256]{1,0:T(8,128)(2,1)S(1)}, u32[]{:S(2)}, u32[]{:S(2)}) collective-permute-start(bf16[704,256]{1,0:T(8,128)(2,1)S(1)} %pad_maximum_fusion), channel_id=1, source_target_pairs={{0,16},{1,17},{2,18},{3,19},{4,20},{5,21},{6,22},{7,23},{8,24},{9,... | collective-permute-start | bytes 1081352 | tf_op jit(solution)/shard_map/ppermute | solution.py:307
  21.5 8.3 %collective-permute-start.2 = (bf16[672,256]{1,0:T(8,128)(2,1)S(1)}, bf16[672,256]{1,0:T(8,128)(2,1)S(1)}, u32[]{:S(2)}, u32[]{:S(2)}) collective-permute-start(bf16[672,256]{1,0:T(8,128)(2,1)S(1)} %collective-permute-done.1.refs_2_), channel_id=1, source_target_pairs={{0,4},{1,5},{4,8},{5,9},{8,12},{9,13},{12,14},{13,15},{14,10},{15,... | collective-permute-start | bytes 1032200 | tf_op jit(solution)/shard_map/ppermute | solution.py:307
  23.1 7.8 %collective-permute-start.5 = (bf16[672,256]{1,0:T(8,128)(2,1)S(1)}, bf16[672,256]{1,0:T(8,128)(2,1)S(1)}, u32[]{:S(2)}, u32[]{:S(2)}) collective-permute-start(bf16[672,256]{1,0:T(8,128)(2,1)S(1)} %collective-permute-done.4.refs_3_), channel_id=1, source_target_pairs={{0,2},{1,3},{4,0},{5,1},{8,4},{9,5},{12,8},{13,9},{14,12},{15,13},... | collective-permute-start | bytes 1032200 | tf_op jit(solution)/shard_map/ppermute | solution.py:307
  23.6 12.6 %collective-permute-start.9 = (bf16[704,256]{1,0:T(8,128)(2,1)S(1)}, bf16[704,256]{1,0:T(8,128)(2,1)S(1)}, u32[]{:S(2)}, u32[]{:S(2)}) collective-permute-start(bf16[704,256]{1,0:T(8,128)(2,1)S(1)} %pad_maximum_fusion.1), channel_id=1, source_target_pairs={{0,16},{1,17},{2,18},{3,19},{4,20},{5,21},{6,22},{7,23},{8,24},{9,... | collective-permute-start | bytes 1081352 | tf_op jit(solution)/shard_map/ppermute | solution.py:307
  31.0 3.6 %copy-start.3 = (bf16[1024,256]{1,0:T(8,128)(2,1)S(1)}, bf16[1024,256]{1,0:T(8,128)(2,1)}, u32[]{:S(2)}) copy-start(bf16[1024,256]{1,0:T(8,128)(2,1)} %refs_2_.7) | copy-start | bytes 1572868
  31.0 9.0 %collective-permute-start.10 = (bf16[704,256]{1,0:T(8,128)(2,1)S(1)}, bf16[704,256]{1,0:T(8,128)(2,1)S(1)}, u32[]{:S(2)}, u32[]{:S(2)}) collective-permute-start(bf16[704,256]{1,0:T(8,128)(2,1)S(1)} %pad_maximum_fusion.2), channel_id=1, source_target_pairs={{0,16},{1,17},{2,18},{3,19},{4,20},{5,21},{6,22},{7,23},{8,24},{9,... | collective-permute-start | bytes 1081352 | tf_op jit(solution)/shard_map/ppermute | solution.py:307
  32.6 6.4 %collective-permute-start.7 = (bf16[512,256]{1,0:T(8,128)(2,1)S(1)}, bf16[512,256]{1,0:T(8,128)(2,1)S(1)}, u32[]{:S(2)}, u32[]{:S(2)}) collective-permute-start(bf16[512,256]{1,0:T(8,128)(2,1)S(1)} %slice.34), channel_id=1, source_target_pairs={{0,4},{1,5},{4,8},{5,9},{8,12},{9,13},{12,14},{13,15},{14,10},{15,... | collective-permute-start | bytes 786440 | tf_op jit(solution)/shard_map/ppermute | solution.py:307
  33.1 6.4 %collective-permute-start.8 = (bf16[512,256]{1,0:T(8,128)(2,1)S(1)}, bf16[512,256]{1,0:T(8,128)(2,1)S(1)}, u32[]{:S(2)}, u32[]{:S(2)}) collective-permute-start(bf16[512,256]{1,0:T(8,128)(2,1)S(1)} %slice.35), channel_id=1, source_target_pairs={{0,2},{1,3},{4,0},{5,1},{8,4},{9,5},{12,8},{13,9},{14,12},{15,13},... | collective-permute-start | bytes 786440 | tf_op jit(solution)/shard_map/ppermute | solution.py:307
  35.6 5.4 %collective-permute-start.14 = (bf16[3,512,256]{2,1,0:T(8,128)(2,1)S(1)}, bf16[3,512,256]{2,1,0:T(8,128)(2,1)S(1)}, u32[]{:S(2)}, u32[]{:S(2)}) collective-permute-start(bf16[3,512,256]{2,1,0:T(8,128)(2,1)S(1)} %shard_map.81.refs_0_), channel_id=1, source_target_pairs={{0,1},{1,0},{2,3},{3,2},{4,5},{5,4},{6,7},{7,6},{8,9},{9,8},{10,11... | collective-permute-start | bytes 2359304 | tf_op jit(solution)/shard_map/ppermute | solution.py:307
  40.4 2.7 %collective-permute-start.12 = (bf16[2,512,256]{2,1,0:T(8,128)(2,1)S(1)}, bf16[2,512,256]{2,1,0:T(8,128)(2,1)S(1)}, u32[]{:S(2)}, u32[]{:S(2)}) collective-permute-start(bf16[2,512,256]{2,1,0:T(8,128)(2,1)S(1)} %shard_map.80.refs_2_), channel_id=1, source_target_pairs={{0,1},{1,0},{2,3},{3,2},{4,5},{5,4},{6,7},{7,6},{8,9},{9,8},{10,11... | collective-permute-start | bytes 1572872 | tf_op jit(solution)/shard_map/ppermute | solution.py:307
  40.5 2.3 %collective-permute-start.13 = (bf16[1,512,256]{2,1,0:T(8,128)(2,1)S(1)}, bf16[1,512,256]{2,1,0:T(8,128)(2,1)S(1)}, u32[]{:S(2)}, u32[]{:S(2)}) collective-permute-start(bf16[1,512,256]{2,1,0:T(8,128)(2,1)S(1)} %shard_map.79.refs_1_), channel_id=1, source_target_pairs={{0,1},{1,0},{2,3},{3,2},{4,5},{5,4},{6,7},{7,6},{8,9},{9,8},{10,11... | collective-permute-start | bytes 786440 | tf_op jit(solution)/shard_map/ppermute | solution.py:307
  41.0 2.1 %collective-permute-start.11 = (bf16[1,512,256]{2,1,0:T(8,128)(2,1)S(1)}, bf16[1,512,256]{2,1,0:T(8,128)(2,1)S(1)}, u32[]{:S(2)}, u32[]{:S(2)}) collective-permute-start(bf16[1,512,256]{2,1,0:T(8,128)(2,1)S(1)} %get-tuple-element.43), channel_id=1, source_target_pairs={{0,1},{1,0},{2,3},{3,2},{4,5},{5,4},{6,7},{7,6},{8,9},{9,8},{10,11... | collective-permute-start | bytes 786440 | tf_op jit(solution)/shard_map/ppermute | solution.py:307

commit v10 on v9

--- a/solution.py
+++ b/solution.py
@@ -161,11 +161,14 @@
     return jnp.where(place < 4, 2 * place, 2 * (7 - place) + 1)
 
 
-def project_kernel(plan, n_context, n_weights, choice, *refs):
+def project_kernel(plan, n_context, n_weights, choice, taken, *refs):
     context = refs[:n_context]
     weights = refs[n_context : n_context + n_weights]
     n_out = 2 if choice else 1
     bases, out_ref = refs[n_context + n_weights : -n_out], refs[-n_out]
+    if taken:
+        out_ref[len(plan)] = bases[-1][0]
+        bases = bases[:-1]
     for slot, products in enumerate(plan):
         total = bases[0][slot] if bases and slot < bases[0].shape[0] else None
         for source, column, pieces in products:
@@ -185,17 +188,17 @@
                 refs[-1][0] = total.astype(out_ref.dtype)
 
 
-def project(context, weights, plan, kind, bases=(), choice=None):
+def project(context, weights, plan, kind, bases=(), choice=None, taken=()):
     rows = context[0].shape[0]
     depth = sum(piece[-1] for block in plan for product in block for piece in product[-1])
     vmem = pl.BlockSpec(memory_space=pltpu.VMEM)
     return pl.pallas_call(
-        functools.partial(project_kernel, plan, len(context), len(weights), choice),
+        functools.partial(project_kernel, plan, len(context), len(weights), choice, bool(taken)),
         out_shape=[
             jax.ShapeDtypeStruct((blocks, rows, CHUNK), kind)
-            for blocks in ((len(plan), 1) if choice else (len(plan),))
+            for blocks in ((len(plan), 1) if choice else (len(plan) + len(taken),))
         ],
-        in_specs=[vmem] * (len(context) + len(weights) + len(bases)),
+        in_specs=[vmem] * (len(context) + len(weights) + len(bases) + len(taken)),
         out_specs=[vmem] * (2 if choice else 1),
         compiler_params=pltpu.CompilerParams(vmem_limit_bytes=12 << 20),
         cost_estimate=pl.CostEstimate(
@@ -203,7 +206,7 @@
             bytes_accessed=2 * (len(plan) * rows * CHUNK + depth * CHUNK),
             transcendentals=0,
         ),
-    )(*context, *weights, *bases)
+    )(*context, *weights, *bases, *taken)
 
 
 def live_kernel(counts_ref, donors_ref, after_ref, out_ref):
@@ -235,8 +238,7 @@
     tensor = lax.axis_index("tensor")
     steps = []
     for array, group in enumerate(distances):
-        several = other[array].shape[0] > 1
-        for slot, distance in enumerate(group):
+        for slot, (distance, theirs) in enumerate(group):
             at = len(steps)
             block = block_of(distance)
             column = pl.multiple_of(block % 4 * CHUNK, CHUNK)
@@ -254,7 +256,7 @@
             def _():
                 for passage in range(slots):
                     rows = slice(passage * tokens, (passage + 1) * tokens)
-                    both = kept[array][slot, rows] + other[array][slot if several else 0, rows]
+                    both = kept[array][slot, rows] + other[array][theirs, rows]
                     live = live_ref[passage * LIVE_ROWS : passage * LIVE_ROWS + 1]
                     buffer[at, passage] = both * jnp.broadcast_to(live, both.shape)
                     copies[passage].start()
@@ -347,16 +349,15 @@
     (started,) = project(context, (p3, q3), [p_part, q_part], jnp.float32)
     p4, q4, e2, s2, started = barrier((p4, q4, e2, s2, started))
 
-    (e4,) = project(context, (p4, q4), [opposite], jnp.bfloat16)
-    x1, x2, x4 = send(e1, cores), send(s2, cores), send(e4, cores)
+    (e4,) = project(context, (p4, q4), [opposite], jnp.bfloat16, taken=(s2,))
+    x1, x4 = send(e1, cores), send(e4, cores)
     y3, e4 = barrier((y3, e4))
     (e3,) = project(context, (p3, q3, y3), [p_rest, q_rest], jnp.bfloat16, (started,))
     x3 = send(e3, cores)
-    early = finish((e1,), (x1,), ((0, 1, -1),), live, slots)
-    x2, x3, x4, early = barrier((x2, x3, x4, early))
-    return finish(
-        (e2, e4, e3), (x2, x4, x3), ((2, -2), (4,), (3, -3)), live, slots, (early,)
-    )
+    first = (((0, 0), (1, 1), (-1, 2)), ((2, 1), (-2, 1)), ((4, 0),))
+    early = finish((e1, e2, e4), (x1, x4, x4), first, live, slots)
+    x3, early = barrier((x3, early))
+    return finish((e3,), (x3,), (((3, 0), (-3, 1)),), live, slots, (early,))
 
 
 def with_gather(queries, key_rows, values, position_bias, out_weight, counts, donors):

time: 44.2 us -> 43.6 us (0.986)
  Pallas kernels: 16.2 us -> 15.7 us
    pallas_call x2, Pallas kernels: 1.75 us -> 1.18 us  [finish(): pl.pallas_call(functools.partial(finish_kernel, distances), out_shape=jax...]
    ppermute x15 -> x14, waiting for transfers between devices: 8.1 us -> 7.86 us  [with_ring(): send = lambda value, pairs: lax.ppermute(value, AXES, pairs)]
    ppermute x15 -> x14, starting transfers between devices: 14.9 us -> 14.8 us  [with_ring(): send = lambda value, pairs: lax.ppermute(value, AXES, pairs)]
  transfers between devices with their start and end apart: 15 -> 14, of which waited for: 8 -> 7; matrix products, arithmetic and copies ran while one was open for 0% -> 0% of each run, Pallas kernels for 35% -> 36%
where the time goes in v10:
time: 43.6 us; the launch traced here: 43.1 us
  Pallas kernels  15.7 us (36%)
  starting transfers between devices  14.8 us (34%)
  waiting for transfers between devices  7.86 us (18%)
  local copies, waits for them, and re-layouts  3.8 us (9%)
  between operations  0.89 us (2%)
    ppermute x14, starting transfers between devices, with_ring(): send = lambda value, pairs: lax.ppermute(value, AXES, pairs)  14.8 us
    pallas_call x3, Pallas kernels, attend(): pl.pallas_call(functools.partial(attention_kernel, first, joined), out_sh...  10.1 us
    ppermute x14, waiting for transfers between devices, with_ring(): send = lambda value, pairs: lax.ppermute(value, AXES, pairs)  7.86 us
    pallas_call x5, Pallas kernels, project(): pl.pallas_call(functools.partial(project_kernel, plan, len(context), len(...  3.8 us
    unnamed x12, local copies, waits for them, and re-layouts  2.46 us
    slice x1, local copies, waits for them, and re-layouts, with_ring(): p1, q1 = (send(out_weight[:-cut], ahead), send(out_weight[cut:], back))  1.22 us
    pallas_call x2, Pallas kernels, finish(): pl.pallas_call(functools.partial(finish_kernel, distances), out_shape=jax...  1.18 us
  transfers between devices with their start and end apart: 14, of which 7 were waited for; matrix products, arithmetic and copies ran while one was open for 0% of the time, Pallas kernels for 36%

profile of v10, /device:TPU:0, one launch (start us, length us, event | category | flops | bytes accessed | tf_op | source)
XLA Modules:
  0.0 43.1 jit_solution(12105094492957960042)
XLA Ops:
  0.0 1.2 %fusion = (bf16[672,256]{1,0:T(8,128)(2,1)S(1)}, bf16[672,256]{1,0:T(8,128)(2,1)S(1)}) fusion(bf16[1024,256]{1,0:T(8,128)(2,1)} %refs_2_.7), kind=kLoop, calls=%fused_computation.3 | loop fusion | bytes 1376256 | tf_op jit(solution)/shard_map/slice | solution.py:318
  1.2 3.1 %collective-permute-start = (bf16[672,256]{1,0:T(8,128)(2,1)S(1)}, bf16[672,256]{1,0:T(8,128)(2,1)S(1)}, u32[]{:S(2)}, u32[]{:S(2)}) collective-permute-start(bf16[672,256]{1,0:T(8,128)(2,1)S(1)} %get-tuple-element.46), channel_id=1, source_target_pairs={{0,4},{1,5},{4,8},{5,9},{8,12},{9,13},{12,14},{13,15},{14,10},{15,... | collective-permute-start | bytes 1032200 | tf_op jit(solution)/shard_map/ppermute | solution.py:309
  4.3 1.2 %copy-done.1 = bf16[2,256,1024]{2,1,0:T(8,128)(2,1)S(1)} copy-done((bf16[2,256,1024]{2,1,0:T(8,128)(2,1)S(1)}, bf16[2,256,1024]{2,1,0:T(8,128)(2,1)}, u32[]{:S(2)}) %copy-start.1) | copy-done | bytes 1048600
  5.5 1.2 %copy-done.2 = bf16[2,256,1024]{2,1,0:T(8,128)(2,1)S(1)} copy-done((bf16[2,256,1024]{2,1,0:T(8,128)(2,1)S(1)}, bf16[2,256,1024]{2,1,0:T(8,128)(2,1)}, u32[]{:S(2)}) %copy-start.2) | copy-done | bytes 1048600
  6.8 5.0 %shard_map.73.refs_3_.after_ref.refs_0_ = bf16[512,512]{1,0:T(8,128)(2,1)S(1)} custom-call(f32[16,32]{1,0:T(8,128)S(1)} %bitcast.1, bf16[2,256,1024]{2,1,0:T(8,128)(2,1)S(1)} %copy-done, bf16[2,256,1024]{2,1,0:T(8,128)(2,1)S(1)} %copy-done.1, bf16[2,256,1024]{2,1,0:T(8,128)(2,1)S(1)} %copy-done.2), custom_call_target="tpu_custom_call" | custom-call | flops 268435456 | bytes 2097152 | tf_op jit(solution)/shard_map/pallas_call | solution.py:112
  12.3 1.8 %collective-permute-start.1 = (bf16[672,256]{1,0:T(8,128)(2,1)S(1)}, bf16[672,256]{1,0:T(8,128)(2,1)S(1)}, u32[]{:S(2)}, u32[]{:S(2)}) collective-permute-start(bf16[672,256]{1,0:T(8,128)(2,1)S(1)} %collective-permute-done.refs_3_), channel_id=1, source_target_pairs={{0,4},{1,5},{4,8},{5,9},{8,12},{9,13},{12,14},{13,15},{14,10},{15,... | collective-permute-start | bytes 1032200 | tf_op jit(solution)/shard_map/ppermute | solution.py:309
  14.4 1.8 %collective-permute-start.6 = (bf16[704,256]{1,0:T(8,128)(2,1)S(1)}, bf16[704,256]{1,0:T(8,128)(2,1)S(1)}, u32[]{:S(2)}, u32[]{:S(2)}) collective-permute-start(bf16[704,256]{1,0:T(8,128)(2,1)S(1)} %pad_maximum_fusion), channel_id=1, source_target_pairs={{0,16},{1,17},{2,18},{3,19},{4,20},{5,21},{6,22},{7,23},{8,24},{9,... | collective-permute-start | bytes 1081352 | tf_op jit(solution)/shard_map/ppermute | solution.py:309
  16.9 0.6 %shard_map.75.live_ref = bf16[32,256]{1,0:T(8,128)(2,1)S(1)} custom-call(s32[1]{0:T(128)S(6)} %copy.10.counts_ref, s32[4]{0:T(128)S(1)} %copy-done.5, bf16[512,512]{1,0:T(8,128)(2,1)S(1)} %shard_map.73.refs_3_.after_ref.refs_0_), custom_call_target="tpu_custom_call" | custom-call | tf_op jit(solution)/shard_map/pallas_call | solution.py:224
  17.4 2.6 %shard_map.74.refs_3_ = bf16[512,256]{1,0:T(8,128)(2,1)S(1)} custom-call(f32[16,32]{1,0:T(8,128)S(1)} %bitcast.2, bf16[2,256,1024]{2,1,0:T(8,128)(2,1)S(1)} %copy-done, bf16[2,256,1024]{2,1,0:T(8,128)(2,1)S(1)} %copy-done.1, bf16[2,256,1024]{2,1,0:T(8,128)(2,1)S(1)} %copy-done.2, bf16[512,512]{1,0:T(8,128)(2,1)S(1)} %shard_map.73.refs_3_.after_ref.refs_0_), custom_call_target="tpu_custom_call" | custom-call | flops 134217728 | bytes 1048576 | tf_op jit(solution)/shard_map/pallas_call | solution.py:112
  20.0 1.5 %collective-permute-done.1.refs_2_ = bf16[672,256]{1,0:T(8,128)(2,1)S(1)} collective-permute-done((bf16[672,256]{1,0:T(8,128)(2,1)S(1)}, bf16[672,256]{1,0:T(8,128)(2,1)S(1)}, u32[]{:S(2)}, u32[]{:S(2)}) %collective-permute-start.1) | collective-permute-done | bytes 344096 | tf_op jit(solution)/shard_map/ppermute | solution.py:309
  21.5 1.6 %collective-permute-start.2 = (bf16[672,256]{1,0:T(8,128)(2,1)S(1)}, bf16[672,256]{1,0:T(8,128)(2,1)S(1)}, u32[]{:S(2)}, u32[]{:S(2)}) collective-permute-start(bf16[672,256]{1,0:T(8,128)(2,1)S(1)} %collective-permute-done.1.refs_2_), channel_id=1, source_target_pairs={{0,4},{1,5},{4,8},{5,9},{8,12},{9,13},{12,14},{13,15},{14,10},{15,... | collective-permute-start | bytes 1032200 | tf_op jit(solution)/shard_map/ppermute | solution.py:309
  23.6 1.6 %collective-permute-start.10 = (bf16[704,256]{1,0:T(8,128)(2,1)S(1)}, bf16[704,256]{1,0:T(8,128)(2,1)S(1)}, u32[]{:S(2)}, u32[]{:S(2)}) collective-permute-start(bf16[704,256]{1,0:T(8,128)(2,1)S(1)} %pad_maximum_fusion.2), channel_id=1, source_target_pairs={{0,16},{1,17},{2,18},{3,19},{4,20},{5,21},{6,22},{7,23},{8,24},{9,... | collective-permute-start | bytes 1081352 | tf_op jit(solution)/shard_map/ppermute | solution.py:309
  25.2 2.6 %shard_map.76.refs_1_ = bf16[512,512]{1,0:T(8,128)(2,1)S(1)} custom-call(f32[16,32]{1,0:T(8,128)S(1)} %bitcast.3, bf16[2,256,1024]{2,1,0:T(8,128)(2,1)S(1)} %copy-done, bf16[2,256,1024]{2,1,0:T(8,128)(2,1)S(1)} %copy-done.1, bf16[2,256,1024]{2,1,0:T(8,128)(2,1)S(1)} %copy-done.2, bf16[512,256]{1,0:T(8,128)(2,1)S(1)} %shard_map.74.refs_3_), custom_call_target="tpu_custom_call" | custom-call | flops 134217728 | bytes 1048576 | tf_op jit(solution)/shard_map/pallas_call | solution.py:112
  27.8 2.0 %collective-permute-done.2.refs_2_ = bf16[672,256]{1,0:T(8,128)(2,1)S(1)} collective-permute-done((bf16[672,256]{1,0:T(8,128)(2,1)S(1)}, bf16[672,256]{1,0:T(8,128)(2,1)S(1)}, u32[]{:S(2)}, u32[]{:S(2)}) %collective-permute-start.2) | collective-permute-done | bytes 344096 | tf_op jit(solution)/shard_map/ppermute | solution.py:309
  29.9 1.1 %collective-permute-done.5.refs_3_ = bf16[672,256]{1,0:T(8,128)(2,1)S(1)} collective-permute-done((bf16[672,256]{1,0:T(8,128)(2,1)S(1)}, bf16[672,256]{1,0:T(8,128)(2,1)S(1)}, u32[]{:S(2)}, u32[]{:S(2)}) %collective-permute-start.5) | collective-permute-done | bytes 344096 | tf_op jit(solution)/shard_map/ppermute | solution.py:309
  31.0 1.5 %collective-permute-start.7 = (bf16[704,256]{1,0:T(8,128)(2,1)S(1)}, bf16[704,256]{1,0:T(8,128)(2,1)S(1)}, u32[]{:S(2)}, u32[]{:S(2)}) collective-permute-start(bf16[704,256]{1,0:T(8,128)(2,1)S(1)} %pad_maximum_fusion.1), channel_id=1, source_target_pairs={{0,16},{1,17},{2,18},{3,19},{4,20},{5,21},{6,22},{7,23},{8,24},{9,... | collective-permute-start | bytes 1081352 | tf_op jit(solution)/shard_map/ppermute | solution.py:309
  32.6 0.6 %collective-permute-start.8 = (bf16[512,256]{1,0:T(8,128)(2,1)S(1)}, bf16[512,256]{1,0:T(8,128)(2,1)S(1)}, u32[]{:S(2)}, u32[]{:S(2)}) collective-permute-start(bf16[512,256]{1,0:T(8,128)(2,1)S(1)} %slice.36), channel_id=1, source_target_pairs={{0,4},{1,5},{4,8},{5,9},{8,12},{9,13},{12,14},{13,15},{14,10},{15,... | collective-permute-start | bytes 786440 | tf_op jit(solution)/shard_map/ppermute | solution.py:309
  33.1 1.5 %collective-permute-start.9 = (bf16[512,256]{1,0:T(8,128)(2,1)S(1)}, bf16[512,256]{1,0:T(8,128)(2,1)S(1)}, u32[]{:S(2)}, u32[]{:S(2)}) collective-permute-start(bf16[512,256]{1,0:T(8,128)(2,1)S(1)} %slice.37), channel_id=1, source_target_pairs={{0,2},{1,3},{4,0},{5,1},{8,4},{9,5},{12,8},{13,9},{14,12},{15,13},... | collective-permute-start | bytes 786440 | tf_op jit(solution)/shard_map/ppermute | solution.py:309
  34.6 1.0 %shard_map.81.refs_0_ = bf16[3,512,256]{2,1,0:T(8,128)(2,1)S(1)} custom-call(bf16[512,512]{1,0:T(8,128)(2,1)S(1)} %shard_map.73.refs_3_.after_ref.refs_0_, bf16[512,512]{1,0:T(8,128)(2,1)S(1)} %shard_map.76.refs_1_, bf16[1024,256]{1,0:T(8,128)(2,1)S(1)} %copy-done.3, bf16[672,256]{1,0:T(8,128)(2,1)S(1)} %collective-permute-done.refs_3_, ...), custom_call_target="tpu_custom_call" | custom-call | flops 805306368 | bytes 2359296 | tf_op jit(solution)/shard_map/pallas_call | solution.py:195
  35.7 0.6 %shard_map.78.refs_5_ = f32[2,512,256]{2,1,0:T(8,128)S(1)} custom-call(bf16[512,512]{1,0:T(8,128)(2,1)S(1)} %shard_map.73.refs_3_.after_ref.refs_0_, bf16[512,512]{1,0:T(8,128)(2,1)S(1)} %shard_map.76.refs_1_, bf16[672,256]{1,0:T(8,128)(2,1)S(1)} %collective-permute-done.2.refs_2_, bf16[672,256]{1,0:T(8,128)(2,1)S(1)} %collective-permute-done.5.refs_3_), custom_call_target="tpu_custom_call" | custom-call | flops 335544320 | bytes 1179648 | tf_op jit(solution)/shard_map/pallas_call | solution.py:195
  36.3 1.4 %shard_map.77 = (bf16[2,512,256]{2,1,0:T(8,128)(2,1)S(1)}, bf16[1,512,256]{2,1,0:T(8,128)(2,1)S(1)}) custom-call(bf16[512,512]{1,0:T(8,128)(2,1)S(1)} %shard_map.73.refs_3_.after_ref.refs_0_, bf16[512,512]{1,0:T(8,128)(2,1)S(1)} %shard_map.76.refs_1_, bf16[672,256]{1,0:T(8,128)(2,1)S(1)} %collective-permute-done.1.refs_2_, ...), custom_call_target="tpu_custom_call" | custom-call | flops 536870912 | bytes 1572864 | tf_op jit(solution)/shard_map/pallas_call | solution.py:195
  37.7 1.3 %collective-permute-done.8.refs_2_ = bf16[512,256]{1,0:T(8,128)(2,1)S(1)} collective-permute-done((bf16[512,256]{1,0:T(8,128)(2,1)S(1)}, bf16[512,256]{1,0:T(8,128)(2,1)S(1)}, u32[]{:S(2)}, u32[]{:S(2)}) %collective-permute-start.8) | collective-permute-done | bytes 262176 | tf_op jit(solution)/shard_map/ppermute | solution.py:309
  41.0 0.9 %collective-permute-done.13.refs_4_.refs_5_ = bf16[2,512,256]{2,1,0:T(8,128)(2,1)S(1)} collective-permute-done((bf16[2,512,256]{2,1,0:T(8,128)(2,1)S(1)}, bf16[2,512,256]{2,1,0:T(8,128)(2,1)S(1)}, u32[]{:S(2)}, u32[]{:S(2)}) %collective-permute-start.13) | collective-permute-done | bytes 524320 | tf_op jit(solution)/shard_map/ppermute | solution.py:309
  41.9 1.1 %shard_map.82.refs_2_ = bf16[2,256,1024]{2,1,0:T(8,128)(2,1)} custom-call(bf16[32,256]{1,0:T(8,128)(2,1)S(1)} %shard_map.75.live_ref, bf16[3,512,256]{2,1,0:T(8,128)(2,1)S(1)} %shard_map.81.refs_0_, bf16[2,512,256]{2,1,0:T(8,128)(2,1)S(1)} %get-tuple-element.41.refs_1_, bf16[2,512,256]{2,1,0:T(8,128)(2,1)S(1)} %shard_map.79.refs_2_, ...), custom_call_target="tpu_custom_call" | custom-call | flops 786432 | bytes 2359296 | tf_op jit(solution)/shard_map/pallas_call | solution.py:279
  (39 shorter events, 3.6 us)
Async XLA Ops:
  0.0 4.3 %copy-start = (bf16[2,256,1024]{2,1,0:T(8,128)(2,1)S(1)}, bf16[2,256,1024]{2,1,0:T(8,128)(2,1)}, u32[]{:S(2)}) copy-start(bf16[2,256,1024]{2,1,0:T(8,128)(2,1)} %refs_0_.5) | copy-start | bytes 3145732
  0.0 4.3 %copy-start.4 = (f32[32,16]{0,1:T(8,128)S(1)}, f32[32,16]{0,1:T(8,128)}, u32[]{:S(2)}) copy-start(f32[32,16]{0,1:T(8,128)} %param.10) | copy-start | bytes 6148
  1.2 11.1 %collective-permute-start = (bf16[672,256]{1,0:T(8,128)(2,1)S(1)}, bf16[672,256]{1,0:T(8,128)(2,1)S(1)}, u32[]{:S(2)}, u32[]{:S(2)}) collective-permute-start(bf16[672,256]{1,0:T(8,128)(2,1)S(1)} %get-tuple-element.46), channel_id=1, source_target_pairs={{0,4},{1,5},{4,8},{5,9},{8,12},{9,13},{12,14},{13,15},{14,10},{15,... | collective-permute-start | bytes 1032200 | tf_op jit(solution)/shard_map/ppermute | solution.py:309
  4.3 9.8 %collective-permute-start.3 = (bf16[672,256]{1,0:T(8,128)(2,1)S(1)}, bf16[672,256]{1,0:T(8,128)(2,1)S(1)}, u32[]{:S(2)}, u32[]{:S(2)}) collective-permute-start(bf16[672,256]{1,0:T(8,128)(2,1)S(1)} %get-tuple-element.45), channel_id=1, source_target_pairs={{0,2},{1,3},{4,0},{5,1},{8,4},{9,5},{12,8},{13,9},{14,12},{15,13},... | collective-permute-start | bytes 1032200 | tf_op jit(solution)/shard_map/ppermute | solution.py:309
  4.3 1.2 %copy-start.1 = (bf16[2,256,1024]{2,1,0:T(8,128)(2,1)S(1)}, bf16[2,256,1024]{2,1,0:T(8,128)(2,1)}, u32[]{:S(2)}) copy-start(bf16[2,256,1024]{2,1,0:T(8,128)(2,1)} %refs_1_.5) | copy-start | bytes 3145732
  5.5 1.2 %copy-start.2 = (bf16[2,256,1024]{2,1,0:T(8,128)(2,1)S(1)}, bf16[2,256,1024]{2,1,0:T(8,128)(2,1)}, u32[]{:S(2)}) copy-start(bf16[2,256,1024]{2,1,0:T(8,128)(2,1)} %refs_2_.6) | copy-start | bytes 3145732
  12.3 9.2 %collective-permute-start.1 = (bf16[672,256]{1,0:T(8,128)(2,1)S(1)}, bf16[672,256]{1,0:T(8,128)(2,1)S(1)}, u32[]{:S(2)}, u32[]{:S(2)}) collective-permute-start(bf16[672,256]{1,0:T(8,128)(2,1)S(1)} %collective-permute-done.refs_3_), channel_id=1, source_target_pairs={{0,4},{1,5},{4,8},{5,9},{8,12},{9,13},{12,14},{13,15},{14,10},{15,... | collective-permute-start | bytes 1032200 | tf_op jit(solution)/shard_map/ppermute | solution.py:309
  14.1 9.0 %collective-permute-start.4 = (bf16[672,256]{1,0:T(8,128)(2,1)S(1)}, bf16[672,256]{1,0:T(8,128)(2,1)S(1)}, u32[]{:S(2)}, u32[]{:S(2)}) collective-permute-start(bf16[672,256]{1,0:T(8,128)(2,1)S(1)} %collective-permute-done.3.refs_4_), channel_id=1, source_target_pairs={{0,2},{1,3},{4,0},{5,1},{8,4},{9,5},{12,8},{13,9},{14,12},{15,13},... | collective-permute-start | bytes 1032200 | tf_op jit(solution)/shard_map/ppermute | solution.py:309
  14.4 2.5 %copy-start.5 = (s32[4]{0:T(128)S(1)}, s32[4]{0:T(128)}, u32[]{:S(2)}) copy-start(s32[4]{0:T(128)} %donors_ref.1) | copy-start | bytes 52
  14.4 13.4 %collective-permute-start.6 = (bf16[704,256]{1,0:T(8,128)(2,1)S(1)}, bf16[704,256]{1,0:T(8,128)(2,1)S(1)}, u32[]{:S(2)}, u32[]{:S(2)}) collective-permute-start(bf16[704,256]{1,0:T(8,128)(2,1)S(1)} %pad_maximum_fusion), channel_id=1, source_target_pairs={{0,16},{1,17},{2,18},{3,19},{4,20},{5,21},{6,22},{7,23},{8,24},{9,... | collective-permute-start | bytes 1081352 | tf_op jit(solution)/shard_map/ppermute | solution.py:309
  21.5 8.3 %collective-permute-start.2 = (bf16[672,256]{1,0:T(8,128)(2,1)S(1)}, bf16[672,256]{1,0:T(8,128)(2,1)S(1)}, u32[]{:S(2)}, u32[]{:S(2)}) collective-permute-start(bf16[672,256]{1,0:T(8,128)(2,1)S(1)} %collective-permute-done.1.refs_2_), channel_id=1, source_target_pairs={{0,4},{1,5},{4,8},{5,9},{8,12},{9,13},{12,14},{13,15},{14,10},{15,... | collective-permute-start | bytes 1032200 | tf_op jit(solution)/shard_map/ppermute | solution.py:309
  23.1 7.8 %collective-permute-start.5 = (bf16[672,256]{1,0:T(8,128)(2,1)S(1)}, bf16[672,256]{1,0:T(8,128)(2,1)S(1)}, u32[]{:S(2)}, u32[]{:S(2)}) collective-permute-start(bf16[672,256]{1,0:T(8,128)(2,1)S(1)} %collective-permute-done.4.refs_3_), channel_id=1, source_target_pairs={{0,2},{1,3},{4,0},{5,1},{8,4},{9,5},{12,8},{13,9},{14,12},{15,13},... | collective-permute-start | bytes 1032200 | tf_op jit(solution)/shard_map/ppermute | solution.py:309
  23.6 12.6 %collective-permute-start.10 = (bf16[704,256]{1,0:T(8,128)(2,1)S(1)}, bf16[704,256]{1,0:T(8,128)(2,1)S(1)}, u32[]{:S(2)}, u32[]{:S(2)}) collective-permute-start(bf16[704,256]{1,0:T(8,128)(2,1)S(1)} %pad_maximum_fusion.2), channel_id=1, source_target_pairs={{0,16},{1,17},{2,18},{3,19},{4,20},{5,21},{6,22},{7,23},{8,24},{9,... | collective-permute-start | bytes 1081352 | tf_op jit(solution)/shard_map/ppermute | solution.py:309
  31.0 3.6 %copy-start.3 = (bf16[1024,256]{1,0:T(8,128)(2,1)S(1)}, bf16[1024,256]{1,0:T(8,128)(2,1)}, u32[]{:S(2)}) copy-start(bf16[1024,256]{1,0:T(8,128)(2,1)} %refs_2_.7) | copy-start | bytes 1572868
  31.0 9.0 %collective-permute-start.7 = (bf16[704,256]{1,0:T(8,128)(2,1)S(1)}, bf16[704,256]{1,0:T(8,128)(2,1)S(1)}, u32[]{:S(2)}, u32[]{:S(2)}) collective-permute-start(bf16[704,256]{1,0:T(8,128)(2,1)S(1)} %pad_maximum_fusion.1), channel_id=1, source_target_pairs={{0,16},{1,17},{2,18},{3,19},{4,20},{5,21},{6,22},{7,23},{8,24},{9,... | collective-permute-start | bytes 1081352 | tf_op jit(solution)/shard_map/ppermute | solution.py:309
  32.6 6.4 %collective-permute-start.8 = (bf16[512,256]{1,0:T(8,128)(2,1)S(1)}, bf16[512,256]{1,0:T(8,128)(2,1)S(1)}, u32[]{:S(2)}, u32[]{:S(2)}) collective-permute-start(bf16[512,256]{1,0:T(8,128)(2,1)S(1)} %slice.36), channel_id=1, source_target_pairs={{0,4},{1,5},{4,8},{5,9},{8,12},{9,13},{12,14},{13,15},{14,10},{15,... | collective-permute-start | bytes 786440 | tf_op jit(solution)/shard_map/ppermute | solution.py:309
  33.1 6.4 %collective-permute-start.9 = (bf16[512,256]{1,0:T(8,128)(2,1)S(1)}, bf16[512,256]{1,0:T(8,128)(2,1)S(1)}, u32[]{:S(2)}, u32[]{:S(2)}) collective-permute-start(bf16[512,256]{1,0:T(8,128)(2,1)S(1)} %slice.37), channel_id=1, source_target_pairs={{0,2},{1,3},{4,0},{5,1},{8,4},{9,5},{12,8},{13,9},{14,12},{15,13},... | collective-permute-start | bytes 786440 | tf_op jit(solution)/shard_map/ppermute | solution.py:309
  35.6 5.4 %collective-permute-start.12 = (bf16[3,512,256]{2,1,0:T(8,128)(2,1)S(1)}, bf16[3,512,256]{2,1,0:T(8,128)(2,1)S(1)}, u32[]{:S(2)}, u32[]{:S(2)}) collective-permute-start(bf16[3,512,256]{2,1,0:T(8,128)(2,1)S(1)} %shard_map.81.refs_0_), channel_id=1, source_target_pairs={{0,1},{1,0},{2,3},{3,2},{4,5},{5,4},{6,7},{7,6},{8,9},{9,8},{10,11... | collective-permute-start | bytes 2359304 | tf_op jit(solution)/shard_map/ppermute | solution.py:309
  40.0 2.0 %collective-permute-start.13 = (bf16[2,512,256]{2,1,0:T(8,128)(2,1)S(1)}, bf16[2,512,256]{2,1,0:T(8,128)(2,1)S(1)}, u32[]{:S(2)}, u32[]{:S(2)}) collective-permute-start(bf16[2,512,256]{2,1,0:T(8,128)(2,1)S(1)} %shard_map.79.refs_2_), channel_id=1, source_target_pairs={{0,1},{1,0},{2,3},{3,2},{4,5},{5,4},{6,7},{7,6},{8,9},{9,8},{10,11... | collective-permute-start | bytes 1572872 | tf_op jit(solution)/shard_map/ppermute | solution.py:309
  40.5 2.5 %collective-permute-start.11 = (bf16[2,512,256]{2,1,0:T(8,128)(2,1)S(1)}, bf16[2,512,256]{2,1,0:T(8,128)(2,1)S(1)}, u32[]{:S(2)}, u32[]{:S(2)}) collective-permute-start(bf16[2,512,256]{2,1,0:T(8,128)(2,1)S(1)} %shard_map.80.refs_0_), channel_id=1, source_target_pairs={{0,1},{1,0},{2,3},{3,2},{4,5},{5,4},{6,7},{7,6},{8,9},{9,8},{10,11... | collective-permute-start | bytes 1572872 | tf_op jit(solution)/shard_map/ppermute | solution.py:309

commit v11 on v10

--- a/solution.py
+++ b/solution.py
@@ -308,7 +308,7 @@
     ]
     send = lambda value, pairs: lax.ppermute(value, AXES, pairs)
     depth = out_weight.shape[0]
-    half, cut = depth // 2, 11 * depth // 32
+    half, cut = depth // 2, 23 * depth // 64
     over = half - cut
     lead = over // 128 * 128
     spill = over - lead

time: 43.6 us -> 43.5 us (level)
  transfers between devices with their start and end apart: 14 -> 14, of which waited for: 7 -> 8; matrix products, arithmetic and copies ran while one was open for 0% -> 0% of each run, Pallas kernels for 36% -> 36%
where the time goes in v11:
time: 43.5 us; the launch traced here: 43 us
  Pallas kernels  15.7 us (36%)
  starting transfers between devices  14.9 us (34%)
  waiting for transfers between devices  7.58 us (17%)
  local copies, waits for them, and re-layouts  3.79 us (9%)
  between operations  0.89 us (2%)
    ppermute x14, starting transfers between devices, with_ring(): send = lambda value, pairs: lax.ppermute(value, AXES, pairs)  14.9 us
    pallas_call x3, Pallas kernels, attend(): pl.pallas_call(functools.partial(attention_kernel, first, joined), out_sh...  10.1 us
    ppermute x14, waiting for transfers between devices, with_ring(): send = lambda value, pairs: lax.ppermute(value, AXES, pairs)  7.58 us
    pallas_call x5, Pallas kernels, project(): pl.pallas_call(functools.partial(project_kernel, plan, len(context), len(...  3.81 us
    unnamed x12, local copies, waits for them, and re-layouts  2.46 us
    slice x1, local copies, waits for them, and re-layouts, with_ring(): p1, q1 = (send(out_weight[:-cut], ahead), send(out_weight[cut:], back))  1.21 us
    pallas_call x2, Pallas kernels, finish(): pl.pallas_call(functools.partial(finish_kernel, distances), out_shape=jax...  1.18 us
  transfers between devices with their start and end apart: 14, of which 8 were waited for; matrix products, arithmetic and copies ran while one was open for 0% of the time, Pallas kernels for 36%

profile of v11, /device:TPU:0, one launch (start us, length us, event | category | flops | bytes accessed | tf_op | source)
XLA Modules:
  0.0 43.0 jit_solution(6794644602656977742)
XLA Ops:
  0.0 1.2 %fusion = (bf16[656,256]{1,0:T(8,128)(2,1)S(1)}, bf16[656,256]{1,0:T(8,128)(2,1)S(1)}) fusion(bf16[1024,256]{1,0:T(8,128)(2,1)} %refs_2_.7), kind=kLoop, calls=%fused_computation.3 | loop fusion | bytes 1343488 | tf_op jit(solution)/shard_map/slice | solution.py:318
  1.2 3.1 %collective-permute-start = (bf16[656,256]{1,0:T(8,128)(2,1)S(1)}, bf16[656,256]{1,0:T(8,128)(2,1)S(1)}, u32[]{:S(2)}, u32[]{:S(2)}) collective-permute-start(bf16[656,256]{1,0:T(8,128)(2,1)S(1)} %get-tuple-element.46), channel_id=1, source_target_pairs={{0,4},{1,5},{4,8},{5,9},{8,12},{9,13},{12,14},{13,15},{14,10},{15,... | collective-permute-start | bytes 1007624 | tf_op jit(solution)/shard_map/ppermute | solution.py:309
  4.3 1.2 %copy-done.1 = bf16[2,256,1024]{2,1,0:T(8,128)(2,1)S(1)} copy-done((bf16[2,256,1024]{2,1,0:T(8,128)(2,1)S(1)}, bf16[2,256,1024]{2,1,0:T(8,128)(2,1)}, u32[]{:S(2)}) %copy-start.1) | copy-done | bytes 1048600
  5.5 1.2 %copy-done.2 = bf16[2,256,1024]{2,1,0:T(8,128)(2,1)S(1)} copy-done((bf16[2,256,1024]{2,1,0:T(8,128)(2,1)S(1)}, bf16[2,256,1024]{2,1,0:T(8,128)(2,1)}, u32[]{:S(2)}) %copy-start.2) | copy-done | bytes 1048600
  6.8 5.0 %shard_map.73.refs_3_.after_ref.refs_0_ = bf16[512,512]{1,0:T(8,128)(2,1)S(1)} custom-call(f32[16,32]{1,0:T(8,128)S(1)} %bitcast.1, bf16[2,256,1024]{2,1,0:T(8,128)(2,1)S(1)} %copy-done, bf16[2,256,1024]{2,1,0:T(8,128)(2,1)S(1)} %copy-done.1, bf16[2,256,1024]{2,1,0:T(8,128)(2,1)S(1)} %copy-done.2), custom_call_target="tpu_custom_call" | custom-call | flops 268435456 | bytes 2097152 | tf_op jit(solution)/shard_map/pallas_call | solution.py:112
  12.1 1.8 %collective-permute-start.1 = (bf16[656,256]{1,0:T(8,128)(2,1)S(1)}, bf16[656,256]{1,0:T(8,128)(2,1)S(1)}, u32[]{:S(2)}, u32[]{:S(2)}) collective-permute-start(bf16[656,256]{1,0:T(8,128)(2,1)S(1)} %collective-permute-done.refs_3_), channel_id=1, source_target_pairs={{0,4},{1,5},{4,8},{5,9},{8,12},{9,13},{12,14},{13,15},{14,10},{15,... | collective-permute-start | bytes 1007624 | tf_op jit(solution)/shard_map/ppermute | solution.py:309
  14.2 1.8 %collective-permute-start.6 = (bf16[736,256]{1,0:T(8,128)(2,1)S(1)}, bf16[736,256]{1,0:T(8,128)(2,1)S(1)}, u32[]{:S(2)}, u32[]{:S(2)}) collective-permute-start(bf16[736,256]{1,0:T(8,128)(2,1)S(1)} %pad_maximum_fusion), channel_id=1, source_target_pairs={{0,16},{1,17},{2,18},{3,19},{4,20},{5,21},{6,22},{7,23},{8,24},{9,... | collective-permute-start | bytes 1130504 | tf_op jit(solution)/shard_map/ppermute | solution.py:309
  16.7 0.6 %shard_map.75.live_ref = bf16[32,256]{1,0:T(8,128)(2,1)S(1)} custom-call(s32[1]{0:T(128)S(6)} %copy.10.counts_ref, s32[4]{0:T(128)S(1)} %copy-done.5, bf16[512,512]{1,0:T(8,128)(2,1)S(1)} %shard_map.73.refs_3_.after_ref.refs_0_), custom_call_target="tpu_custom_call" | custom-call | tf_op jit(solution)/shard_map/pallas_call | solution.py:224
  17.3 2.6 %shard_map.74.refs_3_ = bf16[512,256]{1,0:T(8,128)(2,1)S(1)} custom-call(f32[16,32]{1,0:T(8,128)S(1)} %bitcast.2, bf16[2,256,1024]{2,1,0:T(8,128)(2,1)S(1)} %copy-done, bf16[2,256,1024]{2,1,0:T(8,128)(2,1)S(1)} %copy-done.1, bf16[2,256,1024]{2,1,0:T(8,128)(2,1)S(1)} %copy-done.2, bf16[512,512]{1,0:T(8,128)(2,1)S(1)} %shard_map.73.refs_3_.after_ref.refs_0_), custom_call_target="tpu_custom_call" | custom-call | flops 134217728 | bytes 1048576 | tf_op jit(solution)/shard_map/pallas_call | solution.py:112
  19.8 1.3 %collective-permute-done.1.refs_2_ = bf16[656,256]{1,0:T(8,128)(2,1)S(1)} collective-permute-done((bf16[656,256]{1,0:T(8,128)(2,1)S(1)}, bf16[656,256]{1,0:T(8,128)(2,1)S(1)}, u32[]{:S(2)}, u32[]{:S(2)}) %collective-permute-start.1) | collective-permute-done | bytes 335904 | tf_op jit(solution)/shard_map/ppermute | solution.py:309
  21.2 1.7 %collective-permute-start.2 = (bf16[656,256]{1,0:T(8,128)(2,1)S(1)}, bf16[656,256]{1,0:T(8,128)(2,1)S(1)}, u32[]{:S(2)}, u32[]{:S(2)}) collective-permute-start(bf16[656,256]{1,0:T(8,128)(2,1)S(1)} %collective-permute-done.1.refs_2_), channel_id=1, source_target_pairs={{0,4},{1,5},{4,8},{5,9},{8,12},{9,13},{12,14},{13,15},{14,10},{15,... | collective-permute-start | bytes 1007624 | tf_op jit(solution)/shard_map/ppermute | solution.py:309
  23.3 1.7 %collective-permute-start.10 = (bf16[736,256]{1,0:T(8,128)(2,1)S(1)}, bf16[736,256]{1,0:T(8,128)(2,1)S(1)}, u32[]{:S(2)}, u32[]{:S(2)}) collective-permute-start(bf16[736,256]{1,0:T(8,128)(2,1)S(1)} %pad_maximum_fusion.2), channel_id=1, source_target_pairs={{0,16},{1,17},{2,18},{3,19},{4,20},{5,21},{6,22},{7,23},{8,24},{9,... | collective-permute-start | bytes 1130504 | tf_op jit(solution)/shard_map/ppermute | solution.py:309
  25.0 2.6 %shard_map.76.refs_1_ = bf16[512,512]{1,0:T(8,128)(2,1)S(1)} custom-call(f32[16,32]{1,0:T(8,128)S(1)} %bitcast.3, bf16[2,256,1024]{2,1,0:T(8,128)(2,1)S(1)} %copy-done, bf16[2,256,1024]{2,1,0:T(8,128)(2,1)S(1)} %copy-done.1, bf16[2,256,1024]{2,1,0:T(8,128)(2,1)S(1)} %copy-done.2, bf16[512,256]{1,0:T(8,128)(2,1)S(1)} %shard_map.74.refs_3_), custom_call_target="tpu_custom_call" | custom-call | flops 134217728 | bytes 1048576 | tf_op jit(solution)/shard_map/pallas_call | solution.py:112
  27.6 1.7 %collective-permute-done.2.refs_2_ = bf16[656,256]{1,0:T(8,128)(2,1)S(1)} collective-permute-done((bf16[656,256]{1,0:T(8,128)(2,1)S(1)}, bf16[656,256]{1,0:T(8,128)(2,1)S(1)}, u32[]{:S(2)}, u32[]{:S(2)}) %collective-permute-start.2) | collective-permute-done | bytes 335904 | tf_op jit(solution)/shard_map/ppermute | solution.py:309
  29.4 1.4 %collective-permute-done.5.refs_3_ = bf16[656,256]{1,0:T(8,128)(2,1)S(1)} collective-permute-done((bf16[656,256]{1,0:T(8,128)(2,1)S(1)}, bf16[656,256]{1,0:T(8,128)(2,1)S(1)}, u32[]{:S(2)}, u32[]{:S(2)}) %collective-permute-start.5) | collective-permute-done | bytes 335904 | tf_op jit(solution)/shard_map/ppermute | solution.py:309
  30.8 1.5 %collective-permute-start.7 = (bf16[736,256]{1,0:T(8,128)(2,1)S(1)}, bf16[736,256]{1,0:T(8,128)(2,1)S(1)}, u32[]{:S(2)}, u32[]{:S(2)}) collective-permute-start(bf16[736,256]{1,0:T(8,128)(2,1)S(1)} %pad_maximum_fusion.1), channel_id=1, source_target_pairs={{0,16},{1,17},{2,18},{3,19},{4,20},{5,21},{6,22},{7,23},{8,24},{9,... | collective-permute-start | bytes 1130504 | tf_op jit(solution)/shard_map/ppermute | solution.py:309
  32.4 0.6 %collective-permute-start.8 = (bf16[512,256]{1,0:T(8,128)(2,1)S(1)}, bf16[512,256]{1,0:T(8,128)(2,1)S(1)}, u32[]{:S(2)}, u32[]{:S(2)}) collective-permute-start(bf16[512,256]{1,0:T(8,128)(2,1)S(1)} %slice.36), channel_id=1, source_target_pairs={{0,4},{1,5},{4,8},{5,9},{8,12},{9,13},{12,14},{13,15},{14,10},{15,... | collective-permute-start | bytes 786440 | tf_op jit(solution)/shard_map/ppermute | solution.py:309
  33.0 1.5 %collective-permute-start.9 = (bf16[512,256]{1,0:T(8,128)(2,1)S(1)}, bf16[512,256]{1,0:T(8,128)(2,1)S(1)}, u32[]{:S(2)}, u32[]{:S(2)}) collective-permute-start(bf16[512,256]{1,0:T(8,128)(2,1)S(1)} %slice.37), channel_id=1, source_target_pairs={{0,2},{1,3},{4,0},{5,1},{8,4},{9,5},{12,8},{13,9},{14,12},{15,13},... | collective-permute-start | bytes 786440 | tf_op jit(solution)/shard_map/ppermute | solution.py:309
  34.5 1.0 %shard_map.81.refs_0_ = bf16[3,512,256]{2,1,0:T(8,128)(2,1)S(1)} custom-call(bf16[512,512]{1,0:T(8,128)(2,1)S(1)} %shard_map.73.refs_3_.after_ref.refs_0_, bf16[512,512]{1,0:T(8,128)(2,1)S(1)} %shard_map.76.refs_1_, bf16[1024,256]{1,0:T(8,128)(2,1)S(1)} %copy-done.3, bf16[656,256]{1,0:T(8,128)(2,1)S(1)} %collective-permute-done.refs_3_, ...), custom_call_target="tpu_custom_call" | custom-call | flops 805306368 | bytes 2359296 | tf_op jit(solution)/shard_map/pallas_call | solution.py:195
  35.5 0.6 %shard_map.78.refs_5_ = f32[2,512,256]{2,1,0:T(8,128)S(1)} custom-call(bf16[512,512]{1,0:T(8,128)(2,1)S(1)} %shard_map.73.refs_3_.after_ref.refs_0_, bf16[512,512]{1,0:T(8,128)(2,1)S(1)} %shard_map.76.refs_1_, bf16[656,256]{1,0:T(8,128)(2,1)S(1)} %collective-permute-done.2.refs_2_, bf16[656,256]{1,0:T(8,128)(2,1)S(1)} %collective-permute-done.5.refs_3_), custom_call_target="tpu_custom_call" | custom-call | flops 335544320 | bytes 1179648 | tf_op jit(solution)/shard_map/pallas_call | solution.py:195
  36.1 1.4 %shard_map.77 = (bf16[2,512,256]{2,1,0:T(8,128)(2,1)S(1)}, bf16[1,512,256]{2,1,0:T(8,128)(2,1)S(1)}) custom-call(bf16[512,512]{1,0:T(8,128)(2,1)S(1)} %shard_map.73.refs_3_.after_ref.refs_0_, bf16[512,512]{1,0:T(8,128)(2,1)S(1)} %shard_map.76.refs_1_, bf16[656,256]{1,0:T(8,128)(2,1)S(1)} %collective-permute-done.1.refs_2_, ...), custom_call_target="tpu_custom_call" | custom-call | flops 536870912 | bytes 1572864 | tf_op jit(solution)/shard_map/pallas_call | solution.py:195
  37.5 1.3 %collective-permute-done.8.refs_2_ = bf16[512,256]{1,0:T(8,128)(2,1)S(1)} collective-permute-done((bf16[512,256]{1,0:T(8,128)(2,1)S(1)}, bf16[512,256]{1,0:T(8,128)(2,1)S(1)}, u32[]{:S(2)}, u32[]{:S(2)}) %collective-permute-start.8) | collective-permute-done | bytes 262176 | tf_op jit(solution)/shard_map/ppermute | solution.py:309
  40.9 0.9 %collective-permute-done.13.refs_4_.refs_5_ = bf16[2,512,256]{2,1,0:T(8,128)(2,1)S(1)} collective-permute-done((bf16[2,512,256]{2,1,0:T(8,128)(2,1)S(1)}, bf16[2,512,256]{2,1,0:T(8,128)(2,1)S(1)}, u32[]{:S(2)}, u32[]{:S(2)}) %collective-permute-start.13) | collective-permute-done | bytes 524320 | tf_op jit(solution)/shard_map/ppermute | solution.py:309
  41.8 1.1 %shard_map.82.refs_2_ = bf16[2,256,1024]{2,1,0:T(8,128)(2,1)} custom-call(bf16[32,256]{1,0:T(8,128)(2,1)S(1)} %shard_map.75.live_ref, bf16[3,512,256]{2,1,0:T(8,128)(2,1)S(1)} %shard_map.81.refs_0_, bf16[2,512,256]{2,1,0:T(8,128)(2,1)S(1)} %get-tuple-element.41.refs_1_, bf16[2,512,256]{2,1,0:T(8,128)(2,1)S(1)} %shard_map.79.refs_2_, ...), custom_call_target="tpu_custom_call" | custom-call | flops 786432 | bytes 2359296 | tf_op jit(solution)/shard_map/pallas_call | solution.py:279
  (39 shorter events, 3.3 us)
Async XLA Ops:
  0.0 4.3 %copy-start = (bf16[2,256,1024]{2,1,0:T(8,128)(2,1)S(1)}, bf16[2,256,1024]{2,1,0:T(8,128)(2,1)}, u32[]{:S(2)}) copy-start(bf16[2,256,1024]{2,1,0:T(8,128)(2,1)} %refs_0_.5) | copy-start | bytes 3145732
  0.0 4.3 %copy-start.4 = (f32[32,16]{0,1:T(8,128)S(1)}, f32[32,16]{0,1:T(8,128)}, u32[]{:S(2)}) copy-start(f32[32,16]{0,1:T(8,128)} %param.10) | copy-start | bytes 6148
  1.2 10.9 %collective-permute-start = (bf16[656,256]{1,0:T(8,128)(2,1)S(1)}, bf16[656,256]{1,0:T(8,128)(2,1)S(1)}, u32[]{:S(2)}, u32[]{:S(2)}) collective-permute-start(bf16[656,256]{1,0:T(8,128)(2,1)S(1)} %get-tuple-element.46), channel_id=1, source_target_pairs={{0,4},{1,5},{4,8},{5,9},{8,12},{9,13},{12,14},{13,15},{14,10},{15,... | collective-permute-start | bytes 1007624 | tf_op jit(solution)/shard_map/ppermute | solution.py:309
  4.3 9.6 %collective-permute-start.3 = (bf16[656,256]{1,0:T(8,128)(2,1)S(1)}, bf16[656,256]{1,0:T(8,128)(2,1)S(1)}, u32[]{:S(2)}, u32[]{:S(2)}) collective-permute-start(bf16[656,256]{1,0:T(8,128)(2,1)S(1)} %get-tuple-element.45), channel_id=1, source_target_pairs={{0,2},{1,3},{4,0},{5,1},{8,4},{9,5},{12,8},{13,9},{14,12},{15,13},... | collective-permute-start | bytes 1007624 | tf_op jit(solution)/shard_map/ppermute | solution.py:309
  4.3 1.2 %copy-start.1 = (bf16[2,256,1024]{2,1,0:T(8,128)(2,1)S(1)}, bf16[2,256,1024]{2,1,0:T(8,128)(2,1)}, u32[]{:S(2)}) copy-start(bf16[2,256,1024]{2,1,0:T(8,128)(2,1)} %refs_1_.5) | copy-start | bytes 3145732
  5.5 1.2 %copy-start.2 = (bf16[2,256,1024]{2,1,0:T(8,128)(2,1)S(1)}, bf16[2,256,1024]{2,1,0:T(8,128)(2,1)}, u32[]{:S(2)}) copy-start(bf16[2,256,1024]{2,1,0:T(8,128)(2,1)} %refs_2_.6) | copy-start | bytes 3145732
  12.1 9.1 %collective-permute-start.1 = (bf16[656,256]{1,0:T(8,128)(2,1)S(1)}, bf16[656,256]{1,0:T(8,128)(2,1)S(1)}, u32[]{:S(2)}, u32[]{:S(2)}) collective-permute-start(bf16[656,256]{1,0:T(8,128)(2,1)S(1)} %collective-permute-done.refs_3_), channel_id=1, source_target_pairs={{0,4},{1,5},{4,8},{5,9},{8,12},{9,13},{12,14},{13,15},{14,10},{15,... | collective-permute-start | bytes 1007624 | tf_op jit(solution)/shard_map/ppermute | solution.py:309
  13.9 9.0 %collective-permute-start.4 = (bf16[656,256]{1,0:T(8,128)(2,1)S(1)}, bf16[656,256]{1,0:T(8,128)(2,1)S(1)}, u32[]{:S(2)}, u32[]{:S(2)}) collective-permute-start(bf16[656,256]{1,0:T(8,128)(2,1)S(1)} %collective-permute-done.3.refs_4_), channel_id=1, source_target_pairs={{0,2},{1,3},{4,0},{5,1},{8,4},{9,5},{12,8},{13,9},{14,12},{15,13},... | collective-permute-start | bytes 1007624 | tf_op jit(solution)/shard_map/ppermute | solution.py:309
  14.2 2.5 %copy-start.5 = (s32[4]{0:T(128)S(1)}, s32[4]{0:T(128)}, u32[]{:S(2)}) copy-start(s32[4]{0:T(128)} %donors_ref.1) | copy-start | bytes 52
  14.2 13.4 %collective-permute-start.6 = (bf16[736,256]{1,0:T(8,128)(2,1)S(1)}, bf16[736,256]{1,0:T(8,128)(2,1)S(1)}, u32[]{:S(2)}, u32[]{:S(2)}) collective-permute-start(bf16[736,256]{1,0:T(8,128)(2,1)S(1)} %pad_maximum_fusion), channel_id=1, source_target_pairs={{0,16},{1,17},{2,18},{3,19},{4,20},{5,21},{6,22},{7,23},{8,24},{9,... | collective-permute-start | bytes 1130504 | tf_op jit(solution)/shard_map/ppermute | solution.py:309
  21.2 8.2 %collective-permute-start.2 = (bf16[656,256]{1,0:T(8,128)(2,1)S(1)}, bf16[656,256]{1,0:T(8,128)(2,1)S(1)}, u32[]{:S(2)}, u32[]{:S(2)}) collective-permute-start(bf16[656,256]{1,0:T(8,128)(2,1)S(1)} %collective-permute-done.1.refs_2_), channel_id=1, source_target_pairs={{0,4},{1,5},{4,8},{5,9},{8,12},{9,13},{12,14},{13,15},{14,10},{15,... | collective-permute-start | bytes 1007624 | tf_op jit(solution)/shard_map/ppermute | solution.py:309
  22.9 7.8 %collective-permute-start.5 = (bf16[656,256]{1,0:T(8,128)(2,1)S(1)}, bf16[656,256]{1,0:T(8,128)(2,1)S(1)}, u32[]{:S(2)}, u32[]{:S(2)}) collective-permute-start(bf16[656,256]{1,0:T(8,128)(2,1)S(1)} %collective-permute-done.4.refs_3_), channel_id=1, source_target_pairs={{0,2},{1,3},{4,0},{5,1},{8,4},{9,5},{12,8},{13,9},{14,12},{15,13},... | collective-permute-start | bytes 1007624 | tf_op jit(solution)/shard_map/ppermute | solution.py:309
  23.3 12.8 %collective-permute-start.10 = (bf16[736,256]{1,0:T(8,128)(2,1)S(1)}, bf16[736,256]{1,0:T(8,128)(2,1)S(1)}, u32[]{:S(2)}, u32[]{:S(2)}) collective-permute-start(bf16[736,256]{1,0:T(8,128)(2,1)S(1)} %pad_maximum_fusion.2), channel_id=1, source_target_pairs={{0,16},{1,17},{2,18},{3,19},{4,20},{5,21},{6,22},{7,23},{8,24},{9,... | collective-permute-start | bytes 1130504 | tf_op jit(solution)/shard_map/ppermute | solution.py:309
  30.8 3.6 %copy-start.3 = (bf16[1024,256]{1,0:T(8,128)(2,1)S(1)}, bf16[1024,256]{1,0:T(8,128)(2,1)}, u32[]{:S(2)}) copy-start(bf16[1024,256]{1,0:T(8,128)(2,1)} %refs_2_.7) | copy-start | bytes 1572868
  30.8 9.1 %collective-permute-start.7 = (bf16[736,256]{1,0:T(8,128)(2,1)S(1)}, bf16[736,256]{1,0:T(8,128)(2,1)S(1)}, u32[]{:S(2)}, u32[]{:S(2)}) collective-permute-start(bf16[736,256]{1,0:T(8,128)(2,1)S(1)} %pad_maximum_fusion.1), channel_id=1, source_target_pairs={{0,16},{1,17},{2,18},{3,19},{4,20},{5,21},{6,22},{7,23},{8,24},{9,... | collective-permute-start | bytes 1130504 | tf_op jit(solution)/shard_map/ppermute | solution.py:309
  32.4 6.4 %collective-permute-start.8 = (bf16[512,256]{1,0:T(8,128)(2,1)S(1)}, bf16[512,256]{1,0:T(8,128)(2,1)S(1)}, u32[]{:S(2)}, u32[]{:S(2)}) collective-permute-start(bf16[512,256]{1,0:T(8,128)(2,1)S(1)} %slice.36), channel_id=1, source_target_pairs={{0,4},{1,5},{4,8},{5,9},{8,12},{9,13},{12,14},{13,15},{14,10},{15,... | collective-permute-start | bytes 786440 | tf_op jit(solution)/shard_map/ppermute | solution.py:309
  33.0 6.4 %collective-permute-start.9 = (bf16[512,256]{1,0:T(8,128)(2,1)S(1)}, bf16[512,256]{1,0:T(8,128)(2,1)S(1)}, u32[]{:S(2)}, u32[]{:S(2)}) collective-permute-start(bf16[512,256]{1,0:T(8,128)(2,1)S(1)} %slice.37), channel_id=1, source_target_pairs={{0,2},{1,3},{4,0},{5,1},{8,4},{9,5},{12,8},{13,9},{14,12},{15,13},... | collective-permute-start | bytes 786440 | tf_op jit(solution)/shard_map/ppermute | solution.py:309
  35.4 5.4 %collective-permute-start.12 = (bf16[3,512,256]{2,1,0:T(8,128)(2,1)S(1)}, bf16[3,512,256]{2,1,0:T(8,128)(2,1)S(1)}, u32[]{:S(2)}, u32[]{:S(2)}) collective-permute-start(bf16[3,512,256]{2,1,0:T(8,128)(2,1)S(1)} %shard_map.81.refs_0_), channel_id=1, source_target_pairs={{0,1},{1,0},{2,3},{3,2},{4,5},{5,4},{6,7},{7,6},{8,9},{9,8},{10,11... | collective-permute-start | bytes 2359304 | tf_op jit(solution)/shard_map/ppermute | solution.py:309
  39.8 2.0 %collective-permute-start.13 = (bf16[2,512,256]{2,1,0:T(8,128)(2,1)S(1)}, bf16[2,512,256]{2,1,0:T(8,128)(2,1)S(1)}, u32[]{:S(2)}, u32[]{:S(2)}) collective-permute-start(bf16[2,512,256]{2,1,0:T(8,128)(2,1)S(1)} %shard_map.79.refs_2_), channel_id=1, source_target_pairs={{0,1},{1,0},{2,3},{3,2},{4,5},{5,4},{6,7},{7,6},{8,9},{9,8},{10,11... | collective-permute-start | bytes 1572872 | tf_op jit(solution)/shard_map/ppermute | solution.py:309
  40.4 2.5 %collective-permute-start.11 = (bf16[2,512,256]{2,1,0:T(8,128)(2,1)S(1)}, bf16[2,512,256]{2,1,0:T(8,128)(2,1)S(1)}, u32[]{:S(2)}, u32[]{:S(2)}) collective-permute-start(bf16[2,512,256]{2,1,0:T(8,128)(2,1)S(1)} %shard_map.80.refs_0_), channel_id=1, source_target_pairs={{0,1},{1,0},{2,3},{3,2},{4,5},{5,4},{6,7},{7,6},{8,9},{9,8},{10,11... | collective-permute-start | bytes 1572872 | tf_op jit(solution)/shard_map/ppermute | solution.py:309
